TPU v7x, 32 devices: a whole 2x2x4 slice. The times are simulated.
32 devices in a mesh: row: 4 (over x, core), col: 8 (over z, y).
Axes of the slice: x: 2, y: 2, z: 4, core: 2. Of those that a mesh axis runs over, the one named last changes fastest.
Arguments:
- pair: float32 [512, 512, 128], P('row', 'col'), may hold values from -6 to 6
- logit_cotangent: bfloat16 [512, 512, 64], P('row', 'col'), may hold values from -6 to 6
- tiles: bfloat16 [512, 1024, 64], P(('row', 'col')), may hold values from -6 to 6
- tile_target: int32 [512, 1], P(('row', 'col')), may hold values from 0 to 7; in each aligned block of 16 rows (0 to 15, 16 to 31, ...) at most 2 rows name the same one
- tile_square: int32 [512], P(('row', 'col')), may hold values from 0 to 7
- tile_count: int32 [512], P(('row', 'col')), may hold values from 1 to 4
- w_template: bfloat16 [64, 128], replicated, may hold values from -0.75 to 0.75
- transition_norm_gain: float32 [128], replicated, may hold values from 0.1 to 1.9
- transition_norm_bias: float32 [128], replicated, may hold values from -3 to 3
- w_gate: bfloat16 [128, 512], replicated, may hold values from -0.5 to 0.5
- w_up: bfloat16 [128, 512], replicated, may hold values from -0.5 to 0.5
- w_out: bfloat16 [512, 128], replicated, may hold values from -0.25 to 0.25
- w_dist: bfloat16 [128, 64], replicated, may hold values from -0.5 to 0.5
Outputs:
- logits: bfloat16 [512, 512, 64], P('row', 'col')
- grad_pair: float32 [512, 512, 128], P('row', 'col')
- grad_tiles: bfloat16 [512, 1024, 64], P(('row', 'col'))
- grad_template: float32 [64, 128], replicated
- grad_gain: float32 [128], replicated
- grad_bias: float32 [128], replicated
- grad_gate: float32 [128, 512], replicated
- grad_up: float32 [128, 512], replicated
- grad_out: float32 [512, 128], replicated
- grad_dist: float32 [128, 64], replicated
Inputs may be any that keep to these rules, and one draw needn't show every extreme that they name: `tile_target`: among the 16 tiles of one device no column device is named more than 2 times; some device names one exactly 2 times.
All inputs are finite; a program needn't handle non-finite values.
Results may differ from a plain program's by a relative error of at most 0.0079.
Values may be sent and summed in bfloat16 or wider, within the bound.
No kernel may reach another device: no remote copies, remote signals or barrier semaphores. Data moves between devices by JAX's collectives and lax.ppermute only.
A program may use at most 128 MiB of HBM per device.

v0:
```python
import math

import jax
import jax.numpy as jnp
from jax import lax
from jax.sharding import PartitionSpec as P

SQ = 32
CAP = 2


def to_squares(values, across, downward):
    return (
        values.reshape(across, SQ, downward, SQ, -1)
        .transpose(0, 2, 1, 3, 4)
        .reshape(across * downward, SQ * SQ, -1)
    )


def from_squares(values, across, downward):
    return (
        values.reshape(across, downward, SQ, SQ, -1)
        .transpose(0, 2, 1, 3, 4)
        .reshape(across * SQ, downward * SQ, -1)
    )


def norm_intermediates(pair_entries, transition_norm_gain, transition_norm_bias):
    centered_entries = pair_entries - jnp.mean(pair_entries, axis=-1, keepdims=True)
    inverse_deviation = lax.rsqrt(
        jnp.mean(centered_entries * centered_entries, axis=-1, keepdims=True) + 1e-05
    )
    standardized_entries = centered_entries * inverse_deviation
    return (
        standardized_entries,
        inverse_deviation,
        (standardized_entries * transition_norm_gain + transition_norm_bias).astype(jnp.bfloat16),
    )


def transition_forward(
    pair_entries, transition_norm_gain, transition_norm_bias, w_gate, w_up, w_out
):
    standardized_entries, inverse_deviation, normalized_entries = norm_intermediates(
        pair_entries, transition_norm_gain, transition_norm_bias
    )
    gate = jnp.dot(normalized_entries, w_gate, preferred_element_type=jnp.float32)
    upper = jnp.dot(normalized_entries, w_up, preferred_element_type=jnp.float32)
    hidden = (jax.nn.silu(gate) * upper).astype(jnp.bfloat16)
    return pair_entries + jnp.dot(hidden, w_out, preferred_element_type=jnp.float32)


def transition_backward(
    pair_entries, upstream, transition_norm_gain, transition_norm_bias, w_gate, w_up, w_out
):
    standardized_entries, inverse_deviation, normalized_entries = norm_intermediates(
        pair_entries, transition_norm_gain, transition_norm_bias
    )
    gate = jnp.dot(normalized_entries, w_gate, preferred_element_type=jnp.float32)
    upper = jnp.dot(normalized_entries, w_up, preferred_element_type=jnp.float32)
    sigma = jax.nn.sigmoid(gate)
    swish = gate * sigma
    hidden = (swish * upper).astype(jnp.bfloat16)
    up_low = upstream.astype(jnp.bfloat16)
    g_out = jnp.dot(hidden.T, up_low, preferred_element_type=jnp.float32)
    d_hidden = jnp.dot(up_low, w_out.T, preferred_element_type=jnp.float32)
    d_gate = (d_hidden * upper * sigma * (1.0 + gate * (1.0 - sigma))).astype(jnp.bfloat16)
    d_upper = (d_hidden * swish).astype(jnp.bfloat16)
    g_gate = jnp.dot(normalized_entries.T, d_gate, preferred_element_type=jnp.float32)
    g_up = jnp.dot(normalized_entries.T, d_upper, preferred_element_type=jnp.float32)
    normalized_gradient = jnp.dot(d_gate, w_gate.T, preferred_element_type=jnp.float32) + jnp.dot(
        d_upper, w_up.T, preferred_element_type=jnp.float32
    )
    gain_gradient = jnp.sum(normalized_gradient * standardized_entries, axis=0)
    g_bias = jnp.sum(normalized_gradient, axis=0)
    standardized_gradient = normalized_gradient * transition_norm_gain
    entries_gradient = (
        standardized_gradient
        - jnp.mean(standardized_gradient, axis=-1, keepdims=True)
        - standardized_entries
        * jnp.mean(standardized_gradient * standardized_entries, axis=-1, keepdims=True)
    ) * inverse_deviation
    return (upstream + entries_gradient, (gain_gradient, g_bias, g_gate, g_up, g_out))


def mirror(block, row_devs, col_devs):
    rows_here, cols_here, bins = block.shape
    piece = rows_here // col_devs
    devices = row_devs * col_devs
    spread = lax.all_to_all(block, "col", split_axis=0, concat_axis=1, tiled=True)
    split = spread.reshape(piece, devices, piece, bins)
    moved = lax.all_to_all(split, ("row", "col"), split_axis=1, concat_axis=0, tiled=True)
    columns = moved.reshape(devices * piece, piece, bins)
    flipped = columns.transpose(1, 0, 2)
    return lax.all_to_all(flipped, "col", split_axis=1, concat_axis=0, tiled=True)


def per_device(
    pair,
    logit_cotangent,
    tiles,
    tile_target,
    tile_square,
    tile_count,
    w_template,
    transition_norm_gain,
    transition_norm_bias,
    w_gate,
    w_up,
    w_out,
    w_dist,
):
    row_devs = lax.axis_size("row")
    col_devs = lax.axis_size("col")
    rows_here, cols_here, width = pair.shape
    bins = w_dist.shape[1]
    length = rows_here * row_devs
    slots, cells_sq, feature = tiles.shape
    sq_rows = rows_here // SQ
    sq_cols = cols_here // SQ
    squares = sq_rows * sq_cols
    mirrored_cot = mirror(logit_cotangent, row_devs, col_devs)
    target = tile_target[:, 0]
    positions = jnp.arange(slots, dtype=jnp.int32)
    earlier = positions[None, :] < positions[:, None]
    same_target = target[:, None] == target[None, :]
    slot_rank = jnp.sum((same_target & earlier).astype(jnp.int32), axis=1)
    chooser_bool = (
        target[:, None, None] == jnp.arange(col_devs, dtype=jnp.int32)[None, :, None]
    ) & (slot_rank[:, None, None] == jnp.arange(CAP, dtype=jnp.int32)[None, None, :])
    chooser_int = chooser_bool.astype(jnp.int32)
    chooser = chooser_bool.astype(jnp.bfloat16)
    occupied = jnp.sum(chooser_int, axis=0)
    send_ids = jnp.sum(chooser_int * (tile_square + 1)[:, None, None], axis=0) - 1
    send_counts = jnp.sum(chooser_int * tile_count[:, None, None], axis=0) + 1 - occupied
    payload = jnp.einsum(
        "sdk,spt->dkpt", chooser, tiles, preferred_element_type=jnp.float32
    ).astype(jnp.bfloat16)
    received, got_ids, got_counts = (
        lax.all_to_all(payload, "col", split_axis=0, concat_axis=0, tiled=True),
        lax.all_to_all(send_ids, "col", split_axis=0, concat_axis=0, tiled=True),
        lax.all_to_all(send_counts, "col", split_axis=0, concat_axis=0, tiled=True),
    )
    incoming = col_devs * CAP
    got_ids = got_ids.reshape(incoming)
    got_counts_f = got_counts.reshape(incoming).astype(jnp.float32)
    raw_in = received.reshape(incoming, cells_sq, feature)
    proj_in = jnp.dot(
        raw_in.reshape(incoming * cells_sq, feature), w_template, preferred_element_type=jnp.float32
    )
    proj_in = (proj_in.reshape(incoming, cells_sq, width) / got_counts_f[:, None, None]).astype(
        jnp.bfloat16
    )
    placing = (got_ids[:, None] == jnp.arange(squares, dtype=jnp.int32)[None, :]).astype(
        jnp.bfloat16
    )
    added = jnp.einsum("ns,npc->spc", placing, proj_in, preferred_element_type=jnp.float32)
    z_one = pair + from_squares(added, sq_rows, sq_cols)
    pair_entries = rows_here * cols_here
    block = math.gcd(pair_entries, 2048)
    blocks = pair_entries // block
    z_blocks = z_one.reshape(blocks, block, width)
    z_two = lax.map(
        lambda piece: transition_forward(
            piece, transition_norm_gain, transition_norm_bias, w_gate, w_up, w_out
        ),
        z_blocks,
    )
    z_low = z_two.reshape(pair_entries, width).astype(jnp.bfloat16)
    heads = (
        jnp.dot(z_low, w_dist, preferred_element_type=jnp.float32)
        .astype(jnp.bfloat16)
        .reshape(rows_here, cols_here, bins)
    )
    heads_mirror = mirror(heads, row_devs, col_devs)
    logits = (heads.astype(jnp.float32) + heads_mirror.astype(jnp.float32)).astype(jnp.bfloat16)
    d_heads = (
        (logit_cotangent.astype(jnp.float32) + mirrored_cot.astype(jnp.float32))
        .astype(jnp.bfloat16)
        .reshape(pair_entries, bins)
    )
    dz_two = jnp.dot(d_heads, w_dist.T, preferred_element_type=jnp.float32)
    g_dist = jnp.dot(z_low.T, d_heads, preferred_element_type=jnp.float32)

    def back_block(carry, items):
        piece, upstream = items
        d_piece, grads = transition_backward(
            piece, upstream, transition_norm_gain, transition_norm_bias, w_gate, w_up, w_out
        )
        return (tuple((total + term for total, term in zip(carry, grads))), d_piece)

    hidden_units = w_gate.shape[1]
    start = (
        jnp.zeros((width,), jnp.float32),
        jnp.zeros((width,), jnp.float32),
        jnp.zeros((width, hidden_units), jnp.float32),
        jnp.zeros((width, hidden_units), jnp.float32),
        jnp.zeros((hidden_units, width), jnp.float32),
    )
    sums, dz_one = lax.scan(back_block, start, (z_blocks, dz_two.reshape(blocks, block, width)))
    grad_pair = dz_one.reshape(rows_here, cols_here, width)
    d_squares = to_squares(grad_pair, sq_rows, sq_cols)
    valid = (got_ids >= 0).astype(jnp.float32)
    picked = jnp.take(d_squares, jnp.maximum(got_ids, 0), axis=0)
    d_proj_in = (picked * valid[:, None, None]).astype(jnp.bfloat16)
    g_in = jnp.dot(
        d_proj_in.reshape(incoming * cells_sq, width),
        w_template.T,
        preferred_element_type=jnp.float32,
    )
    g_in = (g_in.reshape(incoming, cells_sq, feature) / got_counts_f[:, None, None]).astype(
        jnp.bfloat16
    )
    per_slot = jnp.einsum("npt,npc->ntc", raw_in, d_proj_in, preferred_element_type=jnp.float32)
    g_template = jnp.sum(per_slot / got_counts_f[:, None, None], axis=0)
    returned = lax.all_to_all(
        g_in.reshape(col_devs, CAP, cells_sq, feature),
        "col",
        split_axis=0,
        concat_axis=0,
        tiled=True,
    )
    grad_tiles = jnp.einsum(
        "sdk,dkpt->spt", chooser, returned, preferred_element_type=jnp.float32
    ).astype(jnp.bfloat16)
    totals = lax.psum(
        (g_template, sums[0], sums[1], sums[2], sums[3], sums[4], g_dist), ("row", "col")
    )
    scale = jnp.float32(length)
    return (
        logits,
        grad_pair,
        grad_tiles,
        totals[0] / scale,
        totals[1] / scale,
        totals[2] / scale,
        totals[3] / scale,
        totals[4] / scale,
        totals[5] / scale,
        totals[6] / scale,
    )


def solution(mesh):
    return jax.shard_map(
        per_device,
        mesh=mesh,
        in_specs=(
            P("row", "col", None),
            P("row", "col", None),
            P(("row", "col"), None, None),
            P(("row", "col"), None),
            P(("row", "col")),
            P(("row", "col")),
            P(),
            P(),
            P(),
            P(),
            P(),
            P(),
            P(),
        ),
        out_specs=(
            P("row", "col", None),
            P("row", "col", None),
            P(("row", "col"), None, None),
            P(),
            P(),
            P(),
            P(),
            P(),
            P(),
            P(),
        ),
        check_vma=False,
    )
```

profile of v0, /device:TPU:18, one launch (start us, length us, event | category | flops | bytes accessed | tf_op | source)
XLA Modules:
  0.0 730.4 jit_solution(10956410309977062716)
XLA Ops:
  11.0 6.2 all-to-all-start
  21.2 5.6 all-to-all-start.2
  33.4 6.0 all-to-all-start.6
  45.0 15.4 %all-to-all-done.6 = bf16[8,2,32768]{2,1,0:T(2,128)(2,1)S(1)} async-done(((bf16[8,2,32768]{2,1,0:T(2,128)(2,1)}), bf16[8,2,32768]{2,1,0:T(2,128)(2,1)S(1)}, u32[]{:S(2)}, u32[]{:S(2)}) %all-to-all-start.6) | async-done | bytes 1048608 | tf_op jit(solution)/shard_map/all_to_all | solution.py:90
  60.4 7.5 %all-to-all-start.1 = ((bf16[8,2,1024,64]{2,3,1,0:T(8,128)(2,1)}), bf16[8,2,1024,64]{2,3,1,0:T(8,128)(2,1)}, u32[]{:S(2)}, u32[]{:S(2)}) async-start(bf16[8,2,1024,64]{2,3,1,0:T(8,128)(2,1)} %copy.187), calls=%async_computation.1 | async-start | bytes 4194304 | tf_op jit(solution)/shard_map/all_to_all | solution.py:140
  75.8 4.6 reshape.309
  80.4 31.6 %all-to-all-done.1 = bf16[8,2,1024,64]{2,3,1,0:T(8,128)(2,1)} async-done(((bf16[8,2,1024,64]{2,3,1,0:T(8,128)(2,1)}), bf16[8,2,1024,64]{2,3,1,0:T(8,128)(2,1)}, u32[]{:S(2)}, u32[]{:S(2)}) %all-to-all-start.1) | async-done | bytes 2097184 | tf_op jit(solution)/shard_map/all_to_all | solution.py:140
  112.1 7.5 %all-to-all-start.7 = ((bf16[32,2,8192]{2,1,0:T(2,128)(2,1)}), bf16[32,2,8192]{2,1,0:T(2,128)(2,1)}, u32[]{:S(2)}, u32[]{:S(2)}) async-start(bf16[32,2,8192]{2,1,0:T(2,128)(2,1)} %reshape.309), calls=%async_computation.7 | async-start | bytes 2097152 | tf_op jit(solution)/shard_map/all_to_all | solution.py:92
  119.6 6.2 copy.188
  125.8 6.3 fusion.15
  138.5 48.8 %while.33 = (s32[]{:T(128)}, bf16[4,2048,128]{2,1,0:T(8,128)(2,1)S(1)}, f32[4,2048,128]{2,1,0:T(8,128)}, f32[128]{0:T(128)S(1)}, f32[128]{0:T(128)S(1)}, /*index...) while((s32[]{:T(128)}, ...), condition=%wide.region_7.8_spmd.clone, body=%wide.region_4.7_spmd.sunk.clone | while | flops 815532032 | bytes 15166569 | solution.py:163
  146.0 4.7 fusion.121
  158.2 4.7 fusion.121
  170.4 4.7 fusion.121
  182.6 4.7 fusion.121
  195.7 4.3 reshape.301
  200.0 6.2 all-to-all-start.3
  212.7 16.3 %all-to-all-done.3 = bf16[8,2,32768]{2,1,0:T(2,128)(2,1)S(1)} async-done(((bf16[8,2,32768]{2,1,0:T(2,128)(2,1)}), bf16[8,2,32768]{2,1,0:T(2,128)(2,1)S(1)}, u32[]{:S(2)}, u32[]{:S(2)}) %all-to-all-start.3) | async-done | bytes 1048608 | tf_op jit(solution)/shard_map/all_to_all | solution.py:90
  230.0 6.9 all-to-all-start.8
  247.0 12.6 %all-to-all-done.8 = bf16[8,2,32768]{2,1,0:T(2,128)(2,1)S(1)} async-done(((bf16[8,2,32768]{2,1,0:T(2,128)(2,1)}), bf16[8,2,32768]{2,1,0:T(2,128)(2,1)S(1)}, u32[]{:S(2)}, u32[]{:S(2)}) %all-to-all-start.8) | async-done | bytes 1048608 | tf_op jit(solution)/shard_map/all_to_all | solution.py:95
  259.6 6.7 all-to-all-start.4
  276.1 5.4 copy.202
  303.2 6.4 all-to-all-start.5
  309.5 68.8 %while.34 = (s32[]{:T(128)}, f32[128]{0:T(128)S(1)}, f32[128]{0:T(128)S(1)}, f32[128,512]{1,0:T(8,128)S(1)}, f32[128,512]{1,0:T(8,128)S(1)}, /*index=5*/f32[512,...) while((s32[]{:T(128)}, f32[128]{0:T(128)S(1)}, ...), condition=%wide.region_15.16_spmd.clone.clone, body=%wide.region_8.15_spmd.clone.sunk.clone | while | flops 2174880000 | bytes 88914152 | solution.py:200
  378.4 5.0 copy.206
  383.4 6.5 gather_fusion
  389.9 4.5 multiply_convert_fusion.7
  399.9 6.1 all-to-all-start.9
  415.6 134.5 %all-reduce.5.cloned.1.call-done = (f32[64,128]{1,0:T(8,128)}, f32[128]{0:T(128)}, f32[128]{0:T(128)}, f32[128,64]{0,1:T(8,128)}) async-done(((f32[64,128]{1,0:T(8,128)}, f32[128]{0:T(128)}, f32[128]{0:T(128)}, f32[128,64]{0,1:T(8,128)}), (f32[64,128]{1,0:T(8,128)}, f32[128]{0:T(128)}, f32[128]{0:T(128)}, f32[128,64]{0,1:T(8,128)})) %all-reduce.5.cloned.1.call-update) | async-done | bytes 66576 | tf_op jit(solution)/shard_map/psum | solution.py:226
  554.0 133.9 %all-reduce.7.cloned.1.call-done = (f32[128,512]{1,0:T(8,128)}, f32[128,512]{1,0:T(8,128)}, f32[512,128]{1,0:T(8,128)}) async-done(((f32[128,512]{1,0:T(8,128)}, f32[128,512]{1,0:T(8,128)}, f32[512,128]{1,0:T(8,128)}), (f32[128,512]{1,0:T(8,128)}, f32[128,512]{1,0:T(8,128)}, f32[512,128]{1,0:T(8,128)})) %all-reduce.7.cloned.1.call-update) | async-done | bytes 786448 | tf_op jit(solution)/shard_map/psum | solution.py:226
  698.9 5.4 copy.196
  704.2 5.8 copy.197
  (235 shorter events, 232.2 us)
Async XLA Ops:
  7.2 118.6 %copy-start = (bf16[64,128]{1,0:T(8,128)(2,1)S(1)}, bf16[64,128]{1,0:T(8,128)(2,1)}, u32[]{:S(2)}) copy-start(bf16[64,128]{1,0:T(8,128)(2,1)} %param.23) | copy-start | bytes 49156
  8.8 30.6 %copy-start.22 = (pred[16,8]{0,1:T(8,128)(4,1)}, pred[16,8]{0,1:T(8,128)(4,1)S(1)}, u32[]{:S(2)}) copy-start(pred[16,8]{0,1:T(8,128)(4,1)S(1)} %iota_compare_fusion.2) | copy-start | bytes 388
  8.8 30.6 %copy-start.24 = (pred[16,2]{0,1:T(4,128)(4,1)}, pred[16,2]{0,1:T(4,128)(4,1)S(1)}, u32[]{:S(2)}) copy-start(pred[16,2]{0,1:T(4,128)(4,1)S(1)} %iota_compare_fusion.3) | copy-start | bytes 100
  11.0 10.2 %all-to-all-start = ((s32[8,1,2]{2,1,0:T(1,128)}), s32[8,1,2]{2,1,0:T(1,128)S(1)}, u32[]{:S(2)}, u32[]{:S(2)}) async-start(s32[8,1,2]{2,1,0:T(1,128)} %copy.185), calls=%async_computation | async-start | bytes 8192 | tf_op jit(solution)/shard_map/all_to_all | solution.py:141
  21.2 12.2 %all-to-all-start.2 = ((s32[8,1,2]{2,1,0:T(1,128)}), s32[8,1,2]{2,1,0:T(1,128)S(1)}, u32[]{:S(2)}, u32[]{:S(2)}) async-start(s32[8,1,2]{2,1,0:T(1,128)} %copy.189), calls=%async_computation.2 | async-start | bytes 8192 | tf_op jit(solution)/shard_map/all_to_all | solution.py:142
  33.4 27.0 %all-to-all-start.6 = ((bf16[8,2,32768]{2,1,0:T(2,128)(2,1)}), bf16[8,2,32768]{2,1,0:T(2,128)(2,1)S(1)}, u32[]{:S(2)}, u32[]{:S(2)}) async-start(bf16[8,2,32768]{2,1,0:T(2,128)(2,1)} %reshape.307), calls=%async_computation.6 | async-start | bytes 2097152 | tf_op jit(solution)/shard_map/all_to_all | solution.py:90
  60.4 51.7 %all-to-all-start.1 = ((bf16[8,2,1024,64]{2,3,1,0:T(8,128)(2,1)}), bf16[8,2,1024,64]{2,3,1,0:T(8,128)(2,1)}, u32[]{:S(2)}, u32[]{:S(2)}) async-start(bf16[8,2,1024,64]{2,3,1,0:T(8,128)(2,1)} %copy.187), calls=%async_computation.1 | async-start | bytes 4194304 | tf_op jit(solution)/shard_map/all_to_all | solution.py:140
  69.4 56.3 %copy-start.26 = (f32[16]{0:T(128)}, f32[16]{0:T(128)S(1)}, u32[]{:S(2)}) copy-start(f32[16]{0:T(128)S(1)} %convert_element_type.113) | copy-start | bytes 196
  112.1 87.9 %all-to-all-start.7 = ((bf16[32,2,8192]{2,1,0:T(2,128)(2,1)}), bf16[32,2,8192]{2,1,0:T(2,128)(2,1)}, u32[]{:S(2)}, u32[]{:S(2)}) async-start(bf16[32,2,8192]{2,1,0:T(2,128)(2,1)} %reshape.309), calls=%async_computation.7 | async-start | bytes 2097152 | tf_op jit(solution)/shard_map/all_to_all | solution.py:92
  138.5 48.8 %copy-start.18 = (bf16[128,64]{0,1:T(8,128)(2,1)S(1)}, bf16[128,64]{0,1:T(8,128)(2,1)}, u32[]{:S(2)}) copy-start(bf16[128,64]{0,1:T(8,128)(2,1)} %param.29) | copy-start | bytes 49156
  187.3 4.1 copy-start.2
  200.0 29.0 %all-to-all-start.3 = ((bf16[8,2,32768]{2,1,0:T(2,128)(2,1)}), bf16[8,2,32768]{2,1,0:T(2,128)(2,1)S(1)}, u32[]{:S(2)}, u32[]{:S(2)}) async-start(bf16[8,2,32768]{2,1,0:T(2,128)(2,1)} %reshape.301), calls=%async_computation.3 | async-start | bytes 2097152 | tf_op jit(solution)/shard_map/all_to_all | solution.py:90
  230.0 29.6 %all-to-all-start.8 = ((bf16[8,2,32768]{2,1,0:T(2,128)(2,1)}), bf16[8,2,32768]{2,1,0:T(2,128)(2,1)S(1)}, u32[]{:S(2)}, u32[]{:S(2)}) async-start(bf16[8,2,32768]{2,1,0:T(2,128)(2,1)} %reshape.311), calls=%async_computation.8 | async-start | bytes 2097152 | tf_op jit(solution)/shard_map/all_to_all | solution.py:95
  259.6 6.7 copy-start.13
  259.6 37.1 %all-to-all-start.4 = ((bf16[32,2,8192]{2,1,0:T(2,128)(2,1)}), bf16[32,2,8192]{2,1,0:T(2,128)(2,1)}, u32[]{:S(2)}, u32[]{:S(2)}) async-start(bf16[32,2,8192]{2,1,0:T(2,128)(2,1)} %reshape.303), calls=%async_computation.4 | async-start | bytes 2097152 | tf_op jit(solution)/shard_map/all_to_all | solution.py:92
  290.2 6.4 copy-start.6
  296.7 12.9 %copy-start.15 = (f32[512,128]{1,0:T(8,128)S(1)}, f32[512,128]{1,0:T(8,128)}, u32[]{:S(2)}) copy-start(f32[512,128]{1,0:T(8,128)} %custom-call.4) | copy-start | bytes 786436
  296.7 12.9 %copy-start.29 = (bf16[512,128]{1,0:T(8,128)(2,1)S(1)}, bf16[512,128]{1,0:T(8,128)(2,1)}, u32[]{:S(2)}) copy-start(bf16[512,128]{1,0:T(8,128)(2,1)} %param.28) | copy-start | bytes 393220
  303.2 96.8 %all-to-all-start.5 = ((bf16[8,2,32768]{2,1,0:T(2,128)(2,1)}), bf16[8,2,32768]{2,1,0:T(2,128)(2,1)}, u32[]{:S(2)}, u32[]{:S(2)}) async-start(bf16[8,2,32768]{2,1,0:T(2,128)(2,1)} %reshape.305), calls=%async_computation.5 | async-start | bytes 2097152 | tf_op jit(solution)/shard_map/all_to_all | solution.py:95
  378.3 5.1 copy-start.9
  378.3 5.1 copy-start.10
  378.4 5.0 copy-start.16
  378.4 5.0 copy-start.20
  378.4 5.0 copy-start.21
  389.9 4.5 copy-start.27
  399.9 9.4 %copy-start.3 = (bf16[4,2048,128]{2,1,0:T(8,128)(2,1)S(1)}, bf16[4,2048,128]{2,1,0:T(8,128)(2,1)}, u32[]{:S(2)}) copy-start(bf16[4,2048,128]{2,1,0:T(8,128)(2,1)} %copy-done.2) | copy-start | bytes 6291460
  399.9 317.7 %all-to-all-start.9 = ((bf16[8,2,1024,64]{2,1,3,0:T(2,128)(2,1)}), bf16[8,2,1024,64]{2,1,3,0:T(2,128)(2,1)}, u32[]{:S(2)}, u32[]{:S(2)}) async-start(bf16[8,2,1024,64]{2,1,3,0:T(2,128)(2,1)} %copy.207), calls=%async_computation.9 | async-start | bytes 4194304 | tf_op jit(solution)/shard_map/all_to_all | solution.py:216
  406.1 144.0 %all-reduce.5.cloned.1.call-start = ((), (), s32[]{:S(2)}) async-start(), calls=%async_computation.10 | async-start | bytes 133120 | tf_op jit(solution)/shard_map/psum | solution.py:226
  414.8 273.0 %all-reduce.7.cloned.1.call-start = ((), (), s32[]{:S(2)}) async-start(), calls=%async_computation.11 | async-start | bytes 1572864 | tf_op jit(solution)/shard_map/psum | solution.py:226
  704.2 5.8 copy-start.7
  710.1 7.6 %copy-start.23 = (pred[16,8]{0,1:T(8,128)(4,1)S(1)}, pred[16,8]{0,1:T(8,128)(4,1)}, u32[]{:S(2)}) copy-start(pred[16,8]{0,1:T(8,128)(4,1)} %copy-done.22) | copy-start | bytes 388
  710.1 7.6 %copy-start.25 = (pred[16,2]{0,1:T(4,128)(4,1)S(1)}, pred[16,2]{0,1:T(4,128)(4,1)}, u32[]{:S(2)}) copy-start(pred[16,2]{0,1:T(4,128)(4,1)} %copy-done.24) | copy-start | bytes 100
  (16 other events, 38.5 us)
Sparse Core Ops, SparseCore 0:
  415.0 135.0 all-reduce.4
  556.7 131.1 all-reduce.6
where the time goes:
time: 742 us; the launch traced here: 730 us
  waiting for transfers between devices  348 us (47%)
  local copies, waits for them, and re-layouts  139 us (19%)
  matrix products  91 us (12%)
  other arithmetic  70.7 us (10%)
  starting transfers between devices  65.2 us (9%)
  between operations  15 us (2%)
    psum x2, waiting for transfers between devices, per_device(): lax.psum((g_template, sums[0], sums[1], sums[2], sums[3], sums[4], g_dist...  268 us
    unnamed x71, local copies, waits for them, and re-layouts  50.6 us
    all_to_all x2, waiting for transfers between devices, mirror(): lax.all_to_all(block, 'col', split_axis=0, concat_axis=1, tiled=True)  31.7 us
    all_to_all x1, waiting for transfers between devices, per_device(): lax.all_to_all(payload, 'col', split_axis=0, concat_axis=0, tiled=True)  31.6 us
    dot_general x4, matrix products, transition_forward(): jnp.dot(hidden, w_out, preferred_element_type=jnp.float32)  18.8 us
    dot_general x4, matrix products, transition_forward(): jnp.dot(normalized_entries, w_gate, preferred_element_type=jnp.float32)  16.1 us
    reduce_sum x8, other arithmetic, norm_intermediates(): jnp.mean(centered_entries * centered_entries, axis=-1, keepdims=True)  14.9 us
  transfers between devices with their start and end apart: 12, of which 7 were waited for; matrix products, arithmetic and copies ran while one was open for 38% of the time, Pallas kernels for 0%

commit v1 on v0

v1 whole, which is shorter than its diff:
```python
import functools

import jax
import jax.numpy as jnp
from jax import lax
from jax.experimental import pallas as pl
from jax.experimental.pallas import tpu as pltpu
from jax.sharding import PartitionSpec as P

SQ = 32
CAP = 2
LANES = 128
META = 16
GROUP = LANES // SQ
STEP_ROWS = 16
PIECE = 256
VMEM_BYTES = 52 * 2**20
BF16 = jnp.bfloat16
F32 = jnp.float32

VMEM = pl.BlockSpec(memory_space=pltpu.VMEM)
SMEM = pl.BlockSpec(memory_space=pltpu.SMEM)
ANY = pl.BlockSpec(memory_space=pl.ANY)


def params():
    return pltpu.CompilerParams(vmem_limit_bytes=VMEM_BYTES)


def dot_nn(a, b):
    return lax.dot_general(a, b, (((1,), (0,)), ((), ())), preferred_element_type=F32)


def dot_nt(a, b):
    return lax.dot_general(a, b, (((1,), (1,)), ((), ())), preferred_element_type=F32)


def dot_tn(a, b):
    return lax.dot_general(a, b, (((0,), (0,)), ((), ())), preferred_element_type=F32)


def fill_slots(me, target, source, devs):
    def clear(i, unused):
        source[i] = -1
        return unused

    def place(s, unused):
        place_of = lax.rem(target[s] - me + devs, devs) * CAP
        taken = source[place_of] >= 0
        source[place_of + jnp.where(taken, 1, 0)] = s
        return unused

    lax.fori_loop(0, devs * CAP, clear, 0)
    lax.fori_loop(0, target.shape[0], place, 0)


def low_lanes(shape):
    return lax.broadcasted_iota(jnp.int32, shape, 1) < LANES // 2


def pack_kernel(devs, where_am, target, square, count, tiles, cot, *refs):
    payloads, (cot_a, cot_b), (source,) = refs[:devs], refs[devs : devs + 2], refs[devs + 2 :]
    feature, cells = tiles.shape[1:]
    groups = cells // LANES
    fill_slots(where_am[0], target, source, devs)
    first = where_am[1] == 0
    low = low_lanes(cot.shape[1:])

    def pack_pair(p, unused):
        even, odd = cot[2 * p].astype(F32), cot[2 * p + 1].astype(F32)
        front = jnp.where(low, even, pltpu.roll(odd, LANES // 2, 1)).astype(BF16)
        back = jnp.where(low, pltpu.roll(even, LANES // 2, 1), odd).astype(BF16)
        cot_a[p] = jnp.where(first, front, back)
        cot_b[p] = jnp.where(first, back, front)
        return unused

    lax.fori_loop(0, cot.shape[0] // 2, pack_pair, 0, unroll=4)
    line = lax.broadcasted_iota(jnp.int32, (META, LANES), 0)
    for k in range(devs):
        meta = jnp.zeros((META, LANES), F32)
        for r in range(CAP):
            slot = source[k * CAP + r]
            held = jnp.maximum(slot, 0)
            ident = jnp.where(slot >= 0, square[held], -1).astype(F32)
            meta = jnp.where(line == r, ident, meta)
            meta = jnp.where(line == 8 + r, count[held].astype(F32), meta)
            for c in range(groups):
                at = (r * groups + c) * feature
                payloads[k][at : at + feature, :] = tiles[held, :, c * LANES : (c + 1) * LANES]
        payloads[k][CAP * groups * feature :, :] = meta.astype(BF16)


def cotangent_kernel(where_am, cot, got_a, got_b, out, turned):
    cols, bins, rows = cot.shape

    def turn(j, unused):
        turned[pl.ds(j, rows, stride=cols), 0:bins] = cot[j].astype(F32).T
        return unused

    lax.fori_loop(0, cols, turn, 0, unroll=4)
    pairs = got_a.shape[0]
    for half in range(rows // cols):
        straight = where_am[1] == half

        def add(p, unused):
            mirrored = jnp.where(straight, got_a[p].astype(F32), got_b[p].astype(F32)).T
            at = pl.multiple_of((half * pairs + p) * LANES, LANES)
            out[pl.ds(at, LANES), :] = (turned[pl.ds(at, LANES), 0:bins] + mirrored).astype(BF16)
            return unused

        lax.fori_loop(0, pairs, add, 0, unroll=4)


def fold_rows(values):
    return jnp.sum(values.reshape(values.shape[0] // 8, 8, values.shape[1]), axis=0)


def main_kernel(devs, cols, *refs):
    where_am, refs = refs[0], refs[1:]
    payloads, refs = refs[:devs], refs[devs:]
    (pair, dheads, w_template, gain, bias, w_gate, w_up, w_out, w_gate_t, w_up_t, w_out_t, w_dist_t), refs = refs[:12], refs[12:]
    (grad_pair, z_low_out, heads_a, heads_b), refs = refs[:4], refs[4:]
    returns, refs = refs[:devs], refs[devs:]
    (keep, send), refs = refs[:2], refs[2:]
    idents, total, summed, squares, acc_gu, acc_out, acc_td, acc_gb, low_gu, low_hid, sems = refs
    step = pl.program_id(0)
    steps = pl.num_programs(0)
    feature, width = w_template.shape
    hidden = w_gate.shape[1]
    groups = SQ * SQ // LANES
    slab = groups * feature
    block = pair.shape[0]
    rows = block // cols
    sq_cols = cols // SQ
    parts = SQ // rows
    per_part = groups // parts

    @pl.when(step == 0)
    def _():
        total[...] = jnp.zeros_like(total)
        acc_gu[...] = jnp.zeros_like(acc_gu)
        acc_out[...] = jnp.zeros_like(acc_out)
        acc_td[...] = jnp.zeros_like(acc_td)
        acc_gb[...] = jnp.zeros_like(acc_gb)
        for k in range(devs):
            meta = payloads[k][CAP * slab :, :].astype(F32)
            for r in range(CAP):
                ident = jnp.max(meta[r : r + 1, :]).astype(jnp.int32)
                idents[k * CAP + r] = ident
                scale = 1.0 / meta[8 + r : 9 + r, :]

                @pl.when(ident >= 0)
                def _():
                    at = pl.multiple_of(ident * slab, slab)
                    total[pl.ds(at, slab), :] += payloads[k][r * slab : (r + 1) * slab, :].astype(F32) * scale

        summed[...] = total[...].astype(BF16)

    band, part = step // parts, lax.rem(step, parts)
    proj, pieces = [], []
    for c in range(per_part):
        across = []
        for s in range(sq_cols):
            at = pl.multiple_of(((band * sq_cols + s) * groups + part * per_part + c) * feature, feature)
            piece = summed[pl.ds(at, feature), :]
            across.append(dot_tn(piece, w_template[...]).reshape(GROUP, SQ, width))
            pieces.append(piece)
        proj.append(jnp.concatenate(across, axis=1).reshape(GROUP * cols, width))
    z_one = pair[...] + jnp.concatenate(proj, axis=0)
    mean = jnp.mean(z_one, axis=1, keepdims=True)
    centred = z_one - mean
    deviation = lax.rsqrt(jnp.mean(centred * centred, axis=1, keepdims=True) + 1e-5)
    standard = centred * deviation
    normed = (standard * gain[...] + bias[...]).astype(BF16)
    d_low = dheads[...]
    dz_two = dot_nn(d_low, w_dist_t[...])
    dz_low = dz_two.astype(BF16)

    z_two = z_one
    d_norm = jnp.zeros_like(z_one)
    for h in range(0, hidden, PIECE):
        e = h + PIECE
        gate = dot_nn(normed, w_gate[:, h:e])
        upper = dot_nn(normed, w_up[:, h:e])
        d_hidden = dot_nn(dz_low, w_out_t[:, h:e])
        sigma = 0.5 * jnp.tanh(0.5 * gate) + 0.5
        swish = gate * sigma
        hid = (swish * upper).astype(BF16)
        d_gate = (d_hidden * upper * (sigma + swish * (1.0 - sigma))).astype(BF16)
        d_upper = (d_hidden * swish).astype(BF16)
        z_two = z_two + dot_nn(hid, w_out[h:e, :])
        d_norm = d_norm + dot_nn(d_gate, w_gate_t[h:e, :]) + dot_nn(d_upper, w_up_t[h:e, :])
        low_hid[:, h:e] = hid
        low_gu[:, h:e] = d_gate
        low_gu[:, hidden + h : hidden + e] = d_upper

    acc_gu[...] += dot_tn(normed, low_gu[...])
    acc_out[...] += dot_tn(dz_low, low_hid[...])
    z_low = z_two.astype(BF16)
    z_low_out[...] = z_low
    acc_td[feature:, :] += dot_tn(d_low, z_low)
    acc_gb[0:8, :] += fold_rows(d_norm * standard)
    acc_gb[8:16, :] += fold_rows(d_norm)
    d_standard = d_norm * gain[...]
    grad = dz_two + deviation * (
        d_standard
        - jnp.mean(d_standard, axis=1, keepdims=True)
        - standard * jnp.mean(d_standard * standard, axis=1, keepdims=True)
    )
    grad_pair[...] = grad

    heads = dot_nt(w_dist_t[...], z_low).astype(BF16)
    per_half = steps // 2
    pairs = block // LANES
    at = lax.rem(step, per_half) * pairs
    straight = step // per_half == where_am[1]

    @pl.when(straight)
    def _():
        for p in range(pairs):
            heads_a[at + p] = heads[:, p * LANES : (p + 1) * LANES]

    @pl.when(jnp.logical_not(straight))
    def _():
        for p in range(pairs):
            heads_b[at + p] = heads[:, p * LANES : (p + 1) * LANES]

    d_proj = grad.astype(BF16).reshape(rows, cols, width)
    for s in range(sq_cols):
        cells = d_proj[:, s * SQ : (s + 1) * SQ, :].reshape(rows * SQ, width)
        tile_grad = dot_nt(w_template[...], cells).astype(BF16)
        for c in range(per_part):
            at = pl.multiple_of((part * per_part + c) * feature, feature)
            squares[band * sq_cols + s, pl.ds(at, feature), :] = tile_grad[:, c * LANES : (c + 1) * LANES]
        side = jnp.concatenate([pieces[c * sq_cols + s] for c in range(per_part)], axis=1)
        acc_td[0:feature, :] += dot_nn(side, cells)

    @pl.when(step == steps - 1)
    def _():
        def copy_of(k, r):
            return pltpu.make_async_copy(
                squares.at[jnp.maximum(idents[k * CAP + r], 0)],
                returns[k].at[pl.ds(r * slab, slab)],
                sems.at[k * CAP + r],
            )

        for k in range(devs):
            for r in range(CAP):
                copy_of(k, r).start()
        blocks = [acc_gu[:, c : c + width] for c in range(0, 2 * hidden, width)]
        blocks += [acc_out[:, c : c + width] for c in range(0, hidden, width)]
        blocks += [acc_td[...], jnp.concatenate([acc_gb[...], jnp.zeros((width - 16, width), F32)], axis=0)]
        half = len(blocks) // 2
        for i in range(half):
            rows_of = slice(i * width, (i + 1) * width)

            @pl.when(where_am[2] == 0)
            def _():
                keep[rows_of, :] = blocks[i]
                send[rows_of, :] = blocks[half + i]

            @pl.when(where_am[2] != 0)
            def _():
                keep[rows_of, :] = blocks[half + i]
                send[rows_of, :] = blocks[i]

        for k in range(devs):
            for r in range(CAP):
                copy_of(k, r).wait()


def heads_kernel(z_low, w_dist_t, out, wide):
    cols, bins, rows = out.shape
    wide[...] = z_low[...].astype(F32)

    def one(j, unused):
        column = wide[pl.ds(j, rows, stride=cols), :].astype(BF16)
        out[j] = dot_nt(w_dist_t[...], column).astype(BF16)
        return unused

    lax.fori_loop(0, cols, one, 0, unroll=8)


def logits_kernel(where_am, heads, got_a, got_b, out):
    straight = where_am[1] == 0
    low = low_lanes(heads.shape[1:])

    def one(p, unused):
        a, b = got_a[p].astype(F32), got_b[p].astype(F32)
        front, back = jnp.where(straight, a, b), jnp.where(straight, b, a)
        even = jnp.where(low, front, pltpu.roll(back, LANES // 2, 1))
        odd = jnp.where(low, pltpu.roll(front, LANES // 2, 1), back)
        out[2 * p] = (heads[2 * p].astype(F32) + even).astype(BF16)
        out[2 * p + 1] = (heads[2 * p + 1].astype(F32) + odd).astype(BF16)
        return unused

    lax.fori_loop(0, heads.shape[0] // 2, one, 0, unroll=4)


def tiles_kernel(devs, where_am, target, count, *refs):
    returned, (out, source) = refs[:devs], refs[devs:]
    feature, cells = out.shape[1:]
    groups = cells // LANES
    fill_slots(where_am[0], target, source, devs)
    for k in range(devs):
        for r in range(CAP):
            slot = source[k * CAP + r]

            @pl.when(slot >= 0)
            def _():
                scale = 1.0 / jnp.full((1, LANES), count[slot].astype(F32), F32)
                for c in range(groups):
                    at = (r * groups + c) * feature
                    part = returned[k][at : at + feature, :].astype(F32) * scale
                    out[slot, :, c * LANES : (c + 1) * LANES] = part.astype(BF16)


def weights_kernel(scale, where_am, mine, other, *outs):
    g_template, g_gain, g_bias, g_gate, g_up, g_out, g_dist = outs
    width, hidden = g_gate.shape
    feature = g_template.shape[0]
    half = mine.shape[0] // width
    lead = where_am[2] == 0
    per = hidden // width

    def block(i):
        source = slice(i % half * width, (i % half + 1) * width)
        here, there = mine[source, :], other[source, :]
        return (jnp.where(lead, here, there) if i < half else jnp.where(lead, there, here)) * scale

    for c in range(per):
        at = slice(c * width, (c + 1) * width)
        g_gate[:, at] = block(c)
        g_up[:, at] = block(per + c)
        g_out[at, :] = block(2 * per + c).T
    both = block(3 * per)
    g_template[...] = both[:feature, :]
    g_dist[...] = both[feature:, :]
    last = block(3 * per + 1)
    g_gain[...] = jnp.sum(last[0:8, :], axis=0, keepdims=True)
    g_bias[...] = jnp.sum(last[8:16, :], axis=0, keepdims=True)


def axis_groups(first, last):
    groups, bit = [], first
    while bit < last:
        wide = 2 if (last - bit) % 2 == 0 or last - bit > 2 else 1
        if (last - bit) % 2 == 1:
            wide = 1
        groups.append([m << bit for m in range(1, 1 << wide)])
        bit += wide
    return groups


def exchange_sum(value, axis, masks):
    size = lax.axis_size(axis)
    low = value.astype(BF16)
    got = [lax.ppermute(low, axis, [(i, i ^ m) for i in range(size)]) for m in masks]
    terms = [low.astype(F32)] + [g.astype(F32) for g in got]
    while len(terms) > 1:
        terms = [terms[i] + terms[i + 1] for i in range(0, len(terms), 2)]
    return terms[0]


def per_device(
    pair,
    logit_cotangent,
    tiles,
    tile_target,
    tile_square,
    tile_count,
    w_template,
    transition_norm_gain,
    transition_norm_bias,
    w_gate,
    w_up,
    w_out,
    w_dist,
):
    row_devs = lax.axis_size("row")
    col_devs = lax.axis_size("col")
    rows, cols, width = pair.shape
    bins = w_dist.shape[1]
    hidden = w_gate.shape[1]
    slots, cells_sq, feature = tiles.shape
    groups = cells_sq // LANES
    slab = groups * feature
    entries = rows * cols
    halves = rows // cols
    my_row, my_col = lax.axis_index("row"), lax.axis_index("col")
    where_am = jnp.stack([my_col, my_col % halves, my_row % 2]).astype(jnp.int32)
    target = tile_target[:, 0]
    tiles_t = jnp.transpose(tiles, (0, 2, 1))
    cot_t = jnp.transpose(logit_cotangent, (1, 2, 0))
    w_dist_t = w_dist.T

    def mirror(values):
        moved = []
        for s, value in enumerate(values):
            perm = [
                (r * col_devs + c, (c // halves) * col_devs + halves * r + ((c % halves) ^ s))
                for r in range(row_devs)
                for c in range(col_devs)
            ]
            moved.append(lax.ppermute(value, ("row", "col"), perm))
        return moved

    def shifted(values, sign):
        return [values[0]] + [
            lax.ppermute(values[k], "col", [(i, (i + sign * k) % col_devs) for i in range(col_devs)])
            for k in range(1, col_devs)
        ]

    half_shape = jax.ShapeDtypeStruct((cols // 2, bins, LANES), BF16)
    packed = pl.pallas_call(
        functools.partial(pack_kernel, col_devs),
        out_shape=[jax.ShapeDtypeStruct((CAP * slab + META, LANES), BF16)] * col_devs + [half_shape] * 2,
        in_specs=[SMEM] * 4 + [VMEM] * 2,
        out_specs=[VMEM] * (col_devs + 2),
        scratch_shapes=[pltpu.SMEM((col_devs * CAP,), jnp.int32)],
        compiler_params=params(),
        name="pack",
    )(where_am, target, tile_square, tile_count, tiles_t, cot_t)
    payloads = shifted(packed[:col_devs], 1)
    got_cot = mirror(packed[col_devs:])

    dheads = pl.pallas_call(
        cotangent_kernel,
        out_shape=jax.ShapeDtypeStruct((entries, bins), BF16),
        in_specs=[SMEM] + [VMEM] * 3,
        out_specs=VMEM,
        scratch_shapes=[pltpu.VMEM((entries, LANES), F32)],
        compiler_params=params(),
        name="cotangent",
    )(where_am, cot_t, *got_cot)

    block = STEP_ROWS * cols
    steps = entries // block
    squares = entries // cells_sq
    per_step = lambda lanes: pl.BlockSpec((block, lanes), lambda t: (t, 0))
    whole = lambda *shape: pl.BlockSpec(shape, lambda t: (0,) * len(shape))
    blocks = 3 * hidden // width + 2
    sum_shape = (blocks // 2 * width, width)
    operands = (
        w_template,
        transition_norm_gain[None, :],
        transition_norm_bias[None, :],
        w_gate,
        w_up,
        w_out,
        w_gate.T,
        w_up.T,
        w_out.T,
        w_dist_t,
    )
    outs = pl.pallas_call(
        functools.partial(main_kernel, col_devs, cols),
        grid=(steps,),
        out_shape=[
            jax.ShapeDtypeStruct((entries, width), F32),
            jax.ShapeDtypeStruct((entries, width), BF16),
            half_shape,
            half_shape,
        ]
        + [jax.ShapeDtypeStruct((CAP * slab, LANES), BF16)] * col_devs
        + [jax.ShapeDtypeStruct(sum_shape, F32)] * 2,
        in_specs=[SMEM]
        + [whole(CAP * slab + META, LANES)] * col_devs
        + [per_step(width), per_step(bins)]
        + [whole(*operand.shape) for operand in operands],
        out_specs=[per_step(width), per_step(width), whole(*half_shape.shape), whole(*half_shape.shape)]
        + [ANY] * col_devs
        + [whole(*sum_shape)] * 2,
        scratch_shapes=[
            pltpu.SMEM((col_devs * CAP,), jnp.int32),
            pltpu.VMEM((squares * slab, LANES), F32),
            pltpu.VMEM((squares * slab, LANES), BF16),
            pltpu.VMEM((squares, slab, LANES), BF16),
            pltpu.VMEM((width, 2 * hidden), F32),
            pltpu.VMEM((width, hidden), F32),
            pltpu.VMEM((feature + bins, width), F32),
            pltpu.VMEM((16, width), F32),
            pltpu.VMEM((block, 2 * hidden), BF16),
            pltpu.VMEM((block, hidden), BF16),
            pltpu.SemaphoreType.DMA((col_devs * CAP,)),
        ],
        compiler_params=params(),
        name="transition",
    )(where_am, *payloads, pair.reshape(entries, width), dheads, *operands)
    grad_pair, z_low, heads_a, heads_b = outs[:4]
    returns = outs[4 : 4 + col_devs]
    keep, send = outs[4 + col_devs :]

    sums = keep + lax.ppermute(send, "row", [(i, i ^ 1) for i in range(row_devs)])
    got_heads = mirror([heads_a, heads_b])
    returned = shifted(returns, -1)
    for axis, first, size in (("row", 1, row_devs), ("col", 0, col_devs)):
        for masks in axis_groups(first, size.bit_length() - 1):
            sums = exchange_sum(sums, axis, masks)
    other = lax.ppermute(sums, "row", [(i, i ^ 1) for i in range(row_devs)])

    heads = pl.pallas_call(
        heads_kernel,
        out_shape=jax.ShapeDtypeStruct((cols, bins, rows), BF16),
        in_specs=[VMEM] * 2,
        out_specs=VMEM,
        scratch_shapes=[pltpu.VMEM((entries, width), F32)],
        compiler_params=params(),
        name="own_heads",
    )(z_low, w_dist_t)
    logits = pl.pallas_call(
        logits_kernel,
        out_shape=jax.ShapeDtypeStruct((cols, bins, rows), BF16),
        in_specs=[SMEM] + [VMEM] * 3,
        out_specs=VMEM,
        compiler_params=params(),
        name="logits",
    )(where_am, heads, *got_heads)
    grad_tiles = pl.pallas_call(
        functools.partial(tiles_kernel, col_devs),
        out_shape=jax.ShapeDtypeStruct((slots, feature, cells_sq), BF16),
        in_specs=[SMEM] * 3 + [VMEM] * col_devs,
        out_specs=VMEM,
        scratch_shapes=[pltpu.SMEM((col_devs * CAP,), jnp.int32)],
        compiler_params=params(),
        name="tile_gradients",
    )(where_am, target, tile_count, *returned)
    length = rows * row_devs
    weights = pl.pallas_call(
        functools.partial(weights_kernel, 1.0 / length),
        out_shape=[
            jax.ShapeDtypeStruct((feature, width), F32),
            jax.ShapeDtypeStruct((1, width), F32),
            jax.ShapeDtypeStruct((1, width), F32),
            jax.ShapeDtypeStruct((width, hidden), F32),
            jax.ShapeDtypeStruct((width, hidden), F32),
            jax.ShapeDtypeStruct((hidden, width), F32),
            jax.ShapeDtypeStruct((bins, width), F32),
        ],
        in_specs=[SMEM] + [VMEM] * 2,
        out_specs=[VMEM] * 7,
        compiler_params=params(),
        name="weight_gradients",
    )(where_am, sums, other)
    g_template, g_gain, g_bias, g_gate, g_up, g_out, g_dist = weights
    return (
        jnp.transpose(logits, (2, 0, 1)),
        grad_pair.reshape(rows, cols, width),
        jnp.transpose(grad_tiles, (0, 2, 1)),
        g_template,
        g_gain[0],
        g_bias[0],
        g_gate,
        g_up,
        g_out,
        g_dist.T,
    )


def solution(mesh):
    split = P("row", "col", None)
    held = P(("row", "col"), None, None)
    return jax.shard_map(
        per_device,
        mesh=mesh,
        in_specs=(split, split, held, P(("row", "col"), None), P(("row", "col")), P(("row", "col")))
        + (P(),) * 7,
        out_specs=(split, split, held) + (P(),) * 7,
        check_vma=False,
    )
```

time: 742 us -> 287 us (0.39); the launches traced: 730 us -> 287 us
  waiting for transfers between devices: 348 us -> 151 us
  local copies, waits for them, and re-layouts: 139 us -> 4.87 us
  matrix products: 91 us -> 0 us
  other arithmetic: 70.7 us -> 1.38 us
  Pallas kernels: 0 us -> 61.3 us
  between operations: 15 us -> 0.99 us
    psum x2 -> x0, waiting for transfers between devices: 268 us -> none  [per_device(): lax.psum((g_template, sums[0], sums[1], sums[2], sums[3], sums[4], g_dist...]
    ppermute x0 -> x25, waiting for transfers between devices: none -> 151 us  [the longest x14 108 us: shifted(): lax.ppermute(values[k], 'col', [(i, (i + sign * k) % col_devs) for i in r...]
    dot_general x48 -> x0, matrix products: 91 us -> none  [the longest x4 18.8 us: transition_forward(): jnp.dot(hidden, w_out, preferred_element_type=jnp.float32)]
    all_to_all x10 -> x0, waiting for transfers between devices: 79.3 us -> none  [the longest x2 31.7 us: mirror(): lax.all_to_all(block, 'col', split_axis=0, concat_axis=1, tiled=True)]
    ppermute x0 -> x25, starting transfers between devices: none -> 67.5 us  [the longest x14 47.6 us: shifted(): lax.ppermute(values[k], 'col', [(i, (i + sign * k) % col_devs) for i in r...]
    all_to_all x10 -> x0, starting transfers between devices: 65.2 us -> none  [the longest x2 14.2 us: mirror(): lax.all_to_all(split, ('row', 'col'), split_axis=1, concat_axis=0, tiled=...]
    pallas_call x0 -> x7, Pallas kernels: none -> 61.3 us  [the longest x1 36.1 us: per_device(): pl.pallas_call(functools.partial(main_kernel, col_devs, cols), grid=(step...]
    unnamed x71 -> x49, local copies, waits for them, and re-layouts: 50.6 us -> 4.87 us
  transfers between devices with their start and end apart: 12 -> 25, of which waited for: 7 -> 12; matrix products, arithmetic and copies ran while one was open for 38% -> 0% of each run, Pallas kernels for 0% -> 7%
where the time goes in v1:
time: 287 us
  waiting for transfers between devices  151 us (53%)
  starting transfers between devices  67.5 us (24%)
  Pallas kernels  61.3 us (21%)
  local copies, waits for them, and re-layouts  4.87 us (2%)
    ppermute x14, waiting for transfers between devices, shifted(): lax.ppermute(values[k], 'col', [(i, (i + sign * k) % col_devs) for i in r...  108 us
    ppermute x14, starting transfers between devices, shifted(): lax.ppermute(values[k], 'col', [(i, (i + sign * k) % col_devs) for i in r...  47.6 us
    ppermute x5, waiting for transfers between devices, exchange_sum(): lax.ppermute(low, axis, [(i, i ^ m) for i in range(size)])  41 us
    pallas_call x1, Pallas kernels, per_device(): pl.pallas_call(functools.partial(main_kernel, col_devs, cols), grid=(step...  36.1 us
    ppermute x5, starting transfers between devices, exchange_sum(): lax.ppermute(low, axis, [(i, i ^ m) for i in range(size)])  9.59 us
    pallas_call x1, Pallas kernels, per_device(): pl.pallas_call(cotangent_kernel, out_shape=jax.ShapeDtypeStruct((entries,...  7.8 us
    ppermute x1, starting transfers between devices, per_device(): other = lax.ppermute(sums, 'row', [(i, i ^ 1) for i in range(row_devs)])  6.25 us
  transfers between devices with their start and end apart: 25, of which 12 were waited for; matrix products, arithmetic and copies ran while one was open for 0% of the time, Pallas kernels for 7%

profile of v1, /device:TPU:18, one launch (start us, length us, event | category | flops | bytes accessed | tf_op | source)
XLA Modules:
  0.0 286.6 jit_solution(1313338354863528235)
XLA Ops:
  2.8 4.5 %pack.1 = (bf16[1040,128]{1,0:T(8,128)(2,1)S(1)}, bf16[1040,128]{1,0:T(8,128)(2,1)S(1)}, bf16[1040,128]{1,0:T(8,128)(2,1)S(1)}, bf16[1040,128]{1,0:T(8,128)(2,1)...) custom-call(s32[3]{0:T(128)S(1)} %pad_add_fusion.where_am.refs_0_, ...), custom_call_target="tpu_custom_call" | custom-call | tf_op jit(solution)/shard_map/pack/pallas_call | solution.py:415
  8.0 1.7 collective-permute-start.7
  11.7 3.0 %collective-permute-start.1 = (bf16[1040,128]{1,0:T(8,128)(2,1)S(1)}, bf16[1040,128]{1,0:T(8,128)(2,1)S(1)}, u32[]{:S(2)}, u32[]{:S(2)}) collective-permute-start(bf16[1040,128]{1,0:T(8,128)(2,1)S(1)} %get-tuple-element.43), channel_id=1, source_target_pairs={{0,2},{1,3},{2,4},{3,5},{4,6},{5,7},{6,0},{7,1},{8,10},{9,11},{10,... | collective-permute-start | bytes 798728 | tf_op jit(solution)/shard_map/ppermute | solution.py:410
  14.7 3.1 %collective-permute-start.2 = (bf16[1040,128]{1,0:T(8,128)(2,1)S(1)}, bf16[1040,128]{1,0:T(8,128)(2,1)}, u32[]{:S(2)}, u32[]{:S(2)}) collective-permute-start(bf16[1040,128]{1,0:T(8,128)(2,1)S(1)} %get-tuple-element.44), channel_id=1, source_target_pairs={{0,3},{1,4},{2,5},{3,6},{4,7},{5,0},{6,1},{7,2},{8,11},{9,12},{10,... | collective-permute-start | bytes 798728 | tf_op jit(solution)/shard_map/ppermute | solution.py:410
  17.8 63.6 %collective-permute-done.refs_2_ = bf16[1040,128]{1,0:T(8,128)(2,1)S(1)} collective-permute-done((bf16[1040,128]{1,0:T(8,128)(2,1)S(1)}, bf16[1040,128]{1,0:T(8,128)(2,1)S(1)}, u32[]{:S(2)}, u32[]{:S(2)}) %collective-permute-start) | collective-permute-done | bytes 266272 | tf_op jit(solution)/shard_map/ppermute | solution.py:410
  81.5 2.4 collective-permute-start.5
  83.9 2.9 %collective-permute-start.6 = (bf16[1040,128]{1,0:T(8,128)(2,1)}, bf16[1040,128]{1,0:T(8,128)(2,1)}, u32[]{:S(2)}, u32[]{:S(2)}) collective-permute-start(bf16[1040,128]{1,0:T(8,128)(2,1)} %get-tuple-element.48), channel_id=1, source_target_pairs={{0,7},{1,0},{2,1},{3,2},{4,3},{5,4},{6,5},{7,6},{8,15},{9,8},{10,9... | collective-permute-start | bytes 798728 | tf_op jit(solution)/shard_map/ppermute | solution.py:410
  87.2 7.8 %cotangent.1.refs_10_ = bf16[8192,64]{1,0:T(8,128)(2,1)} custom-call(s32[3]{0:T(128)S(1)} %pad_add_fusion.where_am.refs_0_, bf16[64,64,128]{2,1,0:T(8,128)(2,1)} %bitcast.30, bf16[32,64,128]{2,1,0:T(8,128)(2,1)S(1)} %collective-permute-done.7.got_a, bf16[32,64,128]{2,1,0:T(8,128)(2,1)S(1)} %collective-permute-done.8.got_b), custom_call_target="tpu_custom_call" | custom-call | tf_op jit(solution)/shard_map/cotangent/pallas_call | solution.py:427
  95.1 4.6 %collective-permute-done.4.refs_6_ = bf16[1040,128]{1,0:T(8,128)(2,1)} collective-permute-done((bf16[1040,128]{1,0:T(8,128)(2,1)S(1)}, bf16[1040,128]{1,0:T(8,128)(2,1)}, u32[]{:S(2)}, u32[]{:S(2)}) %collective-permute-start.4) | collective-permute-done | bytes 266272 | tf_op jit(solution)/shard_map/ppermute | solution.py:410
  99.7 5.7 %collective-permute-done.5.refs_7_ = bf16[1040,128]{1,0:T(8,128)(2,1)} collective-permute-done((bf16[1040,128]{1,0:T(8,128)(2,1)S(1)}, bf16[1040,128]{1,0:T(8,128)(2,1)}, u32[]{:S(2)}, u32[]{:S(2)}) %collective-permute-start.5) | collective-permute-done | bytes 266272 | tf_op jit(solution)/shard_map/ppermute | solution.py:410
  105.4 5.7 %collective-permute-done.6.refs_8_ = bf16[1040,128]{1,0:T(8,128)(2,1)} collective-permute-done((bf16[1040,128]{1,0:T(8,128)(2,1)}, bf16[1040,128]{1,0:T(8,128)(2,1)}, u32[]{:S(2)}, u32[]{:S(2)}) %collective-permute-start.6) | collective-permute-done | bytes 266272 | tf_op jit(solution)/shard_map/ppermute | solution.py:410
  111.0 36.1 %transition.1 = (f32[8192,128]{1,0:T(8,128)}, bf16[8192,128]{1,0:T(8,128)(2,1)}, bf16[32,64,128]{2,1,0:T(8,128)(2,1)}, bf16[32,64,128]{2,1,0:T(8,128)(2,1)}, bf1...) custom-call(s32[3]{0:T(128)S(1)} %pad_add_fusion.where_am.refs_0_, ...), custom_call_target="tpu_custom_call" | custom-call | tf_op jit(solution)/shard_map/transition/pallas_call | solution.py:456
  147.3 2.0 collective-permute-done.18
  150.4 7.6 %collective-permute-done.19 = bf16[896,128]{1,0:T(8,128)(2,1)S(1)} collective-permute-done((bf16[896,128]{1,0:T(8,128)(2,1)S(1)}, bf16[896,128]{1,0:T(8,128)(2,1)S(1)}, u32[]{:S(2)}, u32[]{:S(2)}) %collective-permute-start.19) | collective-permute-done | bytes 229408 | tf_op jit(solution)/shard_map/ppermute | solution.py:358
  158.2 3.5 %collective-permute-start.11 = (bf16[1024,128]{1,0:T(8,128)(2,1)S(1)}, bf16[1024,128]{1,0:T(8,128)(2,1)S(1)}, u32[]{:S(2)}, u32[]{:S(2)}) collective-permute-start(bf16[1024,128]{1,0:T(8,128)(2,1)S(1)} %get-tuple-element.56), channel_id=1, source_target_pairs={{0,7},{1,0},{2,1},{3,2},{4,3},{5,4},{6,5},{7,6},{8,15},{9,8},{10,9... | collective-permute-start | bytes 786440 | tf_op jit(solution)/shard_map/ppermute | solution.py:410
  162.2 4.6 %collective-permute-done.20 = bf16[896,128]{1,0:T(8,128)(2,1)S(1)} collective-permute-done((bf16[896,128]{1,0:T(8,128)(2,1)S(1)}, bf16[896,128]{1,0:T(8,128)(2,1)S(1)}, u32[]{:S(2)}, u32[]{:S(2)}) %collective-permute-start.20) | collective-permute-done | bytes 229408 | tf_op jit(solution)/shard_map/ppermute | solution.py:358
  166.8 5.4 %collective-permute-start.23 = (bf16[896,128]{1,0:T(8,128)(2,1)S(1)}, bf16[896,128]{1,0:T(8,128)(2,1)S(1)}, u32[]{:S(2)}, u32[]{:S(2)}) collective-permute-start(bf16[896,128]{1,0:T(8,128)(2,1)S(1)} %add_convert_fusion), channel_id=1, source_target_pairs={{0,6},{1,7},{2,4},{3,5},{4,2},{5,3},{6,0},{7,1},{8,14},{9,15},{10,... | collective-permute-start | bytes 688136 | tf_op jit(solution)/shard_map/ppermute | solution.py:358
  172.2 4.0 %collective-permute-start.22 = (bf16[896,128]{1,0:T(8,128)(2,1)S(1)}, bf16[896,128]{1,0:T(8,128)(2,1)S(1)}, u32[]{:S(2)}, u32[]{:S(2)}) collective-permute-start(bf16[896,128]{1,0:T(8,128)(2,1)S(1)} %add_convert_fusion), channel_id=1, source_target_pairs={{0,4},{1,5},{2,6},{3,7},{4,0},{5,1},{6,2},{7,3},{8,12},{9,13},{10,... | collective-permute-start | bytes 688136 | tf_op jit(solution)/shard_map/ppermute | solution.py:358
  176.3 2.5 collective-permute-start.13
  178.8 2.3 collective-permute-start.14
  181.1 12.2 %collective-permute-done.23 = bf16[896,128]{1,0:T(8,128)(2,1)S(1)} collective-permute-done((bf16[896,128]{1,0:T(8,128)(2,1)S(1)}, bf16[896,128]{1,0:T(8,128)(2,1)S(1)}, u32[]{:S(2)}, u32[]{:S(2)}) %collective-permute-start.23) | collective-permute-done | bytes 229408 | tf_op jit(solution)/shard_map/ppermute | solution.py:358
  193.3 16.5 %collective-permute-done.22 = bf16[896,128]{1,0:T(8,128)(2,1)S(1)} collective-permute-done((bf16[896,128]{1,0:T(8,128)(2,1)S(1)}, bf16[896,128]{1,0:T(8,128)(2,1)S(1)}, u32[]{:S(2)}, u32[]{:S(2)}) %collective-permute-start.22) | collective-permute-done | bytes 229408 | tf_op jit(solution)/shard_map/ppermute | solution.py:358
  210.8 4.7 %collective-permute-done.13.refs_3_ = bf16[1024,128]{1,0:T(8,128)(2,1)S(1)} collective-permute-done((bf16[1024,128]{1,0:T(8,128)(2,1)S(1)}, bf16[1024,128]{1,0:T(8,128)(2,1)S(1)}, u32[]{:S(2)}, u32[]{:S(2)}) %collective-permute-start.13) | collective-permute-done | bytes 262176 | tf_op jit(solution)/shard_map/ppermute | solution.py:410
  215.4 6.2 %collective-permute-start.24 = (f32[896,128]{1,0:T(8,128)S(1)}, f32[896,128]{1,0:T(8,128)S(1)}, u32[]{:S(2)}, u32[]{:S(2)}) collective-permute-start(f32[896,128]{1,0:T(8,128)S(1)} %add_add_fusion.mine), channel_id=1, source_target_pairs={{0,8},{8,0},{16,24},{24,16},{1,9},{9,1},{17,25},{25,17},{2,10},{10... | collective-permute-start | bytes 1376264 | tf_op jit(solution)/shard_map/ppermute | solution.py:500
  221.7 21.3 %collective-permute-start.16 = (bf16[1024,128]{1,0:T(8,128)(2,1)S(1)}, bf16[1024,128]{1,0:T(8,128)(2,1)S(1)}, u32[]{:S(2)}, u32[]{:S(2)}) collective-permute-start(bf16[1024,128]{1,0:T(8,128)(2,1)S(1)} %copy-done.20), channel_id=1, source_target_pairs={{0,2},{1,3},{2,4},{3,5},{4,6},{5,7},{6,0},{7,1},{8,10},{9,11},{10,... | collective-permute-start | bytes 786440 | tf_op jit(solution)/shard_map/ppermute | solution.py:410
  243.0 5.6 %collective-permute-start.17 = (bf16[1024,128]{1,0:T(8,128)(2,1)S(1)}, bf16[1024,128]{1,0:T(8,128)(2,1)S(1)}, u32[]{:S(2)}, u32[]{:S(2)}) collective-permute-start(bf16[1024,128]{1,0:T(8,128)(2,1)S(1)} %copy-done.19), channel_id=1, source_target_pairs={{0,1},{1,2},{2,3},{3,4},{4,5},{5,6},{6,7},{7,0},{8,9},{9,10},{10,1... | collective-permute-start | bytes 786440 | tf_op jit(solution)/shard_map/ppermute | solution.py:410
  248.6 5.1 %own_heads.1.heads = bf16[64,64,128]{2,1,0:T(8,128)(2,1)S(1)} custom-call(bf16[8192,128]{1,0:T(8,128)(2,1)} %get-tuple-element.51.z_low, bf16[64,128]{1,0:T(8,128)(2,1)S(1)} %bitcast.23), custom_call_target="tpu_custom_call" | custom-call | tf_op jit(solution)/shard_map/own_heads/pallas_call | solution.py:502
  254.7 20.4 %collective-permute-done.16.refs_6_ = bf16[1024,128]{1,0:T(8,128)(2,1)S(1)} collective-permute-done((bf16[1024,128]{1,0:T(8,128)(2,1)S(1)}, bf16[1024,128]{1,0:T(8,128)(2,1)S(1)}, u32[]{:S(2)}, u32[]{:S(2)}) %collective-permute-start.16) | collective-permute-done | bytes 262176 | tf_op jit(solution)/shard_map/ppermute | solution.py:410
  275.1 2.9 %collective-permute-done.17.refs_7_ = bf16[1024,128]{1,0:T(8,128)(2,1)S(1)} collective-permute-done((bf16[1024,128]{1,0:T(8,128)(2,1)S(1)}, bf16[1024,128]{1,0:T(8,128)(2,1)S(1)}, u32[]{:S(2)}, u32[]{:S(2)}) %collective-permute-start.17) | collective-permute-done | bytes 262176 | tf_op jit(solution)/shard_map/ppermute | solution.py:410
  278.7 3.3 %tile_gradients.1 = bf16[16,64,1024]{2,1,0:T(8,128)(2,1)} custom-call(s32[3]{0:T(128)S(1)} %pad_add_fusion.where_am.refs_0_, s32[16]{0:T(128)S(1)} %bitcast.25, s32[16]{0:T(128)S(1)} %copy-done.10, bf16[1024,128]{1,0:T(8,128)(2,1)S(1)} %get-tuple-element.55.refs_0_, bf16[1024,128]{1,0:T(8,128)(2,1)S(1)} %collective-permute-done.11.refs_1_, ...), custom_call_target="tpu_custom_call" | custom-call | tf_op jit(solution)/shard_map/tile_gradients/pallas_call | solution.py:519
  281.9 3.1 %logits.1 = bf16[64,64,128]{2,1,0:T(8,128)(2,1)} custom-call(s32[3]{0:T(128)S(1)} %pad_add_fusion.where_am.refs_0_, bf16[64,64,128]{2,1,0:T(8,128)(2,1)} %copy-done, bf16[32,64,128]{2,1,0:T(8,128)(2,1)S(1)} %collective-permute-done.9.got_a, bf16[32,64,128]{2,1,0:T(8,128)(2,1)S(1)} %collective-permute-done.10.got_b), custom_call_target="tpu_custom_call" | custom-call | tf_op jit(solution)/shard_map/logits/pallas_call | solution.py:511
  285.0 1.5 weight_gradients.1
  (79 shorter events, 9.8 us)
Async XLA Ops:
  0.6 86.2 %copy-start.1 = (bf16[128,512]{1,0:T(8,128)(2,1)S(1)}, bf16[128,512]{1,0:T(8,128)(2,1)}, u32[]{:S(2)}) copy-start(bf16[128,512]{1,0:T(8,128)(2,1)} %refs_14_.1) | copy-start | bytes 393220
  0.7 86.3 %copy-start.2 = (bf16[128,512]{1,0:T(8,128)(2,1)S(1)}, bf16[128,512]{1,0:T(8,128)(2,1)}, u32[]{:S(2)}) copy-start(bf16[128,512]{1,0:T(8,128)(2,1)} %refs_15_.1) | copy-start | bytes 393220
  0.7 86.4 %copy-start.3 = (bf16[512,128]{1,0:T(8,128)(2,1)S(1)}, bf16[512,128]{1,0:T(8,128)(2,1)}, u32[]{:S(2)}) copy-start(bf16[512,128]{1,0:T(8,128)(2,1)} %refs_16_.1) | copy-start | bytes 393220
  8.0 73.5 %collective-permute-start.7 = (bf16[32,64,128]{2,1,0:T(8,128)(2,1)}, bf16[32,64,128]{2,1,0:T(8,128)(2,1)S(1)}, u32[]{:S(2)}, u32[]{:S(2)}) collective-permute-start(bf16[32,64,128]{2,1,0:T(8,128)(2,1)} %get-tuple-element.49), channel_id=1, source_target_pairs={{0,0},{1,1},{2,8},{3,9},{4,16},{5,17},{6,24},{7,25},{8,2},{9,3},{1... | collective-permute-start | bytes 1572872 | tf_op jit(solution)/shard_map/ppermute | solution.py:405
  9.7 74.2 %collective-permute-start.8 = (bf16[32,64,128]{2,1,0:T(8,128)(2,1)}, bf16[32,64,128]{2,1,0:T(8,128)(2,1)S(1)}, u32[]{:S(2)}, u32[]{:S(2)}) collective-permute-start(bf16[32,64,128]{2,1,0:T(8,128)(2,1)} %get-tuple-element.50), channel_id=1, source_target_pairs={{0,1},{1,0},{2,9},{3,8},{4,17},{5,16},{6,25},{7,24},{8,3},{9,2},{1... | collective-permute-start | bytes 1572872 | tf_op jit(solution)/shard_map/ppermute | solution.py:405
  11.2 70.2 %collective-permute-start = (bf16[1040,128]{1,0:T(8,128)(2,1)S(1)}, bf16[1040,128]{1,0:T(8,128)(2,1)S(1)}, u32[]{:S(2)}, u32[]{:S(2)}) collective-permute-start(bf16[1040,128]{1,0:T(8,128)(2,1)S(1)} %get-tuple-element.42), channel_id=1, source_target_pairs={{0,1},{1,2},{2,3},{3,4},{4,5},{5,6},{6,7},{7,0},{8,9},{9,10},{10,1... | collective-permute-start | bytes 798728 | tf_op jit(solution)/shard_map/ppermute | solution.py:410
  11.7 69.7 %collective-permute-start.1 = (bf16[1040,128]{1,0:T(8,128)(2,1)S(1)}, bf16[1040,128]{1,0:T(8,128)(2,1)S(1)}, u32[]{:S(2)}, u32[]{:S(2)}) collective-permute-start(bf16[1040,128]{1,0:T(8,128)(2,1)S(1)} %get-tuple-element.43), channel_id=1, source_target_pairs={{0,2},{1,3},{2,4},{3,5},{4,6},{5,7},{6,0},{7,1},{8,10},{9,11},{10,... | collective-permute-start | bytes 798728 | tf_op jit(solution)/shard_map/ppermute | solution.py:410
  14.7 80.3 %collective-permute-start.2 = (bf16[1040,128]{1,0:T(8,128)(2,1)S(1)}, bf16[1040,128]{1,0:T(8,128)(2,1)}, u32[]{:S(2)}, u32[]{:S(2)}) collective-permute-start(bf16[1040,128]{1,0:T(8,128)(2,1)S(1)} %get-tuple-element.44), channel_id=1, source_target_pairs={{0,3},{1,4},{2,5},{3,6},{4,7},{5,0},{6,1},{7,2},{8,11},{9,12},{10,... | collective-permute-start | bytes 798728 | tf_op jit(solution)/shard_map/ppermute | solution.py:410
  81.4 13.6 %collective-permute-start.3 = (bf16[1040,128]{1,0:T(8,128)(2,1)S(1)}, bf16[1040,128]{1,0:T(8,128)(2,1)}, u32[]{:S(2)}, u32[]{:S(2)}) collective-permute-start(bf16[1040,128]{1,0:T(8,128)(2,1)S(1)} %get-tuple-element.45), channel_id=1, source_target_pairs={{0,4},{1,5},{2,6},{3,7},{4,0},{5,1},{6,2},{7,3},{8,12},{9,13},{10,... | collective-permute-start | bytes 798728 | tf_op jit(solution)/shard_map/ppermute | solution.py:410
  81.4 18.2 %collective-permute-start.4 = (bf16[1040,128]{1,0:T(8,128)(2,1)S(1)}, bf16[1040,128]{1,0:T(8,128)(2,1)}, u32[]{:S(2)}, u32[]{:S(2)}) collective-permute-start(bf16[1040,128]{1,0:T(8,128)(2,1)S(1)} %get-tuple-element.46), channel_id=1, source_target_pairs={{0,5},{1,6},{2,7},{3,0},{4,1},{5,2},{6,3},{7,4},{8,13},{9,14},{10,... | collective-permute-start | bytes 798728 | tf_op jit(solution)/shard_map/ppermute | solution.py:410
  81.5 23.9 %collective-permute-start.5 = (bf16[1040,128]{1,0:T(8,128)(2,1)S(1)}, bf16[1040,128]{1,0:T(8,128)(2,1)}, u32[]{:S(2)}, u32[]{:S(2)}) collective-permute-start(bf16[1040,128]{1,0:T(8,128)(2,1)S(1)} %get-tuple-element.47), channel_id=1, source_target_pairs={{0,6},{1,7},{2,0},{3,1},{4,2},{5,3},{6,4},{7,5},{8,14},{9,15},{10,... | collective-permute-start | bytes 798728 | tf_op jit(solution)/shard_map/ppermute | solution.py:410
  83.9 27.1 %collective-permute-start.6 = (bf16[1040,128]{1,0:T(8,128)(2,1)}, bf16[1040,128]{1,0:T(8,128)(2,1)}, u32[]{:S(2)}, u32[]{:S(2)}) collective-permute-start(bf16[1040,128]{1,0:T(8,128)(2,1)} %get-tuple-element.48), channel_id=1, source_target_pairs={{0,7},{1,0},{2,1},{3,2},{4,3},{5,4},{6,5},{7,6},{8,15},{9,8},{10,9... | collective-permute-start | bytes 798728 | tf_op jit(solution)/shard_map/ppermute | solution.py:410
  147.2 74.5 %copy-start.20 = (bf16[1024,128]{1,0:T(8,128)(2,1)S(1)}, bf16[1024,128]{1,0:T(8,128)(2,1)}, u32[]{:S(2)}) copy-start(bf16[1024,128]{1,0:T(8,128)(2,1)} %get-tuple-element.61) | copy-start | bytes 786436
  147.2 95.8 %copy-start.19 = (bf16[1024,128]{1,0:T(8,128)(2,1)S(1)}, bf16[1024,128]{1,0:T(8,128)(2,1)}, u32[]{:S(2)}) copy-start(bf16[1024,128]{1,0:T(8,128)(2,1)} %get-tuple-element.62) | copy-start | bytes 786436
  147.2 2.1 collective-permute-start.18
  150.4 7.7 %collective-permute-start.19 = (bf16[896,128]{1,0:T(8,128)(2,1)S(1)}, bf16[896,128]{1,0:T(8,128)(2,1)S(1)}, u32[]{:S(2)}, u32[]{:S(2)}) collective-permute-start(bf16[896,128]{1,0:T(8,128)(2,1)S(1)} %add_convert_fusion.2), channel_id=1, source_target_pairs={{0,16},{8,24},{16,0},{24,8},{1,17},{9,25},{17,1},{25,9},{2,18},{10... | collective-permute-start | bytes 688136 | tf_op jit(solution)/shard_map/ppermute | solution.py:358
  158.1 8.6 %collective-permute-start.20 = (bf16[896,128]{1,0:T(8,128)(2,1)S(1)}, bf16[896,128]{1,0:T(8,128)(2,1)S(1)}, u32[]{:S(2)}, u32[]{:S(2)}) collective-permute-start(bf16[896,128]{1,0:T(8,128)(2,1)S(1)} %add_convert_fusion.1), channel_id=1, source_target_pairs={{0,1},{1,0},{2,3},{3,2},{4,5},{5,4},{6,7},{7,6},{8,9},{9,8},{10,11... | collective-permute-start | bytes 688136 | tf_op jit(solution)/shard_map/ppermute | solution.py:358
  158.2 18.0 %collective-permute-start.11 = (bf16[1024,128]{1,0:T(8,128)(2,1)S(1)}, bf16[1024,128]{1,0:T(8,128)(2,1)S(1)}, u32[]{:S(2)}, u32[]{:S(2)}) collective-permute-start(bf16[1024,128]{1,0:T(8,128)(2,1)S(1)} %get-tuple-element.56), channel_id=1, source_target_pairs={{0,7},{1,0},{2,1},{3,2},{4,3},{5,4},{6,5},{7,6},{8,15},{9,8},{10,9... | collective-permute-start | bytes 786440 | tf_op jit(solution)/shard_map/ppermute | solution.py:410
  161.7 17.0 %collective-permute-start.12 = (bf16[1024,128]{1,0:T(8,128)(2,1)S(1)}, bf16[1024,128]{1,0:T(8,128)(2,1)S(1)}, u32[]{:S(2)}, u32[]{:S(2)}) collective-permute-start(bf16[1024,128]{1,0:T(8,128)(2,1)S(1)} %get-tuple-element.57), channel_id=1, source_target_pairs={{0,6},{1,7},{2,0},{3,1},{4,2},{5,3},{6,4},{7,5},{8,14},{9,15},{10,... | collective-permute-start | bytes 786440 | tf_op jit(solution)/shard_map/ppermute | solution.py:410
  166.8 26.5 %collective-permute-start.23 = (bf16[896,128]{1,0:T(8,128)(2,1)S(1)}, bf16[896,128]{1,0:T(8,128)(2,1)S(1)}, u32[]{:S(2)}, u32[]{:S(2)}) collective-permute-start(bf16[896,128]{1,0:T(8,128)(2,1)S(1)} %add_convert_fusion), channel_id=1, source_target_pairs={{0,6},{1,7},{2,4},{3,5},{4,2},{5,3},{6,0},{7,1},{8,14},{9,15},{10,... | collective-permute-start | bytes 688136 | tf_op jit(solution)/shard_map/ppermute | solution.py:358
  172.2 37.6 %collective-permute-start.22 = (bf16[896,128]{1,0:T(8,128)(2,1)S(1)}, bf16[896,128]{1,0:T(8,128)(2,1)S(1)}, u32[]{:S(2)}, u32[]{:S(2)}) collective-permute-start(bf16[896,128]{1,0:T(8,128)(2,1)S(1)} %add_convert_fusion), channel_id=1, source_target_pairs={{0,4},{1,5},{2,6},{3,7},{4,0},{5,1},{6,2},{7,3},{8,12},{9,13},{10,... | collective-permute-start | bytes 688136 | tf_op jit(solution)/shard_map/ppermute | solution.py:358
  176.2 34.3 %collective-permute-start.21 = (bf16[896,128]{1,0:T(8,128)(2,1)S(1)}, bf16[896,128]{1,0:T(8,128)(2,1)S(1)}, u32[]{:S(2)}, u32[]{:S(2)}) collective-permute-start(bf16[896,128]{1,0:T(8,128)(2,1)S(1)} %add_convert_fusion), channel_id=1, source_target_pairs={{0,2},{1,3},{2,0},{3,1},{4,6},{5,7},{6,4},{7,5},{8,10},{9,11},{10,... | collective-permute-start | bytes 688136 | tf_op jit(solution)/shard_map/ppermute | solution.py:358
  176.3 39.2 %collective-permute-start.13 = (bf16[1024,128]{1,0:T(8,128)(2,1)S(1)}, bf16[1024,128]{1,0:T(8,128)(2,1)S(1)}, u32[]{:S(2)}, u32[]{:S(2)}) collective-permute-start(bf16[1024,128]{1,0:T(8,128)(2,1)S(1)} %get-tuple-element.58), channel_id=1, source_target_pairs={{0,5},{1,6},{2,7},{3,0},{4,1},{5,2},{6,3},{7,4},{8,13},{9,14},{10,... | collective-permute-start | bytes 786440 | tf_op jit(solution)/shard_map/ppermute | solution.py:410
  178.8 42.9 %collective-permute-start.14 = (bf16[1024,128]{1,0:T(8,128)(2,1)S(1)}, bf16[1024,128]{1,0:T(8,128)(2,1)S(1)}, u32[]{:S(2)}, u32[]{:S(2)}) collective-permute-start(bf16[1024,128]{1,0:T(8,128)(2,1)S(1)} %copy-done.22), channel_id=1, source_target_pairs={{0,4},{1,5},{2,6},{3,7},{4,0},{5,1},{6,2},{7,3},{8,12},{9,13},{10,... | collective-permute-start | bytes 786440 | tf_op jit(solution)/shard_map/ppermute | solution.py:410
  193.3 49.6 %collective-permute-start.15 = (bf16[1024,128]{1,0:T(8,128)(2,1)S(1)}, bf16[1024,128]{1,0:T(8,128)(2,1)S(1)}, u32[]{:S(2)}, u32[]{:S(2)}) collective-permute-start(bf16[1024,128]{1,0:T(8,128)(2,1)S(1)} %copy-done.21), channel_id=1, source_target_pairs={{0,3},{1,4},{2,5},{3,6},{4,7},{5,0},{6,1},{7,2},{8,11},{9,12},{10,... | collective-permute-start | bytes 786440 | tf_op jit(solution)/shard_map/ppermute | solution.py:410
  209.8 72.1 %collective-permute-start.9 = (bf16[32,64,128]{2,1,0:T(8,128)(2,1)S(1)}, bf16[32,64,128]{2,1,0:T(8,128)(2,1)S(1)}, u32[]{:S(2)}, u32[]{:S(2)}) collective-permute-start(bf16[32,64,128]{2,1,0:T(8,128)(2,1)S(1)} %copy-done.18), channel_id=1, source_target_pairs={{0,0},{1,1},{2,8},{3,9},{4,16},{5,17},{6,24},{7,25},{8,2},{9,3},{1... | collective-permute-start | bytes 1572872 | tf_op jit(solution)/shard_map/ppermute | solution.py:405
  210.5 68.1 %copy-start.8 = (s32[16,1]{0,1:T(1,128)S(1)}, s32[16,1]{0,1:T(1,128)}, u32[]{:S(2)}) copy-start(s32[16,1]{0,1:T(1,128)} %param.16) | copy-start | bytes 196
  210.5 68.1 %copy-start.10 = (s32[16]{0:T(128)S(1)}, s32[16]{0:T(128)}, u32[]{:S(2)}) copy-start(s32[16]{0:T(128)} %count.3) | copy-start | bytes 196
  210.6 71.4 %collective-permute-start.10 = (bf16[32,64,128]{2,1,0:T(8,128)(2,1)S(1)}, bf16[32,64,128]{2,1,0:T(8,128)(2,1)S(1)}, u32[]{:S(2)}, u32[]{:S(2)}) collective-permute-start(bf16[32,64,128]{2,1,0:T(8,128)(2,1)S(1)} %copy-done.17), channel_id=1, source_target_pairs={{0,1},{1,0},{2,9},{3,8},{4,17},{5,16},{6,25},{7,24},{8,3},{9,2},{1... | collective-permute-start | bytes 1572872 | tf_op jit(solution)/shard_map/ppermute | solution.py:405
  215.4 69.6 %collective-permute-start.24 = (f32[896,128]{1,0:T(8,128)S(1)}, f32[896,128]{1,0:T(8,128)S(1)}, u32[]{:S(2)}, u32[]{:S(2)}) collective-permute-start(f32[896,128]{1,0:T(8,128)S(1)} %add_add_fusion.mine), channel_id=1, source_target_pairs={{0,8},{8,0},{16,24},{24,16},{1,9},{9,1},{17,25},{25,17},{2,10},{10... | collective-permute-start | bytes 1376264 | tf_op jit(solution)/shard_map/ppermute | solution.py:500
  221.7 53.4 %collective-permute-start.16 = (bf16[1024,128]{1,0:T(8,128)(2,1)S(1)}, bf16[1024,128]{1,0:T(8,128)(2,1)S(1)}, u32[]{:S(2)}, u32[]{:S(2)}) collective-permute-start(bf16[1024,128]{1,0:T(8,128)(2,1)S(1)} %copy-done.20), channel_id=1, source_target_pairs={{0,2},{1,3},{2,4},{3,5},{4,6},{5,7},{6,0},{7,1},{8,10},{9,11},{10,... | collective-permute-start | bytes 786440 | tf_op jit(solution)/shard_map/ppermute | solution.py:410
  243.0 35.0 %collective-permute-start.17 = (bf16[1024,128]{1,0:T(8,128)(2,1)S(1)}, bf16[1024,128]{1,0:T(8,128)(2,1)S(1)}, u32[]{:S(2)}, u32[]{:S(2)}) collective-permute-start(bf16[1024,128]{1,0:T(8,128)(2,1)S(1)} %copy-done.19), channel_id=1, source_target_pairs={{0,1},{1,2},{2,3},{3,4},{4,5},{5,6},{6,7},{7,0},{8,9},{9,10},{10,1... | collective-permute-start | bytes 786440 | tf_op jit(solution)/shard_map/ppermute | solution.py:410
  (16 other events, 330.8 us)

commit v2 on v1

v2 whole, which is shorter than its diff:
```python
import functools

import jax
import jax.numpy as jnp
from jax import lax
from jax.experimental import pallas as pl
from jax.experimental.pallas import tpu as pltpu
from jax.sharding import PartitionSpec as P

SQ = 32
CAP = 2
LANES = 128
META = 16
GROUP = LANES // SQ
PARTS = 2
PIECE = 256
VMEM_BYTES = 52 * 2**20
BF16 = jnp.bfloat16
F32 = jnp.float32

VMEM = pl.BlockSpec(memory_space=pltpu.VMEM)
SMEM = pl.BlockSpec(memory_space=pltpu.SMEM)
ANY = pl.BlockSpec(memory_space=pl.ANY)


def params():
    return pltpu.CompilerParams(vmem_limit_bytes=VMEM_BYTES)


def cost(micros):
    return pl.CostEstimate(flops=int(micros * 1.1e9), bytes_accessed=0, transcendentals=0)


def dot_nn(a, b):
    return lax.dot_general(a, b, (((1,), (0,)), ((), ())), preferred_element_type=F32)


def dot_nt(a, b):
    return lax.dot_general(a, b, (((1,), (1,)), ((), ())), preferred_element_type=F32)


def dot_tn(a, b):
    return lax.dot_general(a, b, (((0,), (0,)), ((), ())), preferred_element_type=F32)


def fill_slots(target, source, devs):
    def clear(i, unused):
        source[i] = -1
        return unused

    def place(s, unused):
        place_of = target[s] * CAP
        taken = source[place_of] >= 0
        source[place_of + jnp.where(taken, 1, 0)] = s
        return unused

    lax.fori_loop(0, devs * CAP, clear, 0)
    lax.fori_loop(0, target.shape[0], place, 0)


def low_lanes(shape):
    return lax.broadcasted_iota(jnp.int32, shape, 1) < LANES // 2


def pack_kernel(devs, where_am, target, square, count, tiles, cot, *refs):
    payloads, (cot_a, cot_b, source) = refs[:PARTS], refs[PARTS:]
    feature, cells = tiles.shape[1:]
    groups = cells // LANES
    per_part = groups // PARTS
    fill_slots(target, source, devs)
    first = where_am[0] == 0
    low = low_lanes(cot.shape[1:])

    def pack_pair(p, unused):
        even, odd = cot[2 * p].astype(F32), cot[2 * p + 1].astype(F32)
        front = jnp.where(low, even, pltpu.roll(odd, LANES // 2, 1)).astype(BF16)
        back = jnp.where(low, pltpu.roll(even, LANES // 2, 1), odd).astype(BF16)
        cot_a[p] = jnp.where(first, front, back)
        cot_b[p] = jnp.where(first, back, front)
        return unused

    lax.fori_loop(0, cot.shape[0] // 2, pack_pair, 0, unroll=4)
    line = lax.broadcasted_iota(jnp.int32, (META, LANES), 0)
    for k in range(devs):
        meta = jnp.zeros((META, LANES), F32)
        for r in range(CAP):
            slot = source[k * CAP + r]
            held = jnp.maximum(slot, 0)
            ident = jnp.where(slot >= 0, square[held], -1).astype(F32)
            meta = jnp.where(line == r, ident, meta)
            meta = jnp.where(line == 8 + r, count[held].astype(F32), meta)
            for c in range(groups):
                at = (r * per_part + c % per_part) * feature
                payloads[c // per_part][k, at : at + feature, :] = tiles[held, :, c * LANES : (c + 1) * LANES]
        for payload in payloads:
            payload[k, CAP * per_part * feature :, :] = meta.astype(BF16)


def arrived(where_am, direct, routed, p):
    return jnp.where(where_am[2] != 0, routed[p].astype(F32), direct[p].astype(F32))


def turn_kernel(cot, out, turned):
    cols, bins, rows = cot.shape

    def turn(j, unused):
        turned[pl.ds(j, rows, stride=cols), 0:bins] = cot[j].astype(F32).T
        return unused

    lax.fori_loop(0, cols, turn, 0, unroll=4)
    out[...] = turned[:, 0:bins].astype(BF16)


def fold_rows(values):
    return jnp.sum(values.reshape(values.shape[0] // 8, 8, values.shape[1]), axis=0)


def share_out(where_am, sums, keep, send):
    acc_gu, acc_out, acc_td, acc_gb = sums
    width = acc_gu.shape[0]
    blocks = [acc_gu[:, c : c + width] for c in range(0, acc_gu.shape[1], width)]
    blocks += [acc_out[:, c : c + width] for c in range(0, acc_out.shape[1], width)]
    blocks += [acc_td[...], jnp.concatenate([acc_gb[...], jnp.zeros((width - 16, width), F32)], axis=0)]
    half = len(blocks) // 2
    for i in range(half):
        rows = slice(i * width, (i + 1) * width)

        @pl.when(where_am[1] == 0)
        def _():
            keep[rows, :] = blocks[i]
            send[rows, :] = blocks[half + i]

        @pl.when(where_am[1] != 0)
        def _():
            keep[rows, :] = blocks[half + i]
            send[rows, :] = blocks[i]


def main_kernel(devs, cols, part, *refs):
    (where_am, payloads), refs = refs[:2], refs[2:]
    (pair, turned, got_a, got_b, got_c), refs = refs[:5], refs[5:]
    (w_template, gain, bias, w_gate, w_up, w_out, w_gate_t, w_up_t, w_out_t, w_dist_t), refs = refs[:10], refs[10:]
    last = part == PARTS - 1
    if part:
        carried, refs = refs[1:5], refs[5:]
    (grad_pair, z_low_out, heads_a, heads_b, returns), refs = refs[:5], refs[5:]
    if last:
        (keep, send), refs = refs[:2], refs[2:]
    acc_gu, acc_out, acc_td, acc_gb = sums = refs[:4]
    idents, total, summed, squares, low_gu, low_hid, sems = refs[4:]
    step = pl.program_id(0)
    steps = pl.num_programs(0)
    feature, width = w_template.shape
    hidden = w_gate.shape[1]
    groups = SQ * SQ // LANES
    slab = groups // PARTS * feature
    block = pair.shape[0]
    rows = block // cols
    sq_cols = cols // SQ
    per_part = groups // PARTS

    @pl.when(step == 0)
    def _():
        total[...] = jnp.zeros_like(total)
        for i, acc in enumerate(sums):
            acc[...] = carried[i][...] if part else jnp.zeros_like(acc)
        for k in range(devs):
            meta = payloads[k, CAP * slab :, :].astype(F32)
            for r in range(CAP):
                ident = jnp.max(meta[r : r + 1, :]).astype(jnp.int32)
                idents[k * CAP + r] = ident
                scale = 1.0 / meta[8 + r : 9 + r, :]

                @pl.when(ident >= 0)
                def _():
                    at = pl.multiple_of(ident * slab, slab)
                    total[pl.ds(at, slab), :] += payloads[k, r * slab : (r + 1) * slab, :].astype(F32) * scale

        summed[...] = total[...].astype(BF16)

    proj, pieces = [], []
    for c in range(per_part):
        across = []
        for s in range(sq_cols):
            at = pl.multiple_of(((step * sq_cols + s) * per_part + c) * feature, feature)
            piece = summed[pl.ds(at, feature), :]
            across.append(dot_tn(piece, w_template[...]).reshape(GROUP, SQ, width))
            pieces.append(piece)
        proj.append(jnp.concatenate(across, axis=1).reshape(GROUP * cols, width))
    z_one = pair[...] + jnp.concatenate(proj, axis=0)
    mean = jnp.mean(z_one, axis=1, keepdims=True)
    centred = z_one - mean
    deviation = lax.rsqrt(jnp.mean(centred * centred, axis=1, keepdims=True) + 1e-5)
    standard = centred * deviation
    normed = (standard * gain[...] + bias[...]).astype(BF16)
    per_half = steps // 2
    pairs = block // LANES
    at = lax.rem(step, per_half) * (PARTS * pairs) + part * pairs
    to = lax.rem(step, per_half) * pairs
    straight = step // per_half == where_am[0]
    mirrored = []
    for p in range(pairs):
        crossed = arrived(where_am, got_b, got_c, at + p)
        mirrored.append(jnp.where(straight, got_a[at + p].astype(F32), crossed).T)
    d_low = (turned[...].astype(F32) + jnp.concatenate(mirrored, axis=0)).astype(BF16)
    dz_two = dot_nn(d_low, w_dist_t[...])
    dz_low = dz_two.astype(BF16)

    z_two = z_one
    d_norm = jnp.zeros_like(z_one)
    for h in range(0, hidden, PIECE):
        e = h + PIECE
        gate = dot_nn(normed, w_gate[:, h:e])
        upper = dot_nn(normed, w_up[:, h:e])
        d_hidden = dot_nn(dz_low, w_out_t[:, h:e])
        sigma = 0.5 * jnp.tanh(0.5 * gate) + 0.5
        swish = gate * sigma
        hid = (swish * upper).astype(BF16)
        d_gate = (d_hidden * upper * (sigma + swish * (1.0 - sigma))).astype(BF16)
        d_upper = (d_hidden * swish).astype(BF16)
        z_two = z_two + dot_nn(hid, w_out[h:e, :])
        d_norm = d_norm + dot_nn(d_gate, w_gate_t[h:e, :]) + dot_nn(d_upper, w_up_t[h:e, :])
        low_hid[:, h:e] = hid
        low_gu[:, h:e] = d_gate
        low_gu[:, hidden + h : hidden + e] = d_upper

    acc_gu[...] += dot_tn(normed, low_gu[...])
    acc_out[...] += dot_tn(dz_low, low_hid[...])
    z_low = z_two.astype(BF16)
    z_low_out[...] = z_low
    acc_td[feature:, :] += dot_tn(d_low, z_low)
    acc_gb[0:8, :] += fold_rows(d_norm * standard)
    acc_gb[8:16, :] += fold_rows(d_norm)
    d_standard = d_norm * gain[...]
    grad = dz_two + deviation * (
        d_standard
        - jnp.mean(d_standard, axis=1, keepdims=True)
        - standard * jnp.mean(d_standard * standard, axis=1, keepdims=True)
    )
    grad_pair[...] = grad

    heads = dot_nt(w_dist_t[...], z_low).astype(BF16)

    @pl.when(straight)
    def _():
        for p in range(pairs):
            heads_a[to + p] = heads[:, p * LANES : (p + 1) * LANES]

    @pl.when(jnp.logical_not(straight))
    def _():
        for p in range(pairs):
            heads_b[to + p] = heads[:, p * LANES : (p + 1) * LANES]

    d_proj = grad.astype(BF16).reshape(rows, cols, width)
    for s in range(sq_cols):
        cells = d_proj[:, s * SQ : (s + 1) * SQ, :].reshape(rows * SQ, width)
        tile_grad = dot_nt(w_template[...], cells).astype(BF16)
        for c in range(per_part):
            squares[step * sq_cols + s, c * feature : (c + 1) * feature, :] = tile_grad[:, c * LANES : (c + 1) * LANES]
        side = jnp.concatenate([pieces[c * sq_cols + s] for c in range(per_part)], axis=1)
        acc_td[0:feature, :] += dot_nn(side, cells)

    @pl.when(step == steps - 1)
    def _():
        def copy_of(k, r):
            return pltpu.make_async_copy(
                squares.at[jnp.maximum(idents[k * CAP + r], 0)],
                returns.at[k, pl.ds(r * slab, slab)],
                sems.at[k * CAP + r],
            )

        for k in range(devs):
            for r in range(CAP):
                copy_of(k, r).start()
        if last:
            share_out(where_am, sums, keep, send)
        for k in range(devs):
            for r in range(CAP):
                copy_of(k, r).wait()


def heads_kernel(*refs):
    z_low, (w_dist_t, out, wide) = refs[:PARTS], refs[PARTS:]
    cols, bins, rows = out.shape
    block = SQ // PARTS * cols
    for part in range(PARTS):
        for band in range(rows // SQ):
            at = (band * PARTS + part) * block
            wide[at : at + block, :] = z_low[part][band * block : (band + 1) * block, :].astype(F32)

    def one(j, unused):
        column = wide[pl.ds(j, rows, stride=cols), :].astype(BF16)
        out[j] = dot_nt(w_dist_t[...], column).astype(BF16)
        return unused

    lax.fori_loop(0, cols, one, 0, unroll=8)


def logits_kernel(where_am, heads, *refs):
    got, out = refs[:-1], refs[-1]
    straight = where_am[0] == 0
    low = low_lanes(heads.shape[1:])
    per = SQ // PARTS // 2
    for part in range(PARTS):
        got_a, got_b, got_c = got[3 * part : 3 * part + 3]

        def one(p, unused):
            a, b = got_a[p].astype(F32), arrived(where_am, got_b, got_c, p)
            front, back = jnp.where(straight, a, b), jnp.where(straight, b, a)
            even = jnp.where(low, front, pltpu.roll(back, LANES // 2, 1))
            odd = jnp.where(low, pltpu.roll(front, LANES // 2, 1), back)
            at = p // per * SQ + part * (SQ // PARTS) + 2 * lax.rem(p, per)
            out[at] = (heads[at].astype(F32) + even).astype(BF16)
            out[at + 1] = (heads[at + 1].astype(F32) + odd).astype(BF16)
            return unused

        lax.fori_loop(0, got_a.shape[0], one, 0, unroll=4)


def tiles_kernel(devs, target, count, *refs):
    returned, (out, source) = refs[:PARTS], refs[PARTS:]
    feature, cells = out.shape[1:]
    groups = cells // LANES
    per_part = groups // PARTS
    fill_slots(target, source, devs)
    for k in range(devs):
        for r in range(CAP):
            slot = source[k * CAP + r]

            @pl.when(slot >= 0)
            def _():
                scale = 1.0 / jnp.full((1, LANES), count[slot].astype(F32), F32)
                for c in range(groups):
                    at = (r * per_part + c % per_part) * feature
                    piece = returned[c // per_part][k, at : at + feature, :].astype(F32) * scale
                    out[slot, :, c * LANES : (c + 1) * LANES] = piece.astype(BF16)


def weights_kernel(scale, where_am, mine, other, *outs):
    g_template, g_gain, g_bias, g_gate, g_up, g_out, g_dist = outs
    width, hidden = g_gate.shape
    feature = g_template.shape[0]
    half = mine.shape[0] // width
    lead = where_am[1] == 0
    per = hidden // width

    def block(i):
        source = slice(i % half * width, (i % half + 1) * width)
        here, there = mine[source, :].astype(F32), other[source, :].astype(F32)
        return (jnp.where(lead, here, there) if i < half else jnp.where(lead, there, here)) * scale

    for c in range(per):
        at = slice(c * width, (c + 1) * width)
        g_gate[:, at] = block(c)
        g_up[:, at] = block(per + c)
        g_out[at, :] = block(2 * per + c).T
    both = block(3 * per)
    g_template[...] = both[:feature, :]
    g_dist[...] = both[feature:, :]
    last = block(3 * per + 1)
    g_gain[...] = jnp.sum(last[0:8, :], axis=0, keepdims=True)
    g_bias[...] = jnp.sum(last[8:16, :], axis=0, keepdims=True)


def axis_groups(axis, first, size):
    last = size.bit_length() - 1
    groups, bit = [], first
    while bit < last:
        wide = 1 if (last - bit) % 2 else 2
        groups.append((axis, bit, [m << bit for m in range(1, 1 << wide)]))
        bit += wide
    return groups


def swap(value, axis, mask):
    return lax.ppermute(value, axis, [(i, i ^ mask) for i in range(lax.axis_size(axis))])


def all_sum(value, settle):
    groups = axis_groups("row", 1, lax.axis_size("row")) + axis_groups("col", 0, lax.axis_size("col"))
    pairs = [(axis, bit) for axis, bit, masks in groups if len(masks) == 1]
    split = []
    for axis, bit in pairs:
        mine = (lax.axis_index(axis) >> bit) & 1
        both = value.reshape(2, value.shape[0] // 2, value.shape[1])
        away = lax.dynamic_index_in_dim(both, 1 - mine, 0, False).astype(BF16)
        value = lax.dynamic_index_in_dim(both, mine, 0, False) + swap(away, axis, 1 << bit).astype(F32)
        split.append(mine)
    value = settle[0](value)
    for axis, bit, masks in groups:
        if len(masks) == 1:
            continue
        low = value.astype(BF16)
        terms = [low.astype(F32)] + [swap(low, axis, m).astype(F32) for m in masks]
        while len(terms) > 1:
            terms = [terms[i] + terms[i + 1] for i in range(0, len(terms), 2)]
        value = terms[0]
    low = settle[1](value.astype(BF16))
    for (axis, bit), mine in reversed(list(zip(pairs, split))):
        other = swap(low, axis, 1 << bit)
        low = jnp.where(mine == 0, jnp.concatenate([low, other]), jnp.concatenate([other, low]))
    return low


def per_device(
    pair,
    logit_cotangent,
    tiles,
    tile_target,
    tile_square,
    tile_count,
    w_template,
    transition_norm_gain,
    transition_norm_bias,
    w_gate,
    w_up,
    w_out,
    w_dist,
):
    row_devs = lax.axis_size("row")
    col_devs = lax.axis_size("col")
    rows, cols, width = pair.shape
    bins = w_dist.shape[1]
    hidden = w_gate.shape[1]
    slots, cells_sq, feature = tiles.shape
    groups = cells_sq // LANES
    slab = groups * feature
    entries = rows * cols
    halves = rows // cols
    my_row, my_col = lax.axis_index("row"), lax.axis_index("col")
    two_chips = row_devs == 4
    crosses = (my_col // halves // 2 != my_row // 2) & two_chips
    where_am = jnp.stack([my_col % halves, my_row % 2, crosses.astype(jnp.int32)]).astype(jnp.int32)
    target = tile_target[:, 0]
    tiles_t = jnp.transpose(tiles, (0, 2, 1))
    cot_t = jnp.transpose(logit_cotangent, (1, 2, 0))
    w_dist_t = w_dist.T

    def mirror(first, second):
        everywhere = [(r, c) for r in range(row_devs) for c in range(col_devs)]

        def move(value, steps):
            perm = [(a * col_devs + b, c * col_devs + d) for (a, b), (c, d) in steps]
            return lax.ppermute(value, ("row", "col"), perm)

        def ends(s):
            return [((r, c), (c // halves, halves * r + ((c % halves) ^ s))) for r, c in everywhere]

        direct = move(first, ends(0))
        if not two_chips:
            other = move(second, ends(1))
            return [direct, other, other], lambda value: value
        across = [((r, c), (e // 2 * 2 + r % 2, c), (e, f)) for (r, c), (e, f) in ends(1) if r // 2 != e // 2]
        stay = move(second, [(a, b) for a, b in ends(1) if a[0] // 2 == b[0] // 2])
        over = move(second, [(a, b) for a, b, c in across])
        return [direct, stay, over], lambda value: move(value, [(b, c) for a, b, c in across])

    def stacked(shape, dtype=BF16):
        return jax.ShapeDtypeStruct(shape, dtype)

    part_slab = slab // PARTS
    packed = pl.pallas_call(
        functools.partial(pack_kernel, col_devs),
        out_shape=[stacked((col_devs, CAP * part_slab + META, LANES))] * PARTS + [stacked((cols // 2, bins, LANES))] * 2,
        in_specs=[SMEM] * 4 + [VMEM] * 2,
        out_specs=[VMEM] * (PARTS + 2),
        scratch_shapes=[pltpu.SMEM((col_devs * CAP,), jnp.int32)],
        compiler_params=params(),
        cost_estimate=cost(5),
        name="pack",
    )(where_am, target, tile_square, tile_count, tiles_t, cot_t)
    payloads = list(packed[:PARTS])
    payloads[0] = lax.all_to_all(payloads[0], "col", 0, 0, tiled=True)
    (*got_cot, over), land = mirror(*packed[PARTS:])
    got_cot.append(land(over))
    payloads[1], *got_cot = lax.optimization_barrier((payloads[1], *got_cot))
    payloads[1] = lax.all_to_all(payloads[1], "col", 0, 0, tiled=True)

    turned = pl.pallas_call(
        turn_kernel,
        out_shape=stacked((entries, bins)),
        in_specs=[VMEM],
        out_specs=VMEM,
        scratch_shapes=[pltpu.VMEM((entries, LANES), F32)],
        compiler_params=params(),
        cost_estimate=cost(5),
        name="turn",
    )(cot_t)

    block = SQ // PARTS * cols
    steps = rows // SQ
    squares = entries // cells_sq
    whole = lambda *shape: pl.BlockSpec(shape, lambda t: (0,) * len(shape))
    blocks = 3 * hidden // width + 2
    sum_shape = (blocks // 2 * width, width)
    operands = (
        w_template,
        transition_norm_gain[None, :],
        transition_norm_bias[None, :],
        w_gate,
        w_up,
        w_out,
        w_gate.T,
        w_up.T,
        w_out.T,
        w_dist_t,
    )
    sums_shapes = [(width, 2 * hidden), (width, hidden), (feature + bins, width), (16, width)]
    half_heads = (cols // 2, bins, LANES)
    part_heads = (cols // 2 // PARTS, bins, LANES)
    pair_cells = pair.reshape(entries, width)

    def transition(part, before):
        last = part == PARTS - 1
        per_step = lambda lanes: pl.BlockSpec((block, lanes), lambda t: (PARTS * t + part, 0))
        out_shape = [
            stacked((entries, width), F32),
            stacked((entries // PARTS, width)),
            stacked(part_heads),
            stacked(part_heads),
            stacked((col_devs, CAP * part_slab, LANES)),
        ]
        out_specs = [
            per_step(width),
            pl.BlockSpec((block, width), lambda t: (t, 0)),
            whole(*part_heads),
            whole(*part_heads),
            ANY,
        ]
        scratch = [
            pltpu.SMEM((col_devs * CAP,), jnp.int32),
            pltpu.VMEM((squares * part_slab, LANES), F32),
            pltpu.VMEM((squares * part_slab, LANES), BF16),
            pltpu.VMEM((squares, part_slab, LANES), BF16),
            pltpu.VMEM((block, 2 * hidden), BF16),
            pltpu.VMEM((block, hidden), BF16),
            pltpu.SemaphoreType.DMA((col_devs * CAP,)),
        ]
        if last:
            out_shape += [stacked(sum_shape, F32)] * 2
            out_specs += [whole(*sum_shape)] * 2
            scratch = [pltpu.VMEM(shape, F32) for shape in sums_shapes] + scratch
        else:
            out_shape += [stacked(shape, F32) for shape in sums_shapes]
            out_specs += [whole(*shape) for shape in sums_shapes]
        inputs = (where_am, payloads[part], pair_cells, turned, *got_cot, *operands)
        in_specs = [SMEM, whole(col_devs, CAP * part_slab + META, LANES), per_step(width), per_step(bins)]
        in_specs += [whole(*half_heads)] * 3
        in_specs += [whole(*operand.shape) for operand in operands]
        aliases = {}
        if part:
            aliases = {len(inputs): 0}
            inputs += tuple(before)
            in_specs += [ANY] + [whole(*shape) for shape in sums_shapes]
        return pl.pallas_call(
            functools.partial(main_kernel, col_devs, cols, part),
            grid=(steps,),
            out_shape=out_shape,
            in_specs=in_specs,
            out_specs=out_specs,
            scratch_shapes=scratch,
            input_output_aliases=aliases,
            compiler_params=params(),
            cost_estimate=cost(20),
            name=f"transition_{part}",
        )(*inputs)

    before, z_low, got_heads, returned = None, [], [], []
    for part in range(PARTS):
        outs = transition(part, before)
        grad_pair = outs[0]
        before = (grad_pair, *outs[5:])
        z_low.append(outs[1])
        if part == PARTS - 1:
            keep, send, returned[0], *got_heads[0] = lax.optimization_barrier((*outs[5:], *returned, *got_heads[0]))
            got_heads[0][2] = land(got_heads[0][2])
            sums = keep + swap(send, "row", 1)
        got, land = mirror(outs[2], outs[3])
        got_heads.append(got)
        returned.append(lax.all_to_all(outs[4], "col", 0, 0, tiled=True))

    heads = pl.pallas_call(
        heads_kernel,
        out_shape=stacked((cols, bins, rows)),
        in_specs=[VMEM] * (PARTS + 1),
        out_specs=VMEM,
        scratch_shapes=[pltpu.VMEM((entries, width), F32)],
        compiler_params=params(),
        cost_estimate=cost(5),
        name="own_heads",
    )(*z_low, w_dist_t)

    own = [heads]

    def heads_sent(value):
        got = lax.optimization_barrier((value, *got_heads[1], got_heads[0][2]))
        got_heads[0][2] = got[4]
        got_heads[1] = [got[1], got[2], land(got[3])]
        return got[0]

    def heads_landed(value):
        value, own[0], returned[1] = lax.optimization_barrier((value, own[0], returned[1]))
        return value

    sums = all_sum(sums, (heads_sent, heads_landed))
    other = swap(sums, "row", 1)
    logits = pl.pallas_call(
        logits_kernel,
        out_shape=jax.ShapeDtypeStruct((cols, bins, rows), BF16),
        in_specs=[SMEM] + [VMEM] * (1 + 3 * PARTS),
        out_specs=VMEM,
        compiler_params=params(),
        cost_estimate=cost(3),
        name="logits",
    )(where_am, own[0], *got_heads[0], *got_heads[1])
    grad_tiles = pl.pallas_call(
        functools.partial(tiles_kernel, col_devs),
        out_shape=jax.ShapeDtypeStruct((slots, feature, cells_sq), BF16),
        in_specs=[SMEM] * 2 + [VMEM] * PARTS,
        out_specs=VMEM,
        scratch_shapes=[pltpu.SMEM((col_devs * CAP,), jnp.int32)],
        compiler_params=params(),
        cost_estimate=cost(4),
        name="tile_gradients",
    )(target, tile_count, *returned)
    length = rows * row_devs
    weights = pl.pallas_call(
        functools.partial(weights_kernel, 1.0 / length),
        out_shape=[
            jax.ShapeDtypeStruct((feature, width), F32),
            jax.ShapeDtypeStruct((1, width), F32),
            jax.ShapeDtypeStruct((1, width), F32),
            jax.ShapeDtypeStruct((width, hidden), F32),
            jax.ShapeDtypeStruct((width, hidden), F32),
            jax.ShapeDtypeStruct((hidden, width), F32),
            jax.ShapeDtypeStruct((bins, width), F32),
        ],
        in_specs=[SMEM] + [VMEM] * 2,
        out_specs=[VMEM] * 7,
        compiler_params=params(),
        cost_estimate=cost(2),
        name="weight_gradients",
    )(where_am, sums, other)
    g_template, g_gain, g_bias, g_gate, g_up, g_out, g_dist = weights
    return (
        jnp.transpose(logits, (2, 0, 1)),
        grad_pair.reshape(rows, cols, width),
        jnp.transpose(grad_tiles, (0, 2, 1)),
        g_template,
        g_gain[0],
        g_bias[0],
        g_gate,
        g_up,
        g_out,
        g_dist.T,
    )


def solution(mesh):
    split = P("row", "col", None)
    held = P(("row", "col"), None, None)
    return jax.shard_map(
        per_device,
        mesh=mesh,
        in_specs=(split, split, held, P(("row", "col"), None), P(("row", "col")), P(("row", "col")))
        + (P(),) * 7,
        out_specs=(split, split, held) + (P(),) * 7,
        check_vma=False,
    )
```

time: 287 us -> 209 us (0.73)
  the two profiles are of different devices: /device:TPU:18 before, /device:TPU:25 now
where the time goes in v2:
time: 209 us; the launch traced here: 208 us
  waiting for transfers between devices  72.3 us (35%)
  starting transfers between devices  64.1 us (31%)
  Pallas kernels  64 us (31%)
  local copies, waits for them, and re-layouts  4.06 us (2%)
  other arithmetic  2.21 us (1%)
    ppermute x12, waiting for transfers between devices, move(): return lax.ppermute(value, ('row', 'col'), perm)  60.7 us
    pallas_call x2, Pallas kernels, transition(): pl.pallas_call(functools.partial(main_kernel, col_devs, cols, part), grid...  41 us
    ppermute x12, starting transfers between devices, move(): return lax.ppermute(value, ('row', 'col'), perm)  25.1 us
    all_to_all x2, starting transfers between devices, per_device(): returned.append(lax.all_to_all(outs[4], 'col', 0, 0, tiled=True))  17.8 us
    ppermute x9, starting transfers between devices, swap(): lax.ppermute(value, axis, [(i, i ^ mask) for i in range(lax.axis_size(axi...  9.27 us
    ppermute x9, waiting for transfers between devices, swap(): lax.ppermute(value, axis, [(i, i ^ mask) for i in range(lax.axis_size(axi...  8.7 us
    all_to_all x1, starting transfers between devices, per_device(): payloads[1] = lax.all_to_all(payloads[1], 'col', 0, 0, tiled=True)  6.32 us
    all_to_all x1, starting transfers between devices, per_device(): payloads[0] = lax.all_to_all(payloads[0], 'col', 0, 0, tiled=True)  5.64 us
  transfers between devices with their start and end apart: 25, of which 11 were waited for; matrix products, arithmetic and copies ran while one was open for 1% of the time, Pallas kernels for 28%

profile of v2, /device:TPU:25, one launch (start us, length us, event | category | flops | bytes accessed | tf_op | source)
XLA Modules:
  0.0 207.7 jit_solution(6878451167033086393)
XLA Ops:
  2.7 4.9 %pack.1 = (bf16[8,528,128]{2,1,0:T(8,128)(2,1)}, bf16[8,528,128]{2,1,0:T(8,128)(2,1)}, bf16[32,64,128]{2,1,0:T(8,128)(2,1)S(1)}, bf16[32,64,128]{2,1,0:T(8,128)(2,1)S(1)}) custom-call(s32[3]{0:T(128)S(1)} %pad_add_fusion.where_am.refs_0_, s32[16]{0:T(128)S(1)} %bitcast.44, s32[16]{0:T(128)S(1)} %copy-done.6, s32[16]{0:T(128)S(1)} %copy-done.11, ...), custom_call_target="tpu_custom_call" | custom-call | flops 5500000256 | tf_op jit(solution)/shard_map/pack/pallas_call | solution.py:462
  7.7 5.6 %all-to-all-start.1 = ((bf16[8,528,128]{2,1,0:T(8,128)(2,1)}), bf16[8,528,128]{2,1,0:T(8,128)(2,1)}, u32[]{:S(2)}, u32[]{:S(2)}) async-start(bf16[8,528,128]{2,1,0:T(8,128)(2,1)} %get-tuple-element.62), calls=%async_computation.1 | async-start | bytes 2162688 | tf_op jit(solution)/shard_map/all_to_all | solution.py:473
  13.3 3.9 %collective-permute-start.2 = (bf16[32,64,128]{2,1,0:T(8,128)(2,1)S(1)}, bf16[32,64,128]{2,1,0:T(8,128)(2,1)}, u32[]{:S(2)}, u32[]{:S(2)}) collective-permute-start(bf16[32,64,128]{2,1,0:T(8,128)(2,1)S(1)} %get-tuple-element.57), channel_id=1, source_target_pairs={{4,20},{5,21},{6,22},{7,23},{12,28},{13,29},{14,30},{15,31},{16,0}... | collective-permute-start | bytes 1572872 | tf_op jit(solution)/shard_map/ppermute | solution.py:444
  17.9 2.2 %collective-permute-start = (bf16[32,64,128]{2,1,0:T(8,128)(2,1)S(1)}, bf16[32,64,128]{2,1,0:T(8,128)(2,1)}, u32[]{:S(2)}, u32[]{:S(2)}) collective-permute-start(bf16[32,64,128]{2,1,0:T(8,128)(2,1)S(1)} %get-tuple-element.56), channel_id=1, source_target_pairs={{0,0},{1,1},{2,8},{3,9},{4,16},{5,17},{6,24},{7,25},{8,2},{9,3},{1... | collective-permute-start | bytes 1572872 | tf_op jit(solution)/shard_map/ppermute | solution.py:444
  20.0 6.3 %collective-permute-done.2 = bf16[32,64,128]{2,1,0:T(8,128)(2,1)} collective-permute-done((bf16[32,64,128]{2,1,0:T(8,128)(2,1)S(1)}, bf16[32,64,128]{2,1,0:T(8,128)(2,1)}, u32[]{:S(2)}, u32[]{:S(2)}) %collective-permute-start.2) | collective-permute-done | bytes 524320 | tf_op jit(solution)/shard_map/ppermute | solution.py:444
  26.4 1.3 collective-permute-start.3
  28.1 4.9 %turn.1.refs_3_ = bf16[8192,64]{1,0:T(8,128)(2,1)} custom-call(bf16[64,64,128]{2,1,0:T(8,128)(2,1)S(1)} %bitcast.36), custom_call_target="tpu_custom_call" | custom-call | flops 5500000256 | tf_op jit(solution)/shard_map/turn/pallas_call | solution.py:479
  33.0 28.1 %collective-permute-done.refs_4_ = bf16[32,64,128]{2,1,0:T(8,128)(2,1)} collective-permute-done((bf16[32,64,128]{2,1,0:T(8,128)(2,1)S(1)}, bf16[32,64,128]{2,1,0:T(8,128)(2,1)}, u32[]{:S(2)}, u32[]{:S(2)}) %collective-permute-start) | collective-permute-done | bytes 524320 | tf_op jit(solution)/shard_map/ppermute | solution.py:444
  61.3 6.3 %all-to-all-start = ((bf16[8,528,128]{2,1,0:T(8,128)(2,1)}), bf16[8,528,128]{2,1,0:T(8,128)(2,1)}, u32[]{:S(2)}, u32[]{:S(2)}) async-start(bf16[8,528,128]{2,1,0:T(8,128)(2,1)} %get-tuple-element.58), calls=%async_computation | async-start | bytes 2162688 | tf_op jit(solution)/shard_map/all_to_all | solution.py:477
  67.6 20.3 %transition_0.1 = (f32[8192,128]{1,0:T(8,128)}, bf16[4096,128]{1,0:T(8,128)(2,1)}, bf16[16,64,128]{2,1,0:T(8,128)(2,1)S(1)}, bf16[16,64,128]{2,1,0:T(8,128)(2,1)...) custom-call(s32[3]{0:T(128)S(1)} %pad_add_fusion.where_am.refs_0_, ...), custom_call_target="tpu_custom_call" | custom-call | flops 22000001024 | tf_op jit(solution)/shard_map/transition_0/pallas_call | solution.py:555
  89.3 2.7 %collective-permute-start.6 = (bf16[16,64,128]{2,1,0:T(8,128)(2,1)S(1)}, bf16[16,64,128]{2,1,0:T(8,128)(2,1)}, u32[]{:S(2)}, u32[]{:S(2)}) collective-permute-start(bf16[16,64,128]{2,1,0:T(8,128)(2,1)S(1)} %get-tuple-element.72), channel_id=1, source_target_pairs={{4,20},{5,21},{6,22},{7,23},{12,28},{13,29},{14,30},{15,31},{16,0}... | collective-permute-start | bytes 786440 | tf_op jit(solution)/shard_map/ppermute | solution.py:444
  92.1 5.7 %collective-permute-start.4 = (bf16[16,64,128]{2,1,0:T(8,128)(2,1)S(1)}, bf16[16,64,128]{2,1,0:T(8,128)(2,1)S(1)}, u32[]{:S(2)}, u32[]{:S(2)}) collective-permute-start(bf16[16,64,128]{2,1,0:T(8,128)(2,1)S(1)} %get-tuple-element.71), channel_id=1, source_target_pairs={{0,0},{1,1},{2,8},{3,9},{4,16},{5,17},{6,24},{7,25},{8,2},{9,3},{1... | collective-permute-start | bytes 786440 | tf_op jit(solution)/shard_map/ppermute | solution.py:444
  97.8 5.2 %all-to-all-start.2 = ((bf16[8,512,128]{2,1,0:T(8,128)(2,1)}), bf16[8,512,128]{2,1,0:T(8,128)(2,1)S(1)}, u32[]{:S(2)}, u32[]{:S(2)}) async-start(bf16[8,512,128]{2,1,0:T(8,128)(2,1)} %get-tuple-element.70), calls=%async_computation.2 | async-start | bytes 2097152 | tf_op jit(solution)/shard_map/all_to_all | solution.py:580
  103.9 20.7 %transition_1.1 = (f32[8192,128]{1,0:T(8,128)}, bf16[4096,128]{1,0:T(8,128)(2,1)}, bf16[16,64,128]{2,1,0:T(8,128)(2,1)S(1)}, bf16[16,64,128]{2,1,0:T(8,128)(2,1)...) custom-call(s32[3]{0:T(128)S(1)} %pad_add_fusion.where_am.refs_0_, ...), custom_call_target="tpu_custom_call", output_to_operand_aliasing={{0}: (17, {})} | custom-call | flops 22000001024 | tf_op jit(solution)/shard_map/transition_1/pallas_call | solution.py:555
  124.6 2.8 %all-to-all-done.2.refs_0_ = bf16[8,512,128]{2,1,0:T(8,128)(2,1)S(1)} async-done(((bf16[8,512,128]{2,1,0:T(8,128)(2,1)}), bf16[8,512,128]{2,1,0:T(8,128)(2,1)S(1)}, u32[]{:S(2)}, u32[]{:S(2)}) %all-to-all-start.2) | async-done | bytes 1048608 | tf_op jit(solution)/shard_map/all_to_all | solution.py:580
  127.9 12.6 %all-to-all-start.3 = ((bf16[8,512,128]{2,1,0:T(8,128)(2,1)}), bf16[8,512,128]{2,1,0:T(8,128)(2,1)}, u32[]{:S(2)}, u32[]{:S(2)}) async-start(bf16[8,512,128]{2,1,0:T(8,128)(2,1)} %get-tuple-element.81), calls=%async_computation.3 | async-start | bytes 2097152 | tf_op jit(solution)/shard_map/all_to_all | solution.py:580
  141.7 4.4 %collective-permute-done.8 = bf16[448,128]{1,0:T(8,128)(2,1)S(1)} collective-permute-done((bf16[448,128]{1,0:T(8,128)(2,1)S(1)}, bf16[448,128]{1,0:T(8,128)(2,1)S(1)}, u32[]{:S(2)}, u32[]{:S(2)}) %collective-permute-start.8) | collective-permute-done | bytes 114720 | tf_op jit(solution)/shard_map/ppermute | solution.py:376
  146.1 1.3 collective-permute-start.9
  147.4 2.2 %collective-permute-start.10 = (bf16[16,64,128]{2,1,0:T(8,128)(2,1)S(1)}, bf16[16,64,128]{2,1,0:T(8,128)(2,1)S(1)}, u32[]{:S(2)}, u32[]{:S(2)}) collective-permute-start(bf16[16,64,128]{2,1,0:T(8,128)(2,1)S(1)} %get-tuple-element.75), channel_id=1, source_target_pairs={{0,0},{1,1},{2,8},{3,9},{4,16},{5,17},{6,24},{7,25},{8,2},{9,3},{1... | collective-permute-start | bytes 786440 | tf_op jit(solution)/shard_map/ppermute | solution.py:444
  150.3 2.5 %collective-permute-start.12 = (bf16[16,64,128]{2,1,0:T(8,128)(2,1)S(1)}, bf16[16,64,128]{2,1,0:T(8,128)(2,1)S(1)}, u32[]{:S(2)}, u32[]{:S(2)}) collective-permute-start(bf16[16,64,128]{2,1,0:T(8,128)(2,1)S(1)} %get-tuple-element.76), channel_id=1, source_target_pairs={{4,20},{5,21},{6,22},{7,23},{12,28},{13,29},{14,30},{15,31},{16,0}... | collective-permute-start | bytes 786440 | tf_op jit(solution)/shard_map/ppermute | solution.py:444
  152.8 1.3 collective-permute-start.13
  154.1 3.5 %collective-permute-done.9 = bf16[224,128]{1,0:T(8,128)(2,1)S(1)} collective-permute-done((bf16[224,128]{1,0:T(8,128)(2,1)S(1)}, bf16[224,128]{1,0:T(8,128)(2,1)S(1)}, u32[]{:S(2)}, u32[]{:S(2)}) %collective-permute-start.9) | collective-permute-done | bytes 57376 | tf_op jit(solution)/shard_map/ppermute | solution.py:376
  158.6 16.7 %collective-permute-done.10.refs_3_ = bf16[16,64,128]{2,1,0:T(8,128)(2,1)S(1)} collective-permute-done((bf16[16,64,128]{2,1,0:T(8,128)(2,1)S(1)}, bf16[16,64,128]{2,1,0:T(8,128)(2,1)S(1)}, u32[]{:S(2)}, u32[]{:S(2)}) %collective-permute-start.10) | collective-permute-done | bytes 262176 | tf_op jit(solution)/shard_map/ppermute | solution.py:444
  175.2 1.3 collective-permute-done.13.refs_2_
  176.9 3.2 %collective-permute-start.16 = (bf16[224,128]{1,0:T(8,128)(2,1)S(1)}, bf16[224,128]{1,0:T(8,128)(2,1)S(1)}, u32[]{:S(2)}, u32[]{:S(2)}) collective-permute-start(bf16[224,128]{1,0:T(8,128)(2,1)S(1)} %bitcast_add_fusion.1), channel_id=1, source_target_pairs={{0,6},{1,7},{2,4},{3,5},{4,2},{5,3},{6,0},{7,1},{8,14},{9,15},{10,... | collective-permute-start | bytes 172040 | tf_op jit(solution)/shard_map/ppermute | solution.py:376
  180.1 5.1 %own_heads.1.heads = bf16[64,64,128]{2,1,0:T(8,128)(2,1)S(1)} custom-call(bf16[4096,128]{1,0:T(8,128)(2,1)} %get-tuple-element.79.refs_0_, bf16[4096,128]{1,0:T(8,128)(2,1)} %get-tuple-element.80.refs_1_, bf16[64,128]{1,0:T(8,128)(2,1)S(1)} %bitcast.39), custom_call_target="tpu_custom_call" | custom-call | flops 5500000256 | tf_op jit(solution)/shard_map/own_heads/pallas_call | solution.py:582
  186.4 1.3 collective-permute-start.17
  188.5 3.5 %tile_gradients.1 = bf16[16,64,1024]{2,1,0:T(8,128)(2,1)} custom-call(s32[16]{0:T(128)S(1)} %bitcast.45, s32[16]{0:T(128)S(1)} %copy-done.12, bf16[8,512,128]{2,1,0:T(8,128)(2,1)S(1)} %all-to-all-done.2.refs_0_, bf16[8,512,128]{2,1,0:T(8,128)(2,1)} %all-to-all-done.3.refs_1_), custom_call_target="tpu_custom_call" | custom-call | flops 4400000000 | tf_op jit(solution)/shard_map/tile_gradients/pallas_call | solution.py:616
  192.2 2.7 %collective-permute-start.20 = (bf16[896,128]{1,0:T(8,128)(2,1)S(1)}, bf16[896,128]{1,0:T(8,128)(2,1)S(1)}, u32[]{:S(2)}, u32[]{:S(2)}) collective-permute-start(bf16[896,128]{1,0:T(8,128)(2,1)S(1)} %maximum_select_fusion.mine), channel_id=1, source_target_pairs={{0,8},{8,0},{16,24},{24,16},{1,9},{9,1},{17,25},{25,17},{2,10},{10... | collective-permute-start | bytes 688136 | tf_op jit(solution)/shard_map/ppermute | solution.py:376
  194.9 8.1 %collective-permute-done.17.refs_5_ = bf16[16,64,128]{2,1,0:T(8,128)(2,1)S(1)} collective-permute-done((bf16[16,64,128]{2,1,0:T(8,128)(2,1)}, bf16[16,64,128]{2,1,0:T(8,128)(2,1)S(1)}, u32[]{:S(2)}, u32[]{:S(2)}) %collective-permute-start.17) | collective-permute-done | bytes 262176 | tf_op jit(solution)/shard_map/ppermute | solution.py:444
  203.0 3.1 %logits.1 = bf16[64,64,128]{2,1,0:T(8,128)(2,1)} custom-call(s32[3]{0:T(128)S(1)} %pad_add_fusion.where_am.refs_0_, bf16[64,64,128]{2,1,0:T(8,128)(2,1)} %copy-done.13, bf16[16,64,128]{2,1,0:T(8,128)(2,1)S(1)} %collective-permute-done.4.refs_0_, bf16[16,64,128]{2,1,0:T(8,128)(2,1)S(1)} %collective-permute-done.5.refs_1_, ...), custom_call_target="tpu_custom_call" | custom-call | flops 3300000000 | tf_op jit(solution)/shard_map/logits/pallas_call | solution.py:607
  206.2 1.5 weight_gradients.1
  (78 shorter events, 11.4 us)
Async XLA Ops:
  7.6 20.2 %copy-start.2 = (bf16[512,128]{1,0:T(8,128)(2,1)S(1)}, bf16[512,128]{1,0:T(8,128)(2,1)}, u32[]{:S(2)}) copy-start(bf16[512,128]{1,0:T(8,128)(2,1)} %refs_12_.3) | copy-start | bytes 393220
  7.6 20.3 %copy-start = (bf16[128,512]{1,0:T(8,128)(2,1)S(1)}, bf16[128,512]{1,0:T(8,128)(2,1)}, u32[]{:S(2)}) copy-start(bf16[128,512]{1,0:T(8,128)(2,1)} %refs_10_.3) | copy-start | bytes 393220
  7.6 20.4 %copy-start.3 = (bf16[128,64,64]{0,2,1:T(8,128)(2,1)S(1)}, bf16[128,64,64]{0,2,1:T(8,128)(2,1)}, u32[]{:S(2)}) copy-start(bf16[128,64,64]{0,2,1:T(8,128)(2,1)} %param.14) | copy-start | bytes 3145732
  7.7 53.6 %all-to-all-start.1 = ((bf16[8,528,128]{2,1,0:T(8,128)(2,1)}), bf16[8,528,128]{2,1,0:T(8,128)(2,1)}, u32[]{:S(2)}, u32[]{:S(2)}) async-start(bf16[8,528,128]{2,1,0:T(8,128)(2,1)} %get-tuple-element.62), calls=%async_computation.1 | async-start | bytes 2162688 | tf_op jit(solution)/shard_map/all_to_all | solution.py:473
  13.3 13.1 %collective-permute-start.2 = (bf16[32,64,128]{2,1,0:T(8,128)(2,1)S(1)}, bf16[32,64,128]{2,1,0:T(8,128)(2,1)}, u32[]{:S(2)}, u32[]{:S(2)}) collective-permute-start(bf16[32,64,128]{2,1,0:T(8,128)(2,1)S(1)} %get-tuple-element.57), channel_id=1, source_target_pairs={{4,20},{5,21},{6,22},{7,23},{12,28},{13,29},{14,30},{15,31},{16,0}... | collective-permute-start | bytes 1572872 | tf_op jit(solution)/shard_map/ppermute | solution.py:444
  17.2 43.9 %collective-permute-start.1 = (bf16[32,64,128]{2,1,0:T(8,128)(2,1)S(1)}, bf16[32,64,128]{2,1,0:T(8,128)(2,1)S(1)}, u32[]{:S(2)}, u32[]{:S(2)}) collective-permute-start(bf16[32,64,128]{2,1,0:T(8,128)(2,1)S(1)} %get-tuple-element.57), channel_id=1, source_target_pairs={{0,1},{1,0},{2,9},{3,8},{8,3},{9,2},{10,11},{11,10},{20,21},{21,20... | collective-permute-start | bytes 1572872 | tf_op jit(solution)/shard_map/ppermute | solution.py:444
  17.9 43.2 %collective-permute-start = (bf16[32,64,128]{2,1,0:T(8,128)(2,1)S(1)}, bf16[32,64,128]{2,1,0:T(8,128)(2,1)}, u32[]{:S(2)}, u32[]{:S(2)}) collective-permute-start(bf16[32,64,128]{2,1,0:T(8,128)(2,1)S(1)} %get-tuple-element.56), channel_id=1, source_target_pairs={{0,0},{1,1},{2,8},{3,9},{4,16},{5,17},{6,24},{7,25},{8,2},{9,3},{1... | collective-permute-start | bytes 1572872 | tf_op jit(solution)/shard_map/ppermute | solution.py:444
  26.4 34.9 %collective-permute-start.3 = (bf16[32,64,128]{2,1,0:T(8,128)(2,1)}, bf16[32,64,128]{2,1,0:T(8,128)(2,1)}, u32[]{:S(2)}, u32[]{:S(2)}) collective-permute-start(bf16[32,64,128]{2,1,0:T(8,128)(2,1)} %collective-permute-done.2), channel_id=1, source_target_pairs={{20,17},{21,16},{22,25},{23,24},{28,19},{29,18},{30,27},{31,26},{0... | collective-permute-start | bytes 1572872 | tf_op jit(solution)/shard_map/ppermute | solution.py:444
  33.0 34.6 %copy-start.4 = (bf16[64,128]{1,0:T(8,128)(2,1)S(1)}, bf16[64,128]{1,0:T(8,128)(2,1)}, u32[]{:S(2)}) copy-start(bf16[64,128]{1,0:T(8,128)(2,1)} %refs_7_.3) | copy-start | bytes 49156
  33.0 34.6 %copy-start.5 = (bf16[128,64]{0,1:T(8,128)(2,1)S(1)}, bf16[128,64]{0,1:T(8,128)(2,1)}, u32[]{:S(2)}) copy-start(bf16[128,64]{0,1:T(8,128)(2,1)} %param.25) | copy-start | bytes 49156
  33.0 34.6 %copy-start.7 = (f32[128]{0:T(128)S(1)}, f32[128]{0:T(128)}, u32[]{:S(2)}) copy-start(f32[128]{0:T(128)} %param.20) | copy-start | bytes 1540
  33.0 34.7 %copy-start.8 = (f32[128]{0:T(128)S(1)}, f32[128]{0:T(128)}, u32[]{:S(2)}) copy-start(f32[128]{0:T(128)} %param.21) | copy-start | bytes 1540
  61.3 36.5 %all-to-all-start = ((bf16[8,528,128]{2,1,0:T(8,128)(2,1)}), bf16[8,528,128]{2,1,0:T(8,128)(2,1)}, u32[]{:S(2)}, u32[]{:S(2)}) async-start(bf16[8,528,128]{2,1,0:T(8,128)(2,1)} %get-tuple-element.58), calls=%async_computation | async-start | bytes 2162688 | tf_op jit(solution)/shard_map/all_to_all | solution.py:477
  88.7 36.0 %collective-permute-start.5 = (bf16[16,64,128]{2,1,0:T(8,128)(2,1)S(1)}, bf16[16,64,128]{2,1,0:T(8,128)(2,1)S(1)}, u32[]{:S(2)}, u32[]{:S(2)}) collective-permute-start(bf16[16,64,128]{2,1,0:T(8,128)(2,1)S(1)} %get-tuple-element.72), channel_id=1, source_target_pairs={{0,1},{1,0},{2,9},{3,8},{8,3},{9,2},{10,11},{11,10},{20,21},{21,20... | collective-permute-start | bytes 786440 | tf_op jit(solution)/shard_map/ppermute | solution.py:444
  89.3 35.3 %collective-permute-start.6 = (bf16[16,64,128]{2,1,0:T(8,128)(2,1)S(1)}, bf16[16,64,128]{2,1,0:T(8,128)(2,1)}, u32[]{:S(2)}, u32[]{:S(2)}) collective-permute-start(bf16[16,64,128]{2,1,0:T(8,128)(2,1)S(1)} %get-tuple-element.72), channel_id=1, source_target_pairs={{4,20},{5,21},{6,22},{7,23},{12,28},{13,29},{14,30},{15,31},{16,0}... | collective-permute-start | bytes 786440 | tf_op jit(solution)/shard_map/ppermute | solution.py:444
  92.1 32.6 %collective-permute-start.4 = (bf16[16,64,128]{2,1,0:T(8,128)(2,1)S(1)}, bf16[16,64,128]{2,1,0:T(8,128)(2,1)S(1)}, u32[]{:S(2)}, u32[]{:S(2)}) collective-permute-start(bf16[16,64,128]{2,1,0:T(8,128)(2,1)S(1)} %get-tuple-element.71), channel_id=1, source_target_pairs={{0,0},{1,1},{2,8},{3,9},{4,16},{5,17},{6,24},{7,25},{8,2},{9,3},{1... | collective-permute-start | bytes 786440 | tf_op jit(solution)/shard_map/ppermute | solution.py:444
  97.8 29.7 %all-to-all-start.2 = ((bf16[8,512,128]{2,1,0:T(8,128)(2,1)}), bf16[8,512,128]{2,1,0:T(8,128)(2,1)S(1)}, u32[]{:S(2)}, u32[]{:S(2)}) async-start(bf16[8,512,128]{2,1,0:T(8,128)(2,1)} %get-tuple-element.70), calls=%async_computation.2 | async-start | bytes 2097152 | tf_op jit(solution)/shard_map/all_to_all | solution.py:580
  127.4 13.1 %collective-permute-start.7 = (f32[896,128]{1,0:T(8,128)}, f32[896,128]{1,0:T(8,128)}, u32[]{:S(2)}, u32[]{:S(2)}) collective-permute-start(f32[896,128]{1,0:T(8,128)} %get-tuple-element.74), channel_id=1, source_target_pairs={{0,8},{8,0},{16,24},{24,16},{1,9},{9,1},{17,25},{25,17},{2,10},{10... | collective-permute-start | bytes 1376264 | tf_op jit(solution)/shard_map/ppermute | solution.py:376
  127.9 57.3 %all-to-all-start.3 = ((bf16[8,512,128]{2,1,0:T(8,128)(2,1)}), bf16[8,512,128]{2,1,0:T(8,128)(2,1)}, u32[]{:S(2)}, u32[]{:S(2)}) async-start(bf16[8,512,128]{2,1,0:T(8,128)(2,1)} %get-tuple-element.81), calls=%async_computation.3 | async-start | bytes 2097152 | tf_op jit(solution)/shard_map/all_to_all | solution.py:580
  141.6 4.5 %collective-permute-start.8 = (bf16[448,128]{1,0:T(8,128)(2,1)S(1)}, bf16[448,128]{1,0:T(8,128)(2,1)S(1)}, u32[]{:S(2)}, u32[]{:S(2)}) collective-permute-start(bf16[448,128]{1,0:T(8,128)(2,1)S(1)} %fusion), channel_id=1, source_target_pairs={{0,16},{8,24},{16,0},{24,8},{1,17},{9,25},{17,1},{25,9},{2,18},{10... | collective-permute-start | bytes 344072 | tf_op jit(solution)/shard_map/ppermute | solution.py:376
  146.1 11.5 %collective-permute-start.9 = (bf16[224,128]{1,0:T(8,128)(2,1)S(1)}, bf16[224,128]{1,0:T(8,128)(2,1)S(1)}, u32[]{:S(2)}, u32[]{:S(2)}) collective-permute-start(bf16[224,128]{1,0:T(8,128)(2,1)S(1)} %fusion.1), channel_id=1, source_target_pairs={{0,1},{1,0},{2,3},{3,2},{4,5},{5,4},{6,7},{7,6},{8,9},{9,8},{10,11... | collective-permute-start | bytes 172040 | tf_op jit(solution)/shard_map/ppermute | solution.py:376
  147.4 27.8 %collective-permute-start.10 = (bf16[16,64,128]{2,1,0:T(8,128)(2,1)S(1)}, bf16[16,64,128]{2,1,0:T(8,128)(2,1)S(1)}, u32[]{:S(2)}, u32[]{:S(2)}) collective-permute-start(bf16[16,64,128]{2,1,0:T(8,128)(2,1)S(1)} %get-tuple-element.75), channel_id=1, source_target_pairs={{0,0},{1,1},{2,8},{3,9},{4,16},{5,17},{6,24},{7,25},{8,2},{9,3},{1... | collective-permute-start | bytes 786440 | tf_op jit(solution)/shard_map/ppermute | solution.py:444
  149.6 25.6 %collective-permute-start.11 = (bf16[16,64,128]{2,1,0:T(8,128)(2,1)S(1)}, bf16[16,64,128]{2,1,0:T(8,128)(2,1)S(1)}, u32[]{:S(2)}, u32[]{:S(2)}) collective-permute-start(bf16[16,64,128]{2,1,0:T(8,128)(2,1)S(1)} %get-tuple-element.76), channel_id=1, source_target_pairs={{0,1},{1,0},{2,9},{3,8},{8,3},{9,2},{10,11},{11,10},{20,21},{21,20... | collective-permute-start | bytes 786440 | tf_op jit(solution)/shard_map/ppermute | solution.py:444
  150.3 24.9 %collective-permute-start.12 = (bf16[16,64,128]{2,1,0:T(8,128)(2,1)S(1)}, bf16[16,64,128]{2,1,0:T(8,128)(2,1)S(1)}, u32[]{:S(2)}, u32[]{:S(2)}) collective-permute-start(bf16[16,64,128]{2,1,0:T(8,128)(2,1)S(1)} %get-tuple-element.76), channel_id=1, source_target_pairs={{4,20},{5,21},{6,22},{7,23},{12,28},{13,29},{14,30},{15,31},{16,0}... | collective-permute-start | bytes 786440 | tf_op jit(solution)/shard_map/ppermute | solution.py:444
  152.8 23.7 %collective-permute-start.13 = (bf16[16,64,128]{2,1,0:T(8,128)(2,1)}, bf16[16,64,128]{2,1,0:T(8,128)(2,1)S(1)}, u32[]{:S(2)}, u32[]{:S(2)}) collective-permute-start(bf16[16,64,128]{2,1,0:T(8,128)(2,1)} %collective-permute-done.6), channel_id=1, source_target_pairs={{20,17},{21,16},{22,25},{23,24},{28,19},{29,18},{30,27},{31,26},{0... | collective-permute-start | bytes 786440 | tf_op jit(solution)/shard_map/ppermute | solution.py:444
  176.5 8.6 %collective-permute-start.14 = (bf16[224,128]{1,0:T(8,128)(2,1)S(1)}, bf16[224,128]{1,0:T(8,128)(2,1)S(1)}, u32[]{:S(2)}, u32[]{:S(2)}) collective-permute-start(bf16[224,128]{1,0:T(8,128)(2,1)S(1)} %bitcast_add_fusion.1), channel_id=1, source_target_pairs={{0,2},{1,3},{2,0},{3,1},{4,6},{5,7},{6,4},{7,5},{8,10},{9,11},{10,... | collective-permute-start | bytes 172040 | tf_op jit(solution)/shard_map/ppermute | solution.py:376
  176.9 8.3 %collective-permute-start.15 = (bf16[224,128]{1,0:T(8,128)(2,1)S(1)}, bf16[224,128]{1,0:T(8,128)(2,1)S(1)}, u32[]{:S(2)}, u32[]{:S(2)}) collective-permute-start(bf16[224,128]{1,0:T(8,128)(2,1)S(1)} %bitcast_add_fusion.1), channel_id=1, source_target_pairs={{0,4},{1,5},{2,6},{3,7},{4,0},{5,1},{6,2},{7,3},{8,12},{9,13},{10,... | collective-permute-start | bytes 172040 | tf_op jit(solution)/shard_map/ppermute | solution.py:376
  176.9 8.3 %collective-permute-start.16 = (bf16[224,128]{1,0:T(8,128)(2,1)S(1)}, bf16[224,128]{1,0:T(8,128)(2,1)S(1)}, u32[]{:S(2)}, u32[]{:S(2)}) collective-permute-start(bf16[224,128]{1,0:T(8,128)(2,1)S(1)} %bitcast_add_fusion.1), channel_id=1, source_target_pairs={{0,6},{1,7},{2,4},{3,5},{4,2},{5,3},{6,0},{7,1},{8,14},{9,15},{10,... | collective-permute-start | bytes 172040 | tf_op jit(solution)/shard_map/ppermute | solution.py:376
  185.3 3.1 %collective-permute-start.18 = (bf16[224,128]{1,0:T(8,128)(2,1)S(1)}, bf16[224,128]{1,0:T(8,128)(2,1)S(1)}, u32[]{:S(2)}, u32[]{:S(2)}) collective-permute-start(bf16[224,128]{1,0:T(8,128)(2,1)S(1)} %add_convert_fusion), channel_id=1, source_target_pairs={{0,1},{1,0},{2,3},{3,2},{4,5},{5,4},{6,7},{7,6},{8,9},{9,8},{10,11... | collective-permute-start | bytes 172040 | tf_op jit(solution)/shard_map/ppermute | solution.py:376
  186.4 16.6 %collective-permute-start.17 = (bf16[16,64,128]{2,1,0:T(8,128)(2,1)}, bf16[16,64,128]{2,1,0:T(8,128)(2,1)S(1)}, u32[]{:S(2)}, u32[]{:S(2)}) collective-permute-start(bf16[16,64,128]{2,1,0:T(8,128)(2,1)} %copy-done.19), channel_id=1, source_target_pairs={{20,17},{21,16},{22,25},{23,24},{28,19},{29,18},{30,27},{31,26},{0... | collective-permute-start | bytes 786440 | tf_op jit(solution)/shard_map/ppermute | solution.py:444
  188.4 3.7 %collective-permute-start.19 = (bf16[448,128]{1,0:T(8,128)(2,1)S(1)}, bf16[448,128]{1,0:T(8,128)(2,1)S(1)}, u32[]{:S(2)}, u32[]{:S(2)}) collective-permute-start(bf16[448,128]{1,0:T(8,128)(2,1)S(1)} %maximum_select_fusion.1), channel_id=1, source_target_pairs={{0,16},{8,24},{16,0},{24,8},{1,17},{9,25},{17,1},{25,9},{2,18},{10... | collective-permute-start | bytes 344072 | tf_op jit(solution)/shard_map/ppermute | solution.py:376
  192.2 14.0 %collective-permute-start.20 = (bf16[896,128]{1,0:T(8,128)(2,1)S(1)}, bf16[896,128]{1,0:T(8,128)(2,1)S(1)}, u32[]{:S(2)}, u32[]{:S(2)}) collective-permute-start(bf16[896,128]{1,0:T(8,128)(2,1)S(1)} %maximum_select_fusion.mine), channel_id=1, source_target_pairs={{0,8},{8,0},{16,24},{24,16},{1,9},{9,1},{17,25},{25,17},{2,10},{10... | collective-permute-start | bytes 688136 | tf_op jit(solution)/shard_map/ppermute | solution.py:376
  (13 other events, 75.8 us)

commit v3 on v2

--- a/solution.py
+++ b/solution.py
@@ -62,24 +62,17 @@
     return lax.broadcasted_iota(jnp.int32, shape, 1) < LANES // 2
 
 
-def pack_kernel(devs, where_am, target, square, count, tiles, cot, *refs):
-    payloads, (cot_a, cot_b, source) = refs[:PARTS], refs[PARTS:]
+def pack_kernel(devs, target, square, count, tiles, payload, source, *scratch):
+    *scalars, sems = scratch
+    copies = [pltpu.make_async_copy(a, b, sems.at[i]) for i, (a, b) in enumerate(zip((target, square, count), scalars))]
+    for copy in copies:
+        copy.start()
+    for copy in copies:
+        copy.wait()
+    target, square, count = scalars
     feature, cells = tiles.shape[1:]
     groups = cells // LANES
-    per_part = groups // PARTS
     fill_slots(target, source, devs)
-    first = where_am[0] == 0
-    low = low_lanes(cot.shape[1:])
-
-    def pack_pair(p, unused):
-        even, odd = cot[2 * p].astype(F32), cot[2 * p + 1].astype(F32)
-        front = jnp.where(low, even, pltpu.roll(odd, LANES // 2, 1)).astype(BF16)
-        back = jnp.where(low, pltpu.roll(even, LANES // 2, 1), odd).astype(BF16)
-        cot_a[p] = jnp.where(first, front, back)
-        cot_b[p] = jnp.where(first, back, front)
-        return unused
-
-    lax.fori_loop(0, cot.shape[0] // 2, pack_pair, 0, unroll=4)
     line = lax.broadcasted_iota(jnp.int32, (META, LANES), 0)
     for k in range(devs):
         meta = jnp.zeros((META, LANES), F32)
@@ -90,10 +83,24 @@
             meta = jnp.where(line == r, ident, meta)
             meta = jnp.where(line == 8 + r, count[held].astype(F32), meta)
             for c in range(groups):
-                at = (r * per_part + c % per_part) * feature
-                payloads[c // per_part][k, at : at + feature, :] = tiles[held, :, c * LANES : (c + 1) * LANES]
-        for payload in payloads:
-            payload[k, CAP * per_part * feature :, :] = meta.astype(BF16)
+                at = (r * groups + c) * feature
+                payload[k, at : at + feature, :] = tiles[held, :, c * LANES : (c + 1) * LANES]
+        payload[k, CAP * groups * feature :, :] = meta.astype(BF16)
+
+
+def pack_cotangent_kernel(where_am, cot, cot_a, cot_b):
+    first = where_am[0] == 0
+    low = low_lanes(cot.shape[1:])
+
+    def pack_pair(p, unused):
+        even, odd = cot[2 * p].astype(F32), cot[2 * p + 1].astype(F32)
+        front = jnp.where(low, even, pltpu.roll(odd, LANES // 2, 1)).astype(BF16)
+        back = jnp.where(low, pltpu.roll(even, LANES // 2, 1), odd).astype(BF16)
+        cot_a[p] = jnp.where(first, front, back)
+        cot_b[p] = jnp.where(first, back, front)
+        return unused
+
+    lax.fori_loop(0, cot.shape[0] // 2, pack_pair, 0, unroll=4)
 
 
 def arrived(where_am, direct, routed, p):
@@ -164,17 +171,14 @@
         total[...] = jnp.zeros_like(total)
         for i, acc in enumerate(sums):
             acc[...] = carried[i][...] if part else jnp.zeros_like(acc)
-        for k in range(devs):
-            meta = payloads[k, CAP * slab :, :].astype(F32)
-            for r in range(CAP):
-                ident = jnp.max(meta[r : r + 1, :]).astype(jnp.int32)
-                idents[k * CAP + r] = ident
-                scale = 1.0 / meta[8 + r : 9 + r, :]
-
-                @pl.when(ident >= 0)
-                def _():
-                    at = pl.multiple_of(ident * slab, slab)
-                    total[pl.ds(at, slab), :] += payloads[k, r * slab : (r + 1) * slab, :].astype(F32) * scale
+        metas = [payloads[k, CAP * slab :, :].astype(F32) for k in range(devs)]
+        tops = [(k, r, jnp.max(metas[k][r : r + 1, :])) for k in range(devs) for r in range(CAP)]
+        for k, r, top in tops:
+            ident = top.astype(jnp.int32)
+            idents[k * CAP + r] = ident
+            scale = jnp.where(metas[k][r : r + 1, :] >= 0, 1.0 / metas[k][8 + r : 9 + r, :], 0.0)
+            at = pl.multiple_of(jnp.maximum(ident, 0) * slab, slab)
+            total[pl.ds(at, slab), :] += payloads[k, r * slab : (r + 1) * slab, :].astype(F32) * scale
 
         summed[...] = total[...].astype(BF16)
 
@@ -195,13 +199,12 @@
     normed = (standard * gain[...] + bias[...]).astype(BF16)
     per_half = steps // 2
     pairs = block // LANES
-    at = lax.rem(step, per_half) * (PARTS * pairs) + part * pairs
     to = lax.rem(step, per_half) * pairs
     straight = step // per_half == where_am[0]
     mirrored = []
     for p in range(pairs):
-        crossed = arrived(where_am, got_b, got_c, at + p)
-        mirrored.append(jnp.where(straight, got_a[at + p].astype(F32), crossed).T)
+        crossed = arrived(where_am, got_b, got_c, p)
+        mirrored.append(jnp.where(straight, got_a[p].astype(F32), crossed).T)
     d_low = (turned[...].astype(F32) + jnp.concatenate(mirrored, axis=0)).astype(BF16)
     dz_two = dot_nn(d_low, w_dist_t[...])
     dz_low = dz_two.astype(BF16)
@@ -296,32 +299,23 @@
     lax.fori_loop(0, cols, one, 0, unroll=8)
 
 
-def logits_kernel(where_am, heads, *refs):
-    got, out = refs[:-1], refs[-1]
+def logits_kernel(where_am, heads, got_a, got_b, got_c, *refs):
+    out = refs[-1]
     straight = where_am[0] == 0
     low = low_lanes(heads.shape[1:])
-    per = SQ // PARTS // 2
-    for part in range(PARTS):
-        got_a, got_b, got_c = got[3 * part : 3 * part + 3]
-
-        def one(p, unused):
-            a, b = got_a[p].astype(F32), arrived(where_am, got_b, got_c, p)
-            front, back = jnp.where(straight, a, b), jnp.where(straight, b, a)
-            even = jnp.where(low, front, pltpu.roll(back, LANES // 2, 1))
-            odd = jnp.where(low, pltpu.roll(front, LANES // 2, 1), back)
-            at = p // per * SQ + part * (SQ // PARTS) + 2 * lax.rem(p, per)
-            out[at] = (heads[at].astype(F32) + even).astype(BF16)
-            out[at + 1] = (heads[at + 1].astype(F32) + odd).astype(BF16)
-            return unused
-
-        lax.fori_loop(0, got_a.shape[0], one, 0, unroll=4)
-
-
-def tiles_kernel(devs, target, count, *refs):
-    returned, (out, source) = refs[:PARTS], refs[PARTS:]
+    for p in range(got_a.shape[0]):
+        a, b = got_a[p].astype(F32), arrived(where_am, got_b, got_c, p)
+        front, back = jnp.where(straight, a, b), jnp.where(straight, b, a)
+        even = jnp.where(low, front, pltpu.roll(back, LANES // 2, 1))
+        odd = jnp.where(low, pltpu.roll(front, LANES // 2, 1), back)
+        out[2 * p] = (heads[2 * p].astype(F32) + even).astype(BF16)
+        out[2 * p + 1] = (heads[2 * p + 1].astype(F32) + odd).astype(BF16)
+
+
+def tiles_kernel(devs, target, count, returned, *refs):
+    out, source = refs[-2:]
     feature, cells = out.shape[1:]
     groups = cells // LANES
-    per_part = groups // PARTS
     fill_slots(target, source, devs)
     for k in range(devs):
         for r in range(CAP):
@@ -331,23 +325,26 @@
             def _():
                 scale = 1.0 / jnp.full((1, LANES), count[slot].astype(F32), F32)
                 for c in range(groups):
-                    at = (r * per_part + c % per_part) * feature
-                    piece = returned[c // per_part][k, at : at + feature, :].astype(F32) * scale
+                    at = (r * groups + c) * feature
+                    piece = returned[k, at : at + feature, :].astype(F32) * scale
                     out[slot, :, c * LANES : (c + 1) * LANES] = piece.astype(BF16)
 
 
-def weights_kernel(scale, where_am, mine, other, *outs):
-    g_template, g_gain, g_bias, g_gate, g_up, g_out, g_dist = outs
+def weights_kernel(scale, where_am, *refs):
+    pieces, (g_template, g_gain, g_bias, g_gate, g_up, g_out, g_dist, total) = refs[:-8], refs[-8:]
     width, hidden = g_gate.shape
     feature = g_template.shape[0]
-    half = mine.shape[0] // width
-    lead = where_am[1] == 0
     per = hidden // width
+    rows = pieces[0].shape[0] // 2
+    half = rows * len(pieces)
+    for m, piece in enumerate(pieces):
+        for core in range(2):
+            at = (where_am[1] ^ core) * half + (where_am[3] ^ m) * rows
+            there = pl.ds(pl.multiple_of(at, 32), rows)
+            total[there, :] = piece[core * rows : (core + 1) * rows, :].astype(F32) * scale
 
     def block(i):
-        source = slice(i % half * width, (i % half + 1) * width)
-        here, there = mine[source, :].astype(F32), other[source, :].astype(F32)
-        return (jnp.where(lead, here, there) if i < half else jnp.where(lead, there, here)) * scale
+        return total[i * width : (i + 1) * width, :]
 
     for c in range(per):
         at = slice(c * width, (c + 1) * width)
@@ -400,6 +397,38 @@
         other = swap(low, axis, 1 << bit)
         low = jnp.where(mine == 0, jnp.concatenate([low, other]), jnp.concatenate([other, low]))
     return low
+
+
+def split_kernel(where_am, keep, got, mine, *sends):
+    rows = mine.shape[0]
+    for m, out in enumerate((mine, *sends)):
+        at = pl.multiple_of((where_am[3] ^ m) * rows, 32)
+        out[...] = (keep[pl.ds(at, rows), :] + got[pl.ds(at, rows), :]).astype(out.dtype)
+
+
+def flip(value, m):
+    rows, cols = lax.axis_size("row"), lax.axis_size("col")
+    perm = [(r * cols + c, (r ^ (m & 2)) * cols + (c ^ (m & 1))) for r in range(rows) for c in range(cols)]
+    return lax.ppermute(value, ("row", "col"), perm)
+
+
+def all_sum_four(where_am, keep, got, settle):
+    rows, width = keep.shape[0] // 4, keep.shape[1]
+    mine, *sends = pl.pallas_call(
+        split_kernel,
+        out_shape=[jax.ShapeDtypeStruct((rows, width), F32 if m == 0 else BF16) for m in range(4)],
+        in_specs=[SMEM] + [VMEM] * 2,
+        out_specs=[VMEM] * 4,
+        compiler_params=params(),
+        cost_estimate=cost(1),
+        name="split_sums",
+    )(where_am, keep, got)
+    a, b, c = [flip(send, m + 1).astype(F32) for m, send in enumerate(sends)]
+    low = settle[0](((mine + a) + (b + c)).astype(BF16))
+    a, b, c = [swap(low, "col", m).astype(F32) for m in (2, 4, 6)]
+    low = settle[1](((low.astype(F32) + a) + (b + c)).astype(BF16))
+    both = jnp.concatenate([low, swap(low, "row", 1)])
+    return [both] + [flip(both, m) for m in (1, 2, 3)]
 
 
 def per_device(
@@ -430,7 +459,8 @@
     my_row, my_col = lax.axis_index("row"), lax.axis_index("col")
     two_chips = row_devs == 4
     crosses = (my_col // halves // 2 != my_row // 2) & two_chips
-    where_am = jnp.stack([my_col % halves, my_row % 2, crosses.astype(jnp.int32)]).astype(jnp.int32)
+    quarter = jnp.where(two_chips, my_row // 2 * 2 + my_col % 2, 0)
+    where_am = jnp.stack([my_col % halves, my_row % 2, crosses.astype(jnp.int32), quarter]).astype(jnp.int32)
     target = tile_target[:, 0]
     tiles_t = jnp.transpose(tiles, (0, 2, 1))
     cot_t = jnp.transpose(logit_cotangent, (1, 2, 0))
@@ -459,19 +489,32 @@
         return jax.ShapeDtypeStruct(shape, dtype)
 
     part_slab = slab // PARTS
-    packed = pl.pallas_call(
-        functools.partial(pack_kernel, col_devs),
-        out_shape=[stacked((col_devs, CAP * part_slab + META, LANES))] * PARTS + [stacked((cols // 2, bins, LANES))] * 2,
-        in_specs=[SMEM] * 4 + [VMEM] * 2,
-        out_specs=[VMEM] * (PARTS + 2),
-        scratch_shapes=[pltpu.SMEM((col_devs * CAP,), jnp.int32)],
+    def pack(part):
+        return pl.pallas_call(
+            functools.partial(pack_kernel, col_devs),
+            grid=(1,),
+            out_shape=stacked((col_devs, CAP * part_slab + META, LANES)),
+            in_specs=[pl.BlockSpec(memory_space=pltpu.HBM)] * 3 + [pl.BlockSpec((slots, feature, cells_sq // PARTS), lambda t: (0, 0, part))],
+            out_specs=pl.BlockSpec((col_devs, CAP * part_slab + META, LANES), lambda t: (0, 0, 0)),
+            scratch_shapes=[pltpu.SMEM((col_devs * CAP,), jnp.int32)]
+            + [pltpu.SMEM((slots,), jnp.int32)] * 3
+            + [pltpu.SemaphoreType.DMA((3,))],
+            compiler_params=params(),
+            cost_estimate=cost(3),
+            name=f"pack_{part}",
+        )(target, tile_square, tile_count, tiles_t)
+
+    payloads = [lax.all_to_all(pack(0), "col", 0, 0, tiled=True), pack(1)]
+    packed_cot = pl.pallas_call(
+        pack_cotangent_kernel,
+        out_shape=[stacked((cols // 2, bins, LANES))] * 2,
+        in_specs=[SMEM, VMEM],
+        out_specs=[VMEM] * 2,
         compiler_params=params(),
-        cost_estimate=cost(5),
-        name="pack",
-    )(where_am, target, tile_square, tile_count, tiles_t, cot_t)
-    payloads = list(packed[:PARTS])
-    payloads[0] = lax.all_to_all(payloads[0], "col", 0, 0, tiled=True)
-    (*got_cot, over), land = mirror(*packed[PARTS:])
+        cost_estimate=cost(2),
+        name="pack_cotangent",
+    )(where_am, cot_t)
+    (*got_cot, over), land = mirror(*packed_cot)
     got_cot.append(land(over))
     payloads[1], *got_cot = lax.optimization_barrier((payloads[1], *got_cot))
     payloads[1] = lax.all_to_all(payloads[1], "col", 0, 0, tiled=True)
@@ -506,7 +549,6 @@
         w_dist_t,
     )
     sums_shapes = [(width, 2 * hidden), (width, hidden), (feature + bins, width), (16, width)]
-    half_heads = (cols // 2, bins, LANES)
     part_heads = (cols // 2 // PARTS, bins, LANES)
     pair_cells = pair.reshape(entries, width)
 
@@ -545,7 +587,7 @@
             out_specs += [whole(*shape) for shape in sums_shapes]
         inputs = (where_am, payloads[part], pair_cells, turned, *got_cot, *operands)
         in_specs = [SMEM, whole(col_devs, CAP * part_slab + META, LANES), per_step(width), per_step(bins)]
-        in_specs += [whole(*half_heads)] * 3
+        in_specs += [pl.BlockSpec((block // LANES, bins, LANES), lambda t: (t % (steps // 2) * PARTS + part, 0, 0))] * 3
         in_specs += [whole(*operand.shape) for operand in operands]
         aliases = {}
         if part:
@@ -572,9 +614,10 @@
         before = (grad_pair, *outs[5:])
         z_low.append(outs[1])
         if part == PARTS - 1:
-            keep, send, returned[0], *got_heads[0] = lax.optimization_barrier((*outs[5:], *returned, *got_heads[0]))
+            keep, send = outs[5:]
+            keep, send, returned[0], *got_heads[0] = lax.optimization_barrier((keep, send, *returned, *got_heads[0]))
+            send = swap(send, "row", 1)
             got_heads[0][2] = land(got_heads[0][2])
-            sums = keep + swap(send, "row", 1)
         got, land = mirror(outs[2], outs[3])
         got_heads.append(got)
         returned.append(lax.all_to_all(outs[4], "col", 0, 0, tiled=True))
@@ -602,27 +645,45 @@
         value, own[0], returned[1] = lax.optimization_barrier((value, own[0], returned[1]))
         return value
 
-    sums = all_sum(sums, (heads_sent, heads_landed))
-    other = swap(sums, "row", 1)
-    logits = pl.pallas_call(
-        logits_kernel,
-        out_shape=jax.ShapeDtypeStruct((cols, bins, rows), BF16),
-        in_specs=[SMEM] + [VMEM] * (1 + 3 * PARTS),
-        out_specs=VMEM,
-        compiler_params=params(),
-        cost_estimate=cost(3),
-        name="logits",
-    )(where_am, own[0], *got_heads[0], *got_heads[1])
-    grad_tiles = pl.pallas_call(
-        functools.partial(tiles_kernel, col_devs),
-        out_shape=jax.ShapeDtypeStruct((slots, feature, cells_sq), BF16),
-        in_specs=[SMEM] * 2 + [VMEM] * PARTS,
-        out_specs=VMEM,
-        scratch_shapes=[pltpu.SMEM((col_devs * CAP,), jnp.int32)],
-        compiler_params=params(),
-        cost_estimate=cost(4),
-        name="tile_gradients",
-    )(target, tile_count, *returned)
+    if two_chips:
+        pieces = all_sum_four(where_am, keep, send, (heads_sent, heads_landed))
+    else:
+        sums = all_sum(keep + send, (heads_sent, heads_landed))
+        pieces = [jnp.concatenate([sums, swap(sums, "row", 1)])]
+    def logits_of(part, before):
+        half = SQ // PARTS
+        there = pl.BlockSpec((half, bins, rows), lambda t: (PARTS * t + part, 0, 0))
+        return pl.pallas_call(
+            logits_kernel,
+            grid=(cols // SQ,),
+            out_shape=stacked((cols, bins, rows)),
+            in_specs=[SMEM, there] + [pl.BlockSpec((half // 2, bins, LANES), lambda t: (t, 0, 0))] * 3 + [ANY] * part,
+            out_specs=there,
+            input_output_aliases={5: 0} if part else {},
+            compiler_params=params(),
+            cost_estimate=cost(2),
+            name=f"logits_{part}",
+        )(where_am, own[0], *got_heads[part], *before)
+
+    def tile_gradients(part, before):
+        return pl.pallas_call(
+            functools.partial(tiles_kernel, col_devs),
+            grid=(1,),
+            out_shape=stacked((slots, feature, cells_sq)),
+            in_specs=[SMEM] * 2 + [pl.BlockSpec((col_devs, CAP * part_slab, LANES), lambda t: (0, 0, 0))] + [ANY] * part,
+            out_specs=pl.BlockSpec((slots, feature, cells_sq // PARTS), lambda t: (0, 0, part)),
+            scratch_shapes=[pltpu.SMEM((col_devs * CAP,), jnp.int32)],
+            input_output_aliases={3: 0} if part else {},
+            compiler_params=params(),
+            cost_estimate=cost(2),
+            name=f"tile_gradients_{part}",
+        )(target, tile_count, returned[part], *before)
+
+    logits, grad_tiles = (), ()
+    for part in range(PARTS):
+        logits = (logits_of(part, logits),)
+        grad_tiles = (tile_gradients(part, grad_tiles),)
+    *pieces, logits, grad_tiles = lax.optimization_barrier((*pieces, logits[0], grad_tiles[0]))
     length = rows * row_devs
     weights = pl.pallas_call(
         functools.partial(weights_kernel, 1.0 / length),
@@ -635,12 +696,13 @@
             jax.ShapeDtypeStruct((hidden, width), F32),
             jax.ShapeDtypeStruct((bins, width), F32),
         ],
-        in_specs=[SMEM] + [VMEM] * 2,
+        in_specs=[SMEM] + [VMEM] * len(pieces),
         out_specs=[VMEM] * 7,
+        scratch_shapes=[pltpu.VMEM((2 * sum_shape[0], width), F32)],
         compiler_params=params(),
         cost_estimate=cost(2),
         name="weight_gradients",
-    )(where_am, sums, other)
+    )(where_am, *pieces)
     g_template, g_gain, g_bias, g_gate, g_up, g_out, g_dist = weights
     return (
         jnp.transpose(logits, (2, 0, 1)),

time: 209 us -> 196 us (0.938)
  the two profiles are of different devices: /device:TPU:25 before, /device:TPU:18 now
where the time goes in v3:
time: 196 us; the launch traced here: 194 us
  starting transfers between devices  74.2 us (38%)
  Pallas kernels  66.1 us (34%)
  waiting for transfers between devices  47 us (24%)
  local copies, waits for them, and re-layouts  5.08 us (3%)
    pallas_call x2, Pallas kernels, transition(): pl.pallas_call(functools.partial(main_kernel, col_devs, cols, part), grid...  37.5 us
    ppermute x12, waiting for transfers between devices, move(): return lax.ppermute(value, ('row', 'col'), perm)  36.2 us
    ppermute x12, starting transfers between devices, move(): return lax.ppermute(value, ('row', 'col'), perm)  30.9 us
    all_to_all x2, starting transfers between devices, per_device(): returned.append(lax.all_to_all(outs[4], 'col', 0, 0, tiled=True))  15.6 us
    all_to_all x1, starting transfers between devices, per_device(): payloads[1] = lax.all_to_all(payloads[1], 'col', 0, 0, tiled=True)  8.38 us
    pallas_call x2, Pallas kernels, pack(): pl.pallas_call(functools.partial(pack_kernel, col_devs), grid=(1,), out_s...  6.73 us
    ppermute x6, starting transfers between devices, flip(): return lax.ppermute(value, ('row', 'col'), perm)  6.62 us
    ppermute x5, starting transfers between devices, swap(): lax.ppermute(value, axis, [(i, i ^ mask) for i in range(lax.axis_size(axi...  6.53 us
  transfers between devices with their start and end apart: 27, of which 9 were waited for; matrix products, arithmetic and copies ran while one was open for 0% of the time, Pallas kernels for 32%

profile of v3, /device:TPU:18, one launch (start us, length us, event | category | flops | bytes accessed | tf_op | source)
XLA Modules:
  0.0 193.8 jit_solution(13591660019389298517)
XLA Ops:
  2.6 3.4 %pack_0.1 = bf16[8,528,128]{2,1,0:T(8,128)(2,1)} custom-call(s32[16]{0:T(128)S(1)} %bitcast.35, s32[16]{0:T(128)S(1)} %copy-done.10, s32[16]{0:T(128)S(1)} %copy-done.16, bf16[16,64,1024]{2,1,0:T(8,128)(2,1)} %bitcast.41), custom_call_target="tpu_custom_call" | custom-call | flops 3300000000 | tf_op jit(solution)/shard_map/pack_0/pallas_call | solution.py:493
  6.0 6.2 %all-to-all-start.1 = ((bf16[8,528,128]{2,1,0:T(8,128)(2,1)}), bf16[8,528,128]{2,1,0:T(8,128)(2,1)}, u32[]{:S(2)}, u32[]{:S(2)}) async-start(bf16[8,528,128]{2,1,0:T(8,128)(2,1)} %pack_0.1), calls=%async_computation.1 | async-start | bytes 2162688 | tf_op jit(solution)/shard_map/all_to_all | solution.py:507
  12.2 2.2 %pack_cotangent.1 = (bf16[32,64,128]{2,1,0:T(8,128)(2,1)S(1)}, bf16[32,64,128]{2,1,0:T(8,128)(2,1)S(1)}) custom-call(s32[4]{0:T(128)S(1)} %pad_add_fusion.where_am.refs_0_, bf16[64,64,128]{2,1,0:T(8,128)(2,1)} %bitcast.26), custom_call_target="tpu_custom_call" | custom-call | flops 2200000000 | tf_op jit(solution)/shard_map/pack_cotangent/pallas_call | solution.py:508
  15.7 3.4 %collective-permute-start.1 = (bf16[32,64,128]{2,1,0:T(8,128)(2,1)S(1)}, bf16[32,64,128]{2,1,0:T(8,128)(2,1)S(1)}, u32[]{:S(2)}, u32[]{:S(2)}) collective-permute-start(bf16[32,64,128]{2,1,0:T(8,128)(2,1)S(1)} %get-tuple-element.64), channel_id=1, source_target_pairs={{0,1},{1,0},{2,9},{3,8},{8,3},{9,2},{10,11},{11,10},{20,21},{21,20... | collective-permute-start | bytes 1572872 | tf_op jit(solution)/shard_map/ppermute | solution.py:474
  19.2 1.6 collective-permute-start
  20.8 8.8 %collective-permute-done.2 = bf16[32,64,128]{2,1,0:T(8,128)(2,1)} collective-permute-done((bf16[32,64,128]{2,1,0:T(8,128)(2,1)S(1)}, bf16[32,64,128]{2,1,0:T(8,128)(2,1)}, u32[]{:S(2)}, u32[]{:S(2)}) %collective-permute-start.2) | collective-permute-done | bytes 524320 | tf_op jit(solution)/shard_map/ppermute | solution.py:474
  29.5 2.1 %collective-permute-start.3 = (bf16[32,64,128]{2,1,0:T(8,128)(2,1)}, bf16[32,64,128]{2,1,0:T(8,128)(2,1)}, u32[]{:S(2)}, u32[]{:S(2)}) collective-permute-start(bf16[32,64,128]{2,1,0:T(8,128)(2,1)} %collective-permute-done.2), channel_id=1, source_target_pairs={{20,17},{21,16},{22,25},{23,24},{28,19},{29,18},{30,27},{31,26},{0... | collective-permute-start | bytes 1572872 | tf_op jit(solution)/shard_map/ppermute | solution.py:474
  31.7 3.4 %pack_1.1 = bf16[8,528,128]{2,1,0:T(8,128)(2,1)} custom-call(s32[16]{0:T(128)S(1)} %bitcast.36, s32[16]{0:T(128)S(1)} %copy-done.11, s32[16]{0:T(128)S(1)} %copy-done.17, bf16[16,64,1024]{2,1,0:T(8,128)(2,1)} %bitcast.42), custom_call_target="tpu_custom_call" | custom-call | flops 3300000000 | tf_op jit(solution)/shard_map/pack_1/pallas_call | solution.py:493
  35.5 4.9 %turn.1.refs_3_ = bf16[8192,64]{1,0:T(8,128)(2,1)} custom-call(bf16[64,64,128]{2,1,0:T(8,128)(2,1)S(1)} %bitcast.27), custom_call_target="tpu_custom_call" | custom-call | flops 5500000256 | tf_op jit(solution)/shard_map/turn/pallas_call | solution.py:522
  40.4 17.4 %collective-permute-done.3.refs_6_ = bf16[32,64,128]{2,1,0:T(8,128)(2,1)} collective-permute-done((bf16[32,64,128]{2,1,0:T(8,128)(2,1)}, bf16[32,64,128]{2,1,0:T(8,128)(2,1)}, u32[]{:S(2)}, u32[]{:S(2)}) %collective-permute-start.3) | collective-permute-done | bytes 524320 | tf_op jit(solution)/shard_map/ppermute | solution.py:474
  57.8 8.4 %all-to-all-start = ((bf16[8,528,128]{2,1,0:T(8,128)(2,1)}), bf16[8,528,128]{2,1,0:T(8,128)(2,1)}, u32[]{:S(2)}, u32[]{:S(2)}) async-start(bf16[8,528,128]{2,1,0:T(8,128)(2,1)} %pack_1.1), calls=%async_computation | async-start | bytes 2162688 | tf_op jit(solution)/shard_map/all_to_all | solution.py:520
  66.2 18.6 %transition_0.1 = (f32[8192,128]{1,0:T(8,128)}, bf16[4096,128]{1,0:T(8,128)(2,1)}, bf16[16,64,128]{2,1,0:T(8,128)(2,1)S(1)}, bf16[16,64,128]{2,1,0:T(8,128)(2,1)...) custom-call(s32[4]{0:T(128)S(1)} %pad_add_fusion.where_am.refs_0_, ...), custom_call_target="tpu_custom_call" | custom-call | flops 22000001024 | tf_op jit(solution)/shard_map/transition_0/pallas_call | solution.py:597
  86.1 3.4 %collective-permute-start.5 = (bf16[16,64,128]{2,1,0:T(8,128)(2,1)S(1)}, bf16[16,64,128]{2,1,0:T(8,128)(2,1)S(1)}, u32[]{:S(2)}, u32[]{:S(2)}) collective-permute-start(bf16[16,64,128]{2,1,0:T(8,128)(2,1)S(1)} %get-tuple-element.78), channel_id=1, source_target_pairs={{0,1},{1,0},{2,9},{3,8},{8,3},{9,2},{10,11},{11,10},{20,21},{21,20... | collective-permute-start | bytes 786440 | tf_op jit(solution)/shard_map/ppermute | solution.py:474
  90.2 7.7 %all-to-all-start.2 = ((bf16[8,512,128]{2,1,0:T(8,128)(2,1)}), bf16[8,512,128]{2,1,0:T(8,128)(2,1)S(1)}, u32[]{:S(2)}, u32[]{:S(2)}) async-start(bf16[8,512,128]{2,1,0:T(8,128)(2,1)} %get-tuple-element.76), calls=%async_computation.2 | async-start | bytes 2097152 | tf_op jit(solution)/shard_map/all_to_all | solution.py:623
  98.9 18.9 %transition_1.1 = (f32[8192,128]{1,0:T(8,128)}, bf16[4096,128]{1,0:T(8,128)(2,1)}, bf16[16,64,128]{2,1,0:T(8,128)(2,1)S(1)}, bf16[16,64,128]{2,1,0:T(8,128)(2,1)...) custom-call(s32[4]{0:T(128)S(1)} %pad_add_fusion.where_am.refs_0_, ...), custom_call_target="tpu_custom_call", output_to_operand_aliasing={{0}: (17, {})} | custom-call | flops 22000001024 | tf_op jit(solution)/shard_map/transition_1/pallas_call | solution.py:597
  118.5 4.6 %all-to-all-done.2.returned = bf16[8,512,128]{2,1,0:T(8,128)(2,1)S(1)} async-done(((bf16[8,512,128]{2,1,0:T(8,128)(2,1)}), bf16[8,512,128]{2,1,0:T(8,128)(2,1)S(1)}, u32[]{:S(2)}, u32[]{:S(2)}) %all-to-all-start.2) | async-done | bytes 1048608 | tf_op jit(solution)/shard_map/all_to_all | solution.py:623
  123.1 7.9 %all-to-all-start.3 = ((bf16[8,512,128]{2,1,0:T(8,128)(2,1)}), bf16[8,512,128]{2,1,0:T(8,128)(2,1)S(1)}, u32[]{:S(2)}, u32[]{:S(2)}) async-start(bf16[8,512,128]{2,1,0:T(8,128)(2,1)} %get-tuple-element.91), calls=%async_computation.3 | async-start | bytes 2097152 | tf_op jit(solution)/shard_map/all_to_all | solution.py:623
  131.1 2.0 %collective-permute-done.7.got = f32[896,128]{1,0:T(8,128)S(1)} collective-permute-done((f32[896,128]{1,0:T(8,128)}, f32[896,128]{1,0:T(8,128)S(1)}, u32[]{:S(2)}, u32[]{:S(2)}) %collective-permute-start.7) | collective-permute-done | bytes 458784 | tf_op jit(solution)/shard_map/ppermute | solution.py:373
  139.1 2.5 %collective-permute-start.12 = (bf16[16,64,128]{2,1,0:T(8,128)(2,1)S(1)}, bf16[16,64,128]{2,1,0:T(8,128)(2,1)S(1)}, u32[]{:S(2)}, u32[]{:S(2)}) collective-permute-start(bf16[16,64,128]{2,1,0:T(8,128)(2,1)S(1)} %get-tuple-element.86), channel_id=1, source_target_pairs={{0,1},{1,0},{2,9},{3,8},{8,3},{9,2},{10,11},{11,10},{20,21},{21,20... | collective-permute-start | bytes 786440 | tf_op jit(solution)/shard_map/ppermute | solution.py:474
  142.3 7.2 %collective-permute-start.14 = (bf16[16,64,128]{2,1,0:T(8,128)(2,1)}, bf16[16,64,128]{2,1,0:T(8,128)(2,1)S(1)}, u32[]{:S(2)}, u32[]{:S(2)}) collective-permute-start(bf16[16,64,128]{2,1,0:T(8,128)(2,1)} %collective-permute-done.6), channel_id=1, source_target_pairs={{20,17},{21,16},{22,25},{23,24},{28,19},{29,18},{30,27},{31,26},{0... | collective-permute-start | bytes 786440 | tf_op jit(solution)/shard_map/ppermute | solution.py:474
  149.6 5.0 %own_heads.1.heads = bf16[64,64,128]{2,1,0:T(8,128)(2,1)S(1)} custom-call(bf16[4096,128]{1,0:T(8,128)(2,1)} %get-tuple-element.89.refs_0_, bf16[4096,128]{1,0:T(8,128)(2,1)} %get-tuple-element.90.refs_1_, bf16[64,128]{1,0:T(8,128)(2,1)S(1)} %bitcast.30), custom_call_target="tpu_custom_call" | custom-call | flops 5500000256 | tf_op jit(solution)/shard_map/own_heads/pallas_call | solution.py:625
  155.0 10.0 %collective-permute-done.14.got_c = bf16[16,64,128]{2,1,0:T(8,128)(2,1)S(1)} collective-permute-done((bf16[16,64,128]{2,1,0:T(8,128)(2,1)}, bf16[16,64,128]{2,1,0:T(8,128)(2,1)S(1)}, u32[]{:S(2)}, u32[]{:S(2)}) %collective-permute-start.14) | collective-permute-done | bytes 262176 | tf_op jit(solution)/shard_map/ppermute | solution.py:474
  165.1 2.6 %collective-permute-start.17 = (bf16[224,128]{1,0:T(8,128)(2,1)S(1)}, bf16[224,128]{1,0:T(8,128)(2,1)S(1)}, u32[]{:S(2)}, u32[]{:S(2)}) collective-permute-start(bf16[224,128]{1,0:T(8,128)(2,1)S(1)} %add_convert_fusion.1), channel_id=1, source_target_pairs={{0,6},{1,7},{2,4},{3,5},{4,2},{5,3},{6,0},{7,1},{8,14},{9,15},{10,... | collective-permute-start | bytes 172040 | tf_op jit(solution)/shard_map/ppermute | solution.py:373
  167.7 2.3 %collective-permute-start.16 = (bf16[224,128]{1,0:T(8,128)(2,1)S(1)}, bf16[224,128]{1,0:T(8,128)(2,1)S(1)}, u32[]{:S(2)}, u32[]{:S(2)}) collective-permute-start(bf16[224,128]{1,0:T(8,128)(2,1)S(1)} %add_convert_fusion.1), channel_id=1, source_target_pairs={{0,4},{1,5},{2,6},{3,7},{4,0},{5,1},{6,2},{7,3},{8,12},{9,13},{10,... | collective-permute-start | bytes 172040 | tf_op jit(solution)/shard_map/ppermute | solution.py:373
  171.4 2.2 %tile_gradients_0.1.refs_0_ = bf16[16,64,1024]{2,1,0:T(8,128)(2,1)} custom-call(s32[16]{0:T(128)S(1)} %bitcast.37, s32[16]{0:T(128)S(1)} %copy-done.17, bf16[8,512,128]{2,1,0:T(8,128)(2,1)S(1)} %all-to-all-done.2.returned), custom_call_target="tpu_custom_call" | custom-call | flops 2200000000 | tf_op jit(solution)/shard_map/tile_gradients_0/pallas_call | solution.py:669
  173.7 5.5 %collective-permute-start.22 = (bf16[16,64,128]{2,1,0:T(8,128)(2,1)}, bf16[16,64,128]{2,1,0:T(8,128)(2,1)S(1)}, u32[]{:S(2)}, u32[]{:S(2)}) collective-permute-start(bf16[16,64,128]{2,1,0:T(8,128)(2,1)} %collective-permute-done.13), channel_id=1, source_target_pairs={{20,17},{21,16},{22,25},{23,24},{28,19},{29,18},{30,27},{31,26},{0... | collective-permute-start | bytes 786440 | tf_op jit(solution)/shard_map/ppermute | solution.py:474
  179.4 2.2 %tile_gradients_1.1 = bf16[16,64,1024]{2,1,0:T(8,128)(2,1)} custom-call(s32[16]{0:T(128)S(1)} %bitcast.38, s32[16]{0:T(128)S(1)} %copy-done.17, bf16[8,512,128]{2,1,0:T(8,128)(2,1)S(1)} %all-to-all-done.3.returned, bf16[16,64,1024]{2,1,0:T(8,128)(2,1)} %tile_gradients_0.1.refs_0_), custom_call_target="tpu_custom_call", output_to_operand_aliasing={{}: (3, {})} | custom-call | flops 2200000000 | tf_op jit(solution)/shard_map/tile_gradients_1/pallas_call | solution.py:669
  181.6 1.6 logits_0.1.refs_0_
  183.3 2.2 %collective-permute-start.20 = (bf16[448,128]{1,0:T(8,128)(2,1)S(1)}, bf16[448,128]{1,0:T(8,128)(2,1)S(1)}, u32[]{:S(2)}, u32[]{:S(2)}) collective-permute-start(bf16[448,128]{1,0:T(8,128)(2,1)S(1)} %constant_dynamic-update-slice_fusion.refs_0_), channel_id=1, source_target_pairs={{0,16},{1,17},{2,18},{3,19},{4,20},{5,21},{6,22},{7,23},{8,24},{9,... | collective-permute-start | bytes 344072 | tf_op jit(solution)/shard_map/ppermute | solution.py:412
  186.8 1.6 logits_1.1
  188.4 1.8 collective-permute-done.21.refs_3_
  192.2 1.6 weight_gradients.1
  (91 shorter events, 19.5 us)
Async XLA Ops:
  6.0 51.9 %all-to-all-start.1 = ((bf16[8,528,128]{2,1,0:T(8,128)(2,1)}), bf16[8,528,128]{2,1,0:T(8,128)(2,1)}, u32[]{:S(2)}, u32[]{:S(2)}) async-start(bf16[8,528,128]{2,1,0:T(8,128)(2,1)} %pack_0.1), calls=%async_computation.1 | async-start | bytes 2162688 | tf_op jit(solution)/shard_map/all_to_all | solution.py:507
  14.4 15.1 %collective-permute-start.2 = (bf16[32,64,128]{2,1,0:T(8,128)(2,1)S(1)}, bf16[32,64,128]{2,1,0:T(8,128)(2,1)}, u32[]{:S(2)}, u32[]{:S(2)}) collective-permute-start(bf16[32,64,128]{2,1,0:T(8,128)(2,1)S(1)} %get-tuple-element.64), channel_id=1, source_target_pairs={{4,20},{5,21},{6,22},{7,23},{12,28},{13,29},{14,30},{15,31},{16,0}... | collective-permute-start | bytes 1572872 | tf_op jit(solution)/shard_map/ppermute | solution.py:474
  15.7 24.6 %collective-permute-start.1 = (bf16[32,64,128]{2,1,0:T(8,128)(2,1)S(1)}, bf16[32,64,128]{2,1,0:T(8,128)(2,1)S(1)}, u32[]{:S(2)}, u32[]{:S(2)}) collective-permute-start(bf16[32,64,128]{2,1,0:T(8,128)(2,1)S(1)} %get-tuple-element.64), channel_id=1, source_target_pairs={{0,1},{1,0},{2,9},{3,8},{8,3},{9,2},{10,11},{11,10},{20,21},{21,20... | collective-permute-start | bytes 1572872 | tf_op jit(solution)/shard_map/ppermute | solution.py:474
  19.2 21.2 %collective-permute-start = (bf16[32,64,128]{2,1,0:T(8,128)(2,1)S(1)}, bf16[32,64,128]{2,1,0:T(8,128)(2,1)}, u32[]{:S(2)}, u32[]{:S(2)}) collective-permute-start(bf16[32,64,128]{2,1,0:T(8,128)(2,1)S(1)} %get-tuple-element.63), channel_id=1, source_target_pairs={{0,0},{1,1},{2,8},{3,9},{4,16},{5,17},{6,24},{7,25},{8,2},{9,3},{1... | collective-permute-start | bytes 1572872 | tf_op jit(solution)/shard_map/ppermute | solution.py:474
  29.5 28.3 %collective-permute-start.3 = (bf16[32,64,128]{2,1,0:T(8,128)(2,1)}, bf16[32,64,128]{2,1,0:T(8,128)(2,1)}, u32[]{:S(2)}, u32[]{:S(2)}) collective-permute-start(bf16[32,64,128]{2,1,0:T(8,128)(2,1)} %collective-permute-done.2), channel_id=1, source_target_pairs={{20,17},{21,16},{22,25},{23,24},{28,19},{29,18},{30,27},{31,26},{0... | collective-permute-start | bytes 1572872 | tf_op jit(solution)/shard_map/ppermute | solution.py:474
  40.4 25.8 %copy-start.8 = (bf16[64,128]{1,0:T(8,128)(2,1)S(1)}, bf16[64,128]{1,0:T(8,128)(2,1)}, u32[]{:S(2)}) copy-start(bf16[64,128]{1,0:T(8,128)(2,1)} %refs_7_.3) | copy-start | bytes 49156
  40.4 25.8 %copy-start.9 = (bf16[128,64]{0,1:T(8,128)(2,1)S(1)}, bf16[128,64]{0,1:T(8,128)(2,1)}, u32[]{:S(2)}) copy-start(bf16[128,64]{0,1:T(8,128)(2,1)} %param.25) | copy-start | bytes 49156
  40.4 25.9 %copy-start.12 = (f32[128]{0:T(128)S(1)}, f32[128]{0:T(128)}, u32[]{:S(2)}) copy-start(f32[128]{0:T(128)} %param.20) | copy-start | bytes 1540
  40.4 25.9 %copy-start.13 = (f32[128]{0:T(128)S(1)}, f32[128]{0:T(128)}, u32[]{:S(2)}) copy-start(f32[128]{0:T(128)} %param.21) | copy-start | bytes 1540
  40.4 25.8 %copy-start.23 = (bf16[32,64,128]{2,1,0:T(8,128)(2,1)}, bf16[32,64,128]{2,1,0:T(8,128)(2,1)S(1)}, u32[]{:S(2)}) copy-start(bf16[32,64,128]{2,1,0:T(8,128)(2,1)S(1)} %collective-permute-done.1.refs_5_) | copy-start | bytes 1572868
  57.8 32.4 %all-to-all-start = ((bf16[8,528,128]{2,1,0:T(8,128)(2,1)}), bf16[8,528,128]{2,1,0:T(8,128)(2,1)}, u32[]{:S(2)}, u32[]{:S(2)}) async-start(bf16[8,528,128]{2,1,0:T(8,128)(2,1)} %pack_1.1), calls=%async_computation | async-start | bytes 2162688 | tf_op jit(solution)/shard_map/all_to_all | solution.py:520
  84.8 46.2 %collective-permute-start.6 = (bf16[16,64,128]{2,1,0:T(8,128)(2,1)S(1)}, bf16[16,64,128]{2,1,0:T(8,128)(2,1)}, u32[]{:S(2)}, u32[]{:S(2)}) collective-permute-start(bf16[16,64,128]{2,1,0:T(8,128)(2,1)S(1)} %get-tuple-element.78), channel_id=1, source_target_pairs={{4,20},{5,21},{6,22},{7,23},{12,28},{13,29},{14,30},{15,31},{16,0}... | collective-permute-start | bytes 786440 | tf_op jit(solution)/shard_map/ppermute | solution.py:474
  86.1 44.9 %collective-permute-start.5 = (bf16[16,64,128]{2,1,0:T(8,128)(2,1)S(1)}, bf16[16,64,128]{2,1,0:T(8,128)(2,1)S(1)}, u32[]{:S(2)}, u32[]{:S(2)}) collective-permute-start(bf16[16,64,128]{2,1,0:T(8,128)(2,1)S(1)} %get-tuple-element.78), channel_id=1, source_target_pairs={{0,1},{1,0},{2,9},{3,8},{8,3},{9,2},{10,11},{11,10},{20,21},{21,20... | collective-permute-start | bytes 786440 | tf_op jit(solution)/shard_map/ppermute | solution.py:474
  89.5 41.5 %collective-permute-start.4 = (bf16[16,64,128]{2,1,0:T(8,128)(2,1)S(1)}, bf16[16,64,128]{2,1,0:T(8,128)(2,1)S(1)}, u32[]{:S(2)}, u32[]{:S(2)}) collective-permute-start(bf16[16,64,128]{2,1,0:T(8,128)(2,1)S(1)} %get-tuple-element.77), channel_id=1, source_target_pairs={{0,0},{1,1},{2,8},{3,9},{4,16},{5,17},{6,24},{7,25},{8,2},{9,3},{1... | collective-permute-start | bytes 786440 | tf_op jit(solution)/shard_map/ppermute | solution.py:474
  90.2 32.9 %all-to-all-start.2 = ((bf16[8,512,128]{2,1,0:T(8,128)(2,1)}), bf16[8,512,128]{2,1,0:T(8,128)(2,1)S(1)}, u32[]{:S(2)}, u32[]{:S(2)}) async-start(bf16[8,512,128]{2,1,0:T(8,128)(2,1)} %get-tuple-element.76), calls=%async_computation.2 | async-start | bytes 2097152 | tf_op jit(solution)/shard_map/all_to_all | solution.py:623
  123.1 56.1 %all-to-all-start.3 = ((bf16[8,512,128]{2,1,0:T(8,128)(2,1)}), bf16[8,512,128]{2,1,0:T(8,128)(2,1)S(1)}, u32[]{:S(2)}, u32[]{:S(2)}) async-start(bf16[8,512,128]{2,1,0:T(8,128)(2,1)} %get-tuple-element.91), calls=%async_computation.3 | async-start | bytes 2097152 | tf_op jit(solution)/shard_map/all_to_all | solution.py:623
  131.1 2.1 %collective-permute-start.7 = (f32[896,128]{1,0:T(8,128)}, f32[896,128]{1,0:T(8,128)S(1)}, u32[]{:S(2)}, u32[]{:S(2)}) collective-permute-start(f32[896,128]{1,0:T(8,128)} %get-tuple-element.80), channel_id=1, source_target_pairs={{0,8},{8,0},{16,24},{24,16},{1,9},{9,1},{17,25},{25,17},{2,10},{10... | collective-permute-start | bytes 1376264 | tf_op jit(solution)/shard_map/ppermute | solution.py:373
  134.8 7.5 %collective-permute-start.8 = (bf16[224,128]{1,0:T(8,128)(2,1)S(1)}, bf16[224,128]{1,0:T(8,128)(2,1)S(1)}, u32[]{:S(2)}, u32[]{:S(2)}) collective-permute-start(bf16[224,128]{1,0:T(8,128)(2,1)S(1)} %get-tuple-element.82), channel_id=1, source_target_pairs={{0,1},{1,0},{2,3},{3,2},{4,5},{5,4},{6,7},{7,6},{8,9},{9,8},{10,11... | collective-permute-start | bytes 172040 | tf_op jit(solution)/shard_map/ppermute | solution.py:412
  136.3 13.2 %collective-permute-start.9 = (bf16[224,128]{1,0:T(8,128)(2,1)S(1)}, bf16[224,128]{1,0:T(8,128)(2,1)S(1)}, u32[]{:S(2)}, u32[]{:S(2)}) collective-permute-start(bf16[224,128]{1,0:T(8,128)(2,1)S(1)} %get-tuple-element.83), channel_id=1, source_target_pairs={{0,16},{1,17},{2,18},{3,19},{4,20},{5,21},{6,22},{7,23},{8,24},{9,... | collective-permute-start | bytes 172040 | tf_op jit(solution)/shard_map/ppermute | solution.py:412
  137.8 17.2 %collective-permute-start.13 = (bf16[16,64,128]{2,1,0:T(8,128)(2,1)S(1)}, bf16[16,64,128]{2,1,0:T(8,128)(2,1)}, u32[]{:S(2)}, u32[]{:S(2)}) collective-permute-start(bf16[16,64,128]{2,1,0:T(8,128)(2,1)S(1)} %get-tuple-element.86), channel_id=1, source_target_pairs={{4,20},{5,21},{6,22},{7,23},{12,28},{13,29},{14,30},{15,31},{16,0}... | collective-permute-start | bytes 786440 | tf_op jit(solution)/shard_map/ppermute | solution.py:474
  139.1 15.9 %collective-permute-start.12 = (bf16[16,64,128]{2,1,0:T(8,128)(2,1)S(1)}, bf16[16,64,128]{2,1,0:T(8,128)(2,1)S(1)}, u32[]{:S(2)}, u32[]{:S(2)}) collective-permute-start(bf16[16,64,128]{2,1,0:T(8,128)(2,1)S(1)} %get-tuple-element.86), channel_id=1, source_target_pairs={{0,1},{1,0},{2,9},{3,8},{8,3},{9,2},{10,11},{11,10},{20,21},{21,20... | collective-permute-start | bytes 786440 | tf_op jit(solution)/shard_map/ppermute | solution.py:474
  141.6 13.4 %collective-permute-start.11 = (bf16[16,64,128]{2,1,0:T(8,128)(2,1)S(1)}, bf16[16,64,128]{2,1,0:T(8,128)(2,1)S(1)}, u32[]{:S(2)}, u32[]{:S(2)}) collective-permute-start(bf16[16,64,128]{2,1,0:T(8,128)(2,1)S(1)} %copy-done.5), channel_id=1, source_target_pairs={{0,0},{1,1},{2,8},{3,9},{4,16},{5,17},{6,24},{7,25},{8,2},{9,3},{1... | collective-permute-start | bytes 786440 | tf_op jit(solution)/shard_map/ppermute | solution.py:474
  142.3 22.8 %collective-permute-start.14 = (bf16[16,64,128]{2,1,0:T(8,128)(2,1)}, bf16[16,64,128]{2,1,0:T(8,128)(2,1)S(1)}, u32[]{:S(2)}, u32[]{:S(2)}) collective-permute-start(bf16[16,64,128]{2,1,0:T(8,128)(2,1)} %collective-permute-done.6), channel_id=1, source_target_pairs={{20,17},{21,16},{22,25},{23,24},{28,19},{29,18},{30,27},{31,26},{0... | collective-permute-start | bytes 786440 | tf_op jit(solution)/shard_map/ppermute | solution.py:474
  149.5 5.4 %collective-permute-start.10 = (bf16[224,128]{1,0:T(8,128)(2,1)S(1)}, bf16[224,128]{1,0:T(8,128)(2,1)S(1)}, u32[]{:S(2)}, u32[]{:S(2)}) collective-permute-start(bf16[224,128]{1,0:T(8,128)(2,1)S(1)} %get-tuple-element.84), channel_id=1, source_target_pairs={{0,17},{1,16},{2,19},{3,18},{4,21},{5,20},{6,23},{7,22},{8,25},{9,... | collective-permute-start | bytes 172040 | tf_op jit(solution)/shard_map/ppermute | solution.py:412
  165.1 14.1 %collective-permute-start.17 = (bf16[224,128]{1,0:T(8,128)(2,1)S(1)}, bf16[224,128]{1,0:T(8,128)(2,1)S(1)}, u32[]{:S(2)}, u32[]{:S(2)}) collective-permute-start(bf16[224,128]{1,0:T(8,128)(2,1)S(1)} %add_convert_fusion.1), channel_id=1, source_target_pairs={{0,6},{1,7},{2,4},{3,5},{4,2},{5,3},{6,0},{7,1},{8,14},{9,15},{10,... | collective-permute-start | bytes 172040 | tf_op jit(solution)/shard_map/ppermute | solution.py:373
  167.7 11.5 %collective-permute-start.16 = (bf16[224,128]{1,0:T(8,128)(2,1)S(1)}, bf16[224,128]{1,0:T(8,128)(2,1)S(1)}, u32[]{:S(2)}, u32[]{:S(2)}) collective-permute-start(bf16[224,128]{1,0:T(8,128)(2,1)S(1)} %add_convert_fusion.1), channel_id=1, source_target_pairs={{0,4},{1,5},{2,6},{3,7},{4,0},{5,1},{6,2},{7,3},{8,12},{9,13},{10,... | collective-permute-start | bytes 172040 | tf_op jit(solution)/shard_map/ppermute | solution.py:373
  170.0 9.2 %collective-permute-start.15 = (bf16[224,128]{1,0:T(8,128)(2,1)S(1)}, bf16[224,128]{1,0:T(8,128)(2,1)S(1)}, u32[]{:S(2)}, u32[]{:S(2)}) collective-permute-start(bf16[224,128]{1,0:T(8,128)(2,1)S(1)} %add_convert_fusion.1), channel_id=1, source_target_pairs={{0,2},{1,3},{2,0},{3,1},{4,6},{5,7},{6,4},{7,5},{8,10},{9,11},{10,... | collective-permute-start | bytes 172040 | tf_op jit(solution)/shard_map/ppermute | solution.py:373
  173.7 13.1 %collective-permute-start.22 = (bf16[16,64,128]{2,1,0:T(8,128)(2,1)}, bf16[16,64,128]{2,1,0:T(8,128)(2,1)S(1)}, u32[]{:S(2)}, u32[]{:S(2)}) collective-permute-start(bf16[16,64,128]{2,1,0:T(8,128)(2,1)} %collective-permute-done.13), channel_id=1, source_target_pairs={{20,17},{21,16},{22,25},{23,24},{28,19},{29,18},{30,27},{31,26},{0... | collective-permute-start | bytes 786440 | tf_op jit(solution)/shard_map/ppermute | solution.py:474
  179.3 3.9 %collective-permute-start.18 = (bf16[224,128]{1,0:T(8,128)(2,1)S(1)}, bf16[224,128]{1,0:T(8,128)(2,1)S(1)}, u32[]{:S(2)}, u32[]{:S(2)}) collective-permute-start(bf16[224,128]{1,0:T(8,128)(2,1)S(1)} %add_convert_fusion), channel_id=1, source_target_pairs={{0,8},{8,0},{16,24},{24,16},{1,9},{9,1},{17,25},{25,17},{2,10},{10... | collective-permute-start | bytes 172040 | tf_op jit(solution)/shard_map/ppermute | solution.py:373
  183.2 6.9 %collective-permute-start.21 = (bf16[448,128]{1,0:T(8,128)(2,1)S(1)}, bf16[448,128]{1,0:T(8,128)(2,1)S(1)}, u32[]{:S(2)}, u32[]{:S(2)}) collective-permute-start(bf16[448,128]{1,0:T(8,128)(2,1)S(1)} %constant_dynamic-update-slice_fusion.refs_0_), channel_id=1, source_target_pairs={{0,17},{1,16},{2,19},{3,18},{4,21},{5,20},{6,23},{7,22},{8,25},{9,... | collective-permute-start | bytes 344072 | tf_op jit(solution)/shard_map/ppermute | solution.py:412
  183.3 8.2 %collective-permute-start.20 = (bf16[448,128]{1,0:T(8,128)(2,1)S(1)}, bf16[448,128]{1,0:T(8,128)(2,1)S(1)}, u32[]{:S(2)}, u32[]{:S(2)}) collective-permute-start(bf16[448,128]{1,0:T(8,128)(2,1)S(1)} %constant_dynamic-update-slice_fusion.refs_0_), channel_id=1, source_target_pairs={{0,16},{1,17},{2,18},{3,19},{4,20},{5,21},{6,22},{7,23},{8,24},{9,... | collective-permute-start | bytes 344072 | tf_op jit(solution)/shard_map/ppermute | solution.py:412
  185.5 6.7 %collective-permute-start.19 = (bf16[448,128]{1,0:T(8,128)(2,1)S(1)}, bf16[448,128]{1,0:T(8,128)(2,1)S(1)}, u32[]{:S(2)}, u32[]{:S(2)}) collective-permute-start(bf16[448,128]{1,0:T(8,128)(2,1)S(1)} %constant_dynamic-update-slice_fusion.refs_0_), channel_id=1, source_target_pairs={{0,1},{1,0},{2,3},{3,2},{4,5},{5,4},{6,7},{7,6},{8,9},{9,8},{10,11... | collective-permute-start | bytes 344072 | tf_op jit(solution)/shard_map/ppermute | solution.py:412
  (19 other events, 183.3 us)

commit v4 on v3

--- a/solution.py
+++ b/solution.py
@@ -14,7 +14,7 @@
 GROUP = LANES // SQ
 PARTS = 2
 PIECE = 256
-VMEM_BYTES = 52 * 2**20
+VMEM_BYTES = 32 * 2**20
 BF16 = jnp.bfloat16
 F32 = jnp.float32
 

time: 196 us -> 204 us (1.041)
  local copies, waits for them, and re-layouts: 5.08 us -> 22.7 us
  Pallas kernels: 66.1 us -> 58.9 us
  waiting for transfers between devices: 47 us -> 44.8 us
    unnamed x52 -> x86, local copies, waits for them, and re-layouts: 5.07 us -> 22.7 us
    all_to_all x2, waiting for transfers between devices: 4.63 us -> 0.01 us  [per_device(): returned.append(lax.all_to_all(outs[4], 'col', 0, 0, tiled=True))]
    ppermute x12, starting transfers between devices: 30.9 us -> 35.4 us  [move(): return lax.ppermute(value, ('row', 'col'), perm)]
    all_to_all x2, starting transfers between devices: 15.6 us -> 11.7 us  [per_device(): returned.append(lax.all_to_all(outs[4], 'col', 0, 0, tiled=True))]
    pallas_call x2, Pallas kernels: 37.5 us -> 34.9 us  [transition(): pl.pallas_call(functools.partial(main_kernel, col_devs, cols, part), grid...]
    pallas_call x2, Pallas kernels: 6.73 us -> 4.29 us  [pack(): pl.pallas_call(functools.partial(pack_kernel, col_devs), grid=(1,), out_s...]
    ppermute x6, waiting for transfers between devices: 4.14 us -> 6.4 us  [flip(): return lax.ppermute(value, ('row', 'col'), perm)]
  transfers between devices with their start and end apart: 27 -> 27, of which waited for: 9 -> 9; matrix products, arithmetic and copies ran while one was open for 0% -> 0% of each run, Pallas kernels for 32% -> 27%
where the time goes in v4:
time: 204 us; the launch traced here: 201 us
  starting transfers between devices  73.7 us (36%)
  Pallas kernels  58.9 us (29%)
  waiting for transfers between devices  44.8 us (22%)
  local copies, waits for them, and re-layouts  22.7 us (11%)
    ppermute x12, waiting for transfers between devices, move(): return lax.ppermute(value, ('row', 'col'), perm)  36.7 us
    ppermute x12, starting transfers between devices, move(): return lax.ppermute(value, ('row', 'col'), perm)  35.4 us
    pallas_call x2, Pallas kernels, transition(): pl.pallas_call(functools.partial(main_kernel, col_devs, cols, part), grid...  34.9 us
    unnamed x86, local copies, waits for them, and re-layouts  22.7 us
    all_to_all x2, starting transfers between devices, per_device(): returned.append(lax.all_to_all(outs[4], 'col', 0, 0, tiled=True))  11.7 us
    all_to_all x1, starting transfers between devices, per_device(): payloads[1] = lax.all_to_all(payloads[1], 'col', 0, 0, tiled=True)  7.72 us
    ppermute x5, starting transfers between devices, swap(): lax.ppermute(value, axis, [(i, i ^ mask) for i in range(lax.axis_size(axi...  6.6 us
    ppermute x6, waiting for transfers between devices, flip(): return lax.ppermute(value, ('row', 'col'), perm)  6.4 us
  transfers between devices with their start and end apart: 27, of which 9 were waited for; matrix products, arithmetic and copies ran while one was open for 0% of the time, Pallas kernels for 27%

profile of v4, /device:TPU:18, one launch (start us, length us, event | category | flops | bytes accessed | tf_op | source)
XLA Modules:
  0.0 201.4 jit_solution(16188751634138723346)
XLA Ops:
  4.2 2.1 %pack_0.1 = bf16[8,528,128]{2,1,0:T(8,128)(2,1)} custom-call(s32[16]{0:T(128)S(1)} %bitcast.39, s32[16]{0:T(128)S(1)} %copy-done.16, s32[16]{0:T(128)S(1)} %copy-done.22, bf16[16,64,1024]{2,1,0:T(8,128)(2,1)S(1)} %bitcast.28), custom_call_target="tpu_custom_call" | custom-call | flops 3300000000 | tf_op jit(solution)/shard_map/pack_0/pallas_call | solution.py:493
  6.4 6.3 %all-to-all-start.1 = ((bf16[8,528,128]{2,1,0:T(8,128)(2,1)}), bf16[8,528,128]{2,1,0:T(8,128)(2,1)S(1)}, u32[]{:S(2)}, u32[]{:S(2)}) async-start(bf16[8,528,128]{2,1,0:T(8,128)(2,1)} %pack_0.1), calls=%async_computation.1 | async-start | bytes 2162688 | tf_op jit(solution)/shard_map/all_to_all | solution.py:507
  12.8 2.4 %pack_cotangent.1 = (bf16[32,64,128]{2,1,0:T(8,128)(2,1)}, bf16[32,64,128]{2,1,0:T(8,128)(2,1)}) custom-call(s32[4]{0:T(128)S(1)} %pad_add_fusion.where_am.refs_0_, bf16[64,64,128]{2,1,0:T(8,128)(2,1)S(1)} %bitcast.30), custom_call_target="tpu_custom_call" | custom-call | flops 2200000000 | tf_op jit(solution)/shard_map/pack_cotangent/pallas_call | solution.py:508
  16.5 3.4 %collective-permute-start.1 = (bf16[32,64,128]{2,1,0:T(8,128)(2,1)}, bf16[32,64,128]{2,1,0:T(8,128)(2,1)S(1)}, u32[]{:S(2)}, u32[]{:S(2)}) collective-permute-start(bf16[32,64,128]{2,1,0:T(8,128)(2,1)} %get-tuple-element.64), channel_id=1, source_target_pairs={{0,1},{1,0},{2,9},{3,8},{8,3},{9,2},{10,11},{11,10},{20,21},{21,20... | collective-permute-start | bytes 1572872 | tf_op jit(solution)/shard_map/ppermute | solution.py:474
  19.9 5.5 %collective-permute-start = (bf16[32,64,128]{2,1,0:T(8,128)(2,1)}, bf16[32,64,128]{2,1,0:T(8,128)(2,1)}, u32[]{:S(2)}, u32[]{:S(2)}) collective-permute-start(bf16[32,64,128]{2,1,0:T(8,128)(2,1)} %get-tuple-element.63), channel_id=1, source_target_pairs={{0,0},{1,1},{2,8},{3,9},{4,16},{5,17},{6,24},{7,25},{8,2},{9,3},{1... | collective-permute-start | bytes 1572872 | tf_op jit(solution)/shard_map/ppermute | solution.py:474
  25.4 5.1 %collective-permute-done.2 = bf16[32,64,128]{2,1,0:T(8,128)(2,1)} collective-permute-done((bf16[32,64,128]{2,1,0:T(8,128)(2,1)}, bf16[32,64,128]{2,1,0:T(8,128)(2,1)}, u32[]{:S(2)}, u32[]{:S(2)}) %collective-permute-start.2) | collective-permute-done | bytes 524320 | tf_op jit(solution)/shard_map/ppermute | solution.py:474
  30.5 2.2 %collective-permute-start.3 = (bf16[32,64,128]{2,1,0:T(8,128)(2,1)}, bf16[32,64,128]{2,1,0:T(8,128)(2,1)}, u32[]{:S(2)}, u32[]{:S(2)}) collective-permute-start(bf16[32,64,128]{2,1,0:T(8,128)(2,1)} %collective-permute-done.2), channel_id=1, source_target_pairs={{20,17},{21,16},{22,25},{23,24},{28,19},{29,18},{30,27},{31,26},{0... | collective-permute-start | bytes 1572872 | tf_op jit(solution)/shard_map/ppermute | solution.py:474
  32.7 2.2 %pack_1.1 = bf16[8,528,128]{2,1,0:T(8,128)(2,1)} custom-call(s32[16]{0:T(128)S(1)} %bitcast.40, s32[16]{0:T(128)S(1)} %copy-done.17, s32[16]{0:T(128)S(1)} %copy-done.23, bf16[16,64,1024]{2,1,0:T(8,128)(2,1)S(1)} %bitcast.29), custom_call_target="tpu_custom_call" | custom-call | flops 3300000000 | tf_op jit(solution)/shard_map/pack_1/pallas_call | solution.py:493
  35.3 3.6 %turn.1.refs_3_ = bf16[8192,64]{1,0:T(8,128)(2,1)S(1)} custom-call(bf16[64,64,128]{2,1,0:T(8,128)(2,1)S(1)} %bitcast.31), custom_call_target="tpu_custom_call" | custom-call | flops 5500000256 | tf_op jit(solution)/shard_map/turn/pallas_call | solution.py:522
  40.2 18.1 %collective-permute-done.3.refs_6_ = bf16[32,64,128]{2,1,0:T(8,128)(2,1)} collective-permute-done((bf16[32,64,128]{2,1,0:T(8,128)(2,1)}, bf16[32,64,128]{2,1,0:T(8,128)(2,1)}, u32[]{:S(2)}, u32[]{:S(2)}) %collective-permute-start.3) | collective-permute-done | bytes 524320 | tf_op jit(solution)/shard_map/ppermute | solution.py:474
  58.3 7.7 %all-to-all-start = ((bf16[8,528,128]{2,1,0:T(8,128)(2,1)}), bf16[8,528,128]{2,1,0:T(8,128)(2,1)S(1)}, u32[]{:S(2)}, u32[]{:S(2)}) async-start(bf16[8,528,128]{2,1,0:T(8,128)(2,1)} %pack_1.1), calls=%async_computation | async-start | bytes 2162688 | tf_op jit(solution)/shard_map/all_to_all | solution.py:520
  66.1 2.2 %copy-done.3 = f32[128,64,128]{2,1,0:T(8,128)S(1)} copy-done((f32[128,64,128]{2,1,0:T(8,128)S(1)}, f32[128,64,128]{2,1,0:T(8,128)}, u32[]{:S(2)}) %copy-start.3) | copy-done | bytes 4194328
  69.9 17.5 %transition_0.1 = (f32[8192,128]{1,0:T(8,128)}, bf16[4096,128]{1,0:T(8,128)(2,1)S(1)}, bf16[16,64,128]{2,1,0:T(8,128)(2,1)}, bf16[16,64,128]{2,1,0:T(8,128)(2,1)...) custom-call(s32[4]{0:T(128)S(1)} %pad_add_fusion.where_am.refs_0_, ...), custom_call_target="tpu_custom_call" | custom-call | flops 22000001024 | tf_op jit(solution)/shard_map/transition_0/pallas_call | solution.py:597
  91.8 3.4 %collective-permute-start.5 = (bf16[16,64,128]{2,1,0:T(8,128)(2,1)}, bf16[16,64,128]{2,1,0:T(8,128)(2,1)}, u32[]{:S(2)}, u32[]{:S(2)}) collective-permute-start(bf16[16,64,128]{2,1,0:T(8,128)(2,1)} %get-tuple-element.78), channel_id=1, source_target_pairs={{0,1},{1,0},{2,9},{3,8},{8,3},{9,2},{10,11},{11,10},{20,21},{21,20... | collective-permute-start | bytes 786440 | tf_op jit(solution)/shard_map/ppermute | solution.py:474
  95.1 3.6 %collective-permute-start.4 = (bf16[16,64,128]{2,1,0:T(8,128)(2,1)}, bf16[16,64,128]{2,1,0:T(8,128)(2,1)}, u32[]{:S(2)}, u32[]{:S(2)}) collective-permute-start(bf16[16,64,128]{2,1,0:T(8,128)(2,1)} %get-tuple-element.77), channel_id=1, source_target_pairs={{0,0},{1,1},{2,8},{3,9},{4,16},{5,17},{6,24},{7,25},{8,2},{9,3},{1... | collective-permute-start | bytes 786440 | tf_op jit(solution)/shard_map/ppermute | solution.py:474
  98.8 5.5 %all-to-all-start.2 = ((bf16[8,512,128]{2,1,0:T(8,128)(2,1)}), bf16[8,512,128]{2,1,0:T(8,128)(2,1)S(1)}, u32[]{:S(2)}, u32[]{:S(2)}) async-start(bf16[8,512,128]{2,1,0:T(8,128)(2,1)} %get-tuple-element.76), calls=%async_computation.2 | async-start | bytes 2097152 | tf_op jit(solution)/shard_map/all_to_all | solution.py:623
  104.3 2.2 %copy-done.4 = f32[128,64,128]{2,1,0:T(8,128)S(1)} copy-done((f32[128,64,128]{2,1,0:T(8,128)S(1)}, f32[128,64,128]{2,1,0:T(8,128)}, u32[]{:S(2)}) %copy-start.4) | copy-done | bytes 4194328
  110.9 17.4 %transition_1.1 = (f32[8192,128]{1,0:T(8,128)}, bf16[4096,128]{1,0:T(8,128)(2,1)S(1)}, bf16[16,64,128]{2,1,0:T(8,128)(2,1)S(1)}, bf16[16,64,128]{2,1,0:T(8,128)(...) custom-call(s32[4]{0:T(128)S(1)} %pad_add_fusion.where_am.refs_0_, ...), custom_call_target="tpu_custom_call", output_to_operand_aliasing={{0}: (17, {})} | custom-call | flops 22000001024 | tf_op jit(solution)/shard_map/transition_1/pallas_call | solution.py:597
  132.2 6.2 %all-to-all-start.3 = ((bf16[8,512,128]{2,1,0:T(8,128)(2,1)}), bf16[8,512,128]{2,1,0:T(8,128)(2,1)S(1)}, u32[]{:S(2)}, u32[]{:S(2)}) async-start(bf16[8,512,128]{2,1,0:T(8,128)(2,1)} %get-tuple-element.91), calls=%async_computation.3 | async-start | bytes 2097152 | tf_op jit(solution)/shard_map/all_to_all | solution.py:623
  144.6 2.5 %collective-permute-start.12 = (bf16[16,64,128]{2,1,0:T(8,128)(2,1)S(1)}, bf16[16,64,128]{2,1,0:T(8,128)(2,1)S(1)}, u32[]{:S(2)}, u32[]{:S(2)}) collective-permute-start(bf16[16,64,128]{2,1,0:T(8,128)(2,1)S(1)} %copy-done.11), channel_id=1, source_target_pairs={{0,1},{1,0},{2,9},{3,8},{8,3},{9,2},{10,11},{11,10},{20,21},{21,20... | collective-permute-start | bytes 786440 | tf_op jit(solution)/shard_map/ppermute | solution.py:474
  148.8 6.1 %collective-permute-start.14 = (bf16[16,64,128]{2,1,0:T(8,128)(2,1)}, bf16[16,64,128]{2,1,0:T(8,128)(2,1)S(1)}, u32[]{:S(2)}, u32[]{:S(2)}) collective-permute-start(bf16[16,64,128]{2,1,0:T(8,128)(2,1)} %collective-permute-done.6), channel_id=1, source_target_pairs={{20,17},{21,16},{22,25},{23,24},{28,19},{29,18},{30,27},{31,26},{0... | collective-permute-start | bytes 786440 | tf_op jit(solution)/shard_map/ppermute | solution.py:474
  155.1 3.5 %own_heads.1.heads = bf16[64,64,128]{2,1,0:T(8,128)(2,1)S(1)} custom-call(bf16[4096,128]{1,0:T(8,128)(2,1)S(1)} %copy-done.32, bf16[4096,128]{1,0:T(8,128)(2,1)S(1)} %copy-done.34, bf16[64,128]{1,0:T(8,128)(2,1)S(1)} %bitcast.34), custom_call_target="tpu_custom_call" | custom-call | flops 5500000256 | tf_op jit(solution)/shard_map/own_heads/pallas_call | solution.py:625
  158.6 1.8 collective-permute-done.10
  160.5 12.5 %collective-permute-done.14.got_c = bf16[16,64,128]{2,1,0:T(8,128)(2,1)S(1)} collective-permute-done((bf16[16,64,128]{2,1,0:T(8,128)(2,1)}, bf16[16,64,128]{2,1,0:T(8,128)(2,1)S(1)}, u32[]{:S(2)}, u32[]{:S(2)}) %collective-permute-start.14) | collective-permute-done | bytes 262176 | tf_op jit(solution)/shard_map/ppermute | solution.py:474
  173.0 2.9 %collective-permute-start.17 = (bf16[224,128]{1,0:T(8,128)(2,1)S(1)}, bf16[224,128]{1,0:T(8,128)(2,1)S(1)}, u32[]{:S(2)}, u32[]{:S(2)}) collective-permute-start(bf16[224,128]{1,0:T(8,128)(2,1)S(1)} %add_convert_fusion.1), channel_id=1, source_target_pairs={{0,6},{1,7},{2,4},{3,5},{4,2},{5,3},{6,0},{7,1},{8,14},{9,15},{10,... | collective-permute-start | bytes 172040 | tf_op jit(solution)/shard_map/ppermute | solution.py:373
  175.9 2.0 collective-permute-start.16
  179.3 2.2 %tile_gradients_0.1.refs_0_ = bf16[16,64,1024]{2,1,0:T(8,128)(2,1)} custom-call(s32[16]{0:T(128)S(1)} %bitcast.41, s32[16]{0:T(128)S(1)} %copy-done.23, bf16[8,512,128]{2,1,0:T(8,128)(2,1)S(1)} %all-to-all-done.2.returned), custom_call_target="tpu_custom_call" | custom-call | flops 2200000000 | tf_op jit(solution)/shard_map/tile_gradients_0/pallas_call | solution.py:669
  181.5 4.2 %collective-permute-start.22 = (bf16[16,64,128]{2,1,0:T(8,128)(2,1)}, bf16[16,64,128]{2,1,0:T(8,128)(2,1)S(1)}, u32[]{:S(2)}, u32[]{:S(2)}) collective-permute-start(bf16[16,64,128]{2,1,0:T(8,128)(2,1)} %collective-permute-done.13), channel_id=1, source_target_pairs={{20,17},{21,16},{22,25},{23,24},{28,19},{29,18},{30,27},{31,26},{0... | collective-permute-start | bytes 786440 | tf_op jit(solution)/shard_map/ppermute | solution.py:474
  185.9 2.2 %tile_gradients_1.1 = bf16[16,64,1024]{2,1,0:T(8,128)(2,1)} custom-call(s32[16]{0:T(128)S(1)} %bitcast.42, s32[16]{0:T(128)S(1)} %copy-done.23, bf16[8,512,128]{2,1,0:T(8,128)(2,1)S(1)} %all-to-all-done.3.returned, bf16[16,64,1024]{2,1,0:T(8,128)(2,1)} %tile_gradients_0.1.refs_0_), custom_call_target="tpu_custom_call", output_to_operand_aliasing={{}: (3, {})} | custom-call | flops 2200000000 | tf_op jit(solution)/shard_map/tile_gradients_1/pallas_call | solution.py:669
  188.1 2.0 %logits_0.1.refs_0_ = bf16[64,64,128]{2,1,0:T(8,128)(2,1)} custom-call(s32[4]{0:T(128)S(1)} %pad_add_fusion.where_am.refs_0_, bf16[64,64,128]{2,1,0:T(8,128)(2,1)S(1)} %copy-done.25, bf16[16,64,128]{2,1,0:T(8,128)(2,1)} %collective-permute-done.4.got_a, bf16[16,64,128]{2,1,0:T(8,128)(2,1)} %collective-permute-done.5.got_b, ...), custom_call_target="tpu_custom_call" | custom-call | flops 2200000000 | tf_op jit(solution)/shard_map/logits_0/pallas_call | solution.py:656
  190.3 3.6 %collective-permute-start.20 = (bf16[448,128]{1,0:T(8,128)(2,1)S(1)}, bf16[448,128]{1,0:T(8,128)(2,1)S(1)}, u32[]{:S(2)}, u32[]{:S(2)}) collective-permute-start(bf16[448,128]{1,0:T(8,128)(2,1)S(1)} %constant_dynamic-update-slice_fusion.refs_0_), channel_id=1, source_target_pairs={{0,16},{1,17},{2,18},{3,19},{4,20},{5,21},{6,22},{7,23},{8,24},{9,... | collective-permute-start | bytes 344072 | tf_op jit(solution)/shard_map/ppermute | solution.py:412
  197.1 2.7 %collective-permute-done.20.refs_2_ = bf16[448,128]{1,0:T(8,128)(2,1)S(1)} collective-permute-done((bf16[448,128]{1,0:T(8,128)(2,1)S(1)}, bf16[448,128]{1,0:T(8,128)(2,1)S(1)}, u32[]{:S(2)}, u32[]{:S(2)}) %collective-permute-start.20) | collective-permute-done | bytes 114720 | tf_op jit(solution)/shard_map/ppermute | solution.py:412
  (125 shorter events, 35.5 us)
Async XLA Ops:
  6.4 52.0 %all-to-all-start.1 = ((bf16[8,528,128]{2,1,0:T(8,128)(2,1)}), bf16[8,528,128]{2,1,0:T(8,128)(2,1)S(1)}, u32[]{:S(2)}, u32[]{:S(2)}) async-start(bf16[8,528,128]{2,1,0:T(8,128)(2,1)} %pack_0.1), calls=%async_computation.1 | async-start | bytes 2162688 | tf_op jit(solution)/shard_map/all_to_all | solution.py:507
  15.2 15.3 %collective-permute-start.2 = (bf16[32,64,128]{2,1,0:T(8,128)(2,1)}, bf16[32,64,128]{2,1,0:T(8,128)(2,1)}, u32[]{:S(2)}, u32[]{:S(2)}) collective-permute-start(bf16[32,64,128]{2,1,0:T(8,128)(2,1)} %get-tuple-element.64), channel_id=1, source_target_pairs={{4,20},{5,21},{6,22},{7,23},{12,28},{13,29},{14,30},{15,31},{16,0}... | collective-permute-start | bytes 1572872 | tf_op jit(solution)/shard_map/ppermute | solution.py:474
  16.5 23.7 %collective-permute-start.1 = (bf16[32,64,128]{2,1,0:T(8,128)(2,1)}, bf16[32,64,128]{2,1,0:T(8,128)(2,1)S(1)}, u32[]{:S(2)}, u32[]{:S(2)}) collective-permute-start(bf16[32,64,128]{2,1,0:T(8,128)(2,1)} %get-tuple-element.64), channel_id=1, source_target_pairs={{0,1},{1,0},{2,9},{3,8},{8,3},{9,2},{10,11},{11,10},{20,21},{21,20... | collective-permute-start | bytes 1572872 | tf_op jit(solution)/shard_map/ppermute | solution.py:474
  19.9 20.3 %collective-permute-start = (bf16[32,64,128]{2,1,0:T(8,128)(2,1)}, bf16[32,64,128]{2,1,0:T(8,128)(2,1)}, u32[]{:S(2)}, u32[]{:S(2)}) collective-permute-start(bf16[32,64,128]{2,1,0:T(8,128)(2,1)} %get-tuple-element.63), channel_id=1, source_target_pairs={{0,0},{1,1},{2,8},{3,9},{4,16},{5,17},{6,24},{7,25},{8,2},{9,3},{1... | collective-permute-start | bytes 1572872 | tf_op jit(solution)/shard_map/ppermute | solution.py:474
  30.5 27.8 %collective-permute-start.3 = (bf16[32,64,128]{2,1,0:T(8,128)(2,1)}, bf16[32,64,128]{2,1,0:T(8,128)(2,1)}, u32[]{:S(2)}, u32[]{:S(2)}) collective-permute-start(bf16[32,64,128]{2,1,0:T(8,128)(2,1)} %collective-permute-done.2), channel_id=1, source_target_pairs={{20,17},{21,16},{22,25},{23,24},{28,19},{29,18},{30,27},{31,26},{0... | collective-permute-start | bytes 1572872 | tf_op jit(solution)/shard_map/ppermute | solution.py:474
  40.2 25.8 %copy-start.14 = (bf16[64,128]{1,0:T(8,128)(2,1)S(1)}, bf16[64,128]{1,0:T(8,128)(2,1)}, u32[]{:S(2)}) copy-start(bf16[64,128]{1,0:T(8,128)(2,1)} %refs_7_.3) | copy-start | bytes 49156
  40.2 25.8 %copy-start.15 = (bf16[128,64]{0,1:T(8,128)(2,1)S(1)}, bf16[128,64]{0,1:T(8,128)(2,1)}, u32[]{:S(2)}) copy-start(bf16[128,64]{0,1:T(8,128)(2,1)} %param.25) | copy-start | bytes 49156
  40.2 25.8 %copy-start.18 = (f32[128]{0:T(128)S(1)}, f32[128]{0:T(128)}, u32[]{:S(2)}) copy-start(f32[128]{0:T(128)} %param.20) | copy-start | bytes 1540
  40.2 25.8 %copy-start.19 = (f32[128]{0:T(128)S(1)}, f32[128]{0:T(128)}, u32[]{:S(2)}) copy-start(f32[128]{0:T(128)} %param.21) | copy-start | bytes 1540
  58.3 40.4 %all-to-all-start = ((bf16[8,528,128]{2,1,0:T(8,128)(2,1)}), bf16[8,528,128]{2,1,0:T(8,128)(2,1)S(1)}, u32[]{:S(2)}, u32[]{:S(2)}) async-start(bf16[8,528,128]{2,1,0:T(8,128)(2,1)} %pack_1.1), calls=%async_computation | async-start | bytes 2162688 | tf_op jit(solution)/shard_map/all_to_all | solution.py:520
  90.5 48.0 %collective-permute-start.6 = (bf16[16,64,128]{2,1,0:T(8,128)(2,1)}, bf16[16,64,128]{2,1,0:T(8,128)(2,1)}, u32[]{:S(2)}, u32[]{:S(2)}) collective-permute-start(bf16[16,64,128]{2,1,0:T(8,128)(2,1)} %get-tuple-element.78), channel_id=1, source_target_pairs={{4,20},{5,21},{6,22},{7,23},{12,28},{13,29},{14,30},{15,31},{16,0}... | collective-permute-start | bytes 786440 | tf_op jit(solution)/shard_map/ppermute | solution.py:474
  91.8 46.7 %collective-permute-start.5 = (bf16[16,64,128]{2,1,0:T(8,128)(2,1)}, bf16[16,64,128]{2,1,0:T(8,128)(2,1)}, u32[]{:S(2)}, u32[]{:S(2)}) collective-permute-start(bf16[16,64,128]{2,1,0:T(8,128)(2,1)} %get-tuple-element.78), channel_id=1, source_target_pairs={{0,1},{1,0},{2,9},{3,8},{8,3},{9,2},{10,11},{11,10},{20,21},{21,20... | collective-permute-start | bytes 786440 | tf_op jit(solution)/shard_map/ppermute | solution.py:474
  95.1 43.3 %collective-permute-start.4 = (bf16[16,64,128]{2,1,0:T(8,128)(2,1)}, bf16[16,64,128]{2,1,0:T(8,128)(2,1)}, u32[]{:S(2)}, u32[]{:S(2)}) collective-permute-start(bf16[16,64,128]{2,1,0:T(8,128)(2,1)} %get-tuple-element.77), channel_id=1, source_target_pairs={{0,0},{1,1},{2,8},{3,9},{4,16},{5,17},{6,24},{7,25},{8,2},{9,3},{1... | collective-permute-start | bytes 786440 | tf_op jit(solution)/shard_map/ppermute | solution.py:474
  98.8 33.5 %all-to-all-start.2 = ((bf16[8,512,128]{2,1,0:T(8,128)(2,1)}), bf16[8,512,128]{2,1,0:T(8,128)(2,1)S(1)}, u32[]{:S(2)}, u32[]{:S(2)}) async-start(bf16[8,512,128]{2,1,0:T(8,128)(2,1)} %get-tuple-element.76), calls=%async_computation.2 | async-start | bytes 2097152 | tf_op jit(solution)/shard_map/all_to_all | solution.py:623
  132.2 53.6 %all-to-all-start.3 = ((bf16[8,512,128]{2,1,0:T(8,128)(2,1)}), bf16[8,512,128]{2,1,0:T(8,128)(2,1)S(1)}, u32[]{:S(2)}, u32[]{:S(2)}) async-start(bf16[8,512,128]{2,1,0:T(8,128)(2,1)} %get-tuple-element.91), calls=%async_computation.3 | async-start | bytes 2097152 | tf_op jit(solution)/shard_map/all_to_all | solution.py:623
  138.5 1.9 collective-permute-start.7
  141.0 7.9 %collective-permute-start.8 = (bf16[224,128]{1,0:T(8,128)(2,1)S(1)}, bf16[224,128]{1,0:T(8,128)(2,1)S(1)}, u32[]{:S(2)}, u32[]{:S(2)}) collective-permute-start(bf16[224,128]{1,0:T(8,128)(2,1)S(1)} %get-tuple-element.82), channel_id=1, source_target_pairs={{0,1},{1,0},{2,3},{3,2},{4,5},{5,4},{6,7},{7,6},{8,9},{9,8},{10,11... | collective-permute-start | bytes 172040 | tf_op jit(solution)/shard_map/ppermute | solution.py:412
  142.5 12.5 %collective-permute-start.9 = (bf16[224,128]{1,0:T(8,128)(2,1)S(1)}, bf16[224,128]{1,0:T(8,128)(2,1)S(1)}, u32[]{:S(2)}, u32[]{:S(2)}) collective-permute-start(bf16[224,128]{1,0:T(8,128)(2,1)S(1)} %get-tuple-element.83), channel_id=1, source_target_pairs={{0,16},{1,17},{2,18},{3,19},{4,20},{5,21},{6,22},{7,23},{8,24},{9,... | collective-permute-start | bytes 172040 | tf_op jit(solution)/shard_map/ppermute | solution.py:412
  143.3 17.2 %collective-permute-start.13 = (bf16[16,64,128]{2,1,0:T(8,128)(2,1)S(1)}, bf16[16,64,128]{2,1,0:T(8,128)(2,1)}, u32[]{:S(2)}, u32[]{:S(2)}) collective-permute-start(bf16[16,64,128]{2,1,0:T(8,128)(2,1)S(1)} %copy-done.11), channel_id=1, source_target_pairs={{4,20},{5,21},{6,22},{7,23},{12,28},{13,29},{14,30},{15,31},{16,0}... | collective-permute-start | bytes 786440 | tf_op jit(solution)/shard_map/ppermute | solution.py:474
  144.6 15.9 %collective-permute-start.12 = (bf16[16,64,128]{2,1,0:T(8,128)(2,1)S(1)}, bf16[16,64,128]{2,1,0:T(8,128)(2,1)S(1)}, u32[]{:S(2)}, u32[]{:S(2)}) collective-permute-start(bf16[16,64,128]{2,1,0:T(8,128)(2,1)S(1)} %copy-done.11), channel_id=1, source_target_pairs={{0,1},{1,0},{2,9},{3,8},{8,3},{9,2},{10,11},{11,10},{20,21},{21,20... | collective-permute-start | bytes 786440 | tf_op jit(solution)/shard_map/ppermute | solution.py:474
  147.1 13.4 %collective-permute-start.11 = (bf16[16,64,128]{2,1,0:T(8,128)(2,1)S(1)}, bf16[16,64,128]{2,1,0:T(8,128)(2,1)S(1)}, u32[]{:S(2)}, u32[]{:S(2)}) collective-permute-start(bf16[16,64,128]{2,1,0:T(8,128)(2,1)S(1)} %copy-done.13), channel_id=1, source_target_pairs={{0,0},{1,1},{2,8},{3,9},{4,16},{5,17},{6,24},{7,25},{8,2},{9,3},{1... | collective-permute-start | bytes 786440 | tf_op jit(solution)/shard_map/ppermute | solution.py:474
  148.8 24.2 %collective-permute-start.14 = (bf16[16,64,128]{2,1,0:T(8,128)(2,1)}, bf16[16,64,128]{2,1,0:T(8,128)(2,1)S(1)}, u32[]{:S(2)}, u32[]{:S(2)}) collective-permute-start(bf16[16,64,128]{2,1,0:T(8,128)(2,1)} %collective-permute-done.6), channel_id=1, source_target_pairs={{20,17},{21,16},{22,25},{23,24},{28,19},{29,18},{30,27},{31,26},{0... | collective-permute-start | bytes 786440 | tf_op jit(solution)/shard_map/ppermute | solution.py:474
  155.0 5.4 %collective-permute-start.10 = (bf16[224,128]{1,0:T(8,128)(2,1)S(1)}, bf16[224,128]{1,0:T(8,128)(2,1)S(1)}, u32[]{:S(2)}, u32[]{:S(2)}) collective-permute-start(bf16[224,128]{1,0:T(8,128)(2,1)S(1)} %get-tuple-element.84), channel_id=1, source_target_pairs={{0,17},{1,16},{2,19},{3,18},{4,21},{5,20},{6,23},{7,22},{8,25},{9,... | collective-permute-start | bytes 172040 | tf_op jit(solution)/shard_map/ppermute | solution.py:412
  158.6 23.0 %copy-start.24 = (bf16[64,64,128]{2,1,0:T(8,128)(2,1)}, bf16[64,64,128]{2,1,0:T(8,128)(2,1)S(1)}, u32[]{:S(2)}) copy-start(bf16[64,64,128]{2,1,0:T(8,128)(2,1)S(1)} %own_heads.1.heads) | copy-start | bytes 3145732
  173.0 12.7 %collective-permute-start.17 = (bf16[224,128]{1,0:T(8,128)(2,1)S(1)}, bf16[224,128]{1,0:T(8,128)(2,1)S(1)}, u32[]{:S(2)}, u32[]{:S(2)}) collective-permute-start(bf16[224,128]{1,0:T(8,128)(2,1)S(1)} %add_convert_fusion.1), channel_id=1, source_target_pairs={{0,6},{1,7},{2,4},{3,5},{4,2},{5,3},{6,0},{7,1},{8,14},{9,15},{10,... | collective-permute-start | bytes 172040 | tf_op jit(solution)/shard_map/ppermute | solution.py:373
  175.9 9.8 %collective-permute-start.16 = (bf16[224,128]{1,0:T(8,128)(2,1)S(1)}, bf16[224,128]{1,0:T(8,128)(2,1)S(1)}, u32[]{:S(2)}, u32[]{:S(2)}) collective-permute-start(bf16[224,128]{1,0:T(8,128)(2,1)S(1)} %add_convert_fusion.1), channel_id=1, source_target_pairs={{0,4},{1,5},{2,6},{3,7},{4,0},{5,1},{6,2},{7,3},{8,12},{9,13},{10,... | collective-permute-start | bytes 172040 | tf_op jit(solution)/shard_map/ppermute | solution.py:373
  177.9 7.9 %collective-permute-start.15 = (bf16[224,128]{1,0:T(8,128)(2,1)S(1)}, bf16[224,128]{1,0:T(8,128)(2,1)S(1)}, u32[]{:S(2)}, u32[]{:S(2)}) collective-permute-start(bf16[224,128]{1,0:T(8,128)(2,1)S(1)} %add_convert_fusion.1), channel_id=1, source_target_pairs={{0,2},{1,3},{2,0},{3,1},{4,6},{5,7},{6,4},{7,5},{8,10},{9,11},{10,... | collective-permute-start | bytes 172040 | tf_op jit(solution)/shard_map/ppermute | solution.py:373
  181.5 13.2 %collective-permute-start.22 = (bf16[16,64,128]{2,1,0:T(8,128)(2,1)}, bf16[16,64,128]{2,1,0:T(8,128)(2,1)S(1)}, u32[]{:S(2)}, u32[]{:S(2)}) collective-permute-start(bf16[16,64,128]{2,1,0:T(8,128)(2,1)} %collective-permute-done.13), channel_id=1, source_target_pairs={{20,17},{21,16},{22,25},{23,24},{28,19},{29,18},{30,27},{31,26},{0... | collective-permute-start | bytes 786440 | tf_op jit(solution)/shard_map/ppermute | solution.py:474
  185.8 4.3 %collective-permute-start.18 = (bf16[224,128]{1,0:T(8,128)(2,1)S(1)}, bf16[224,128]{1,0:T(8,128)(2,1)S(1)}, u32[]{:S(2)}, u32[]{:S(2)}) collective-permute-start(bf16[224,128]{1,0:T(8,128)(2,1)S(1)} %add_convert_fusion), channel_id=1, source_target_pairs={{0,8},{8,0},{16,24},{24,16},{1,9},{9,1},{17,25},{25,17},{2,10},{10... | collective-permute-start | bytes 172040 | tf_op jit(solution)/shard_map/ppermute | solution.py:373
  190.2 6.9 %collective-permute-start.21 = (bf16[448,128]{1,0:T(8,128)(2,1)S(1)}, bf16[448,128]{1,0:T(8,128)(2,1)S(1)}, u32[]{:S(2)}, u32[]{:S(2)}) collective-permute-start(bf16[448,128]{1,0:T(8,128)(2,1)S(1)} %constant_dynamic-update-slice_fusion.refs_0_), channel_id=1, source_target_pairs={{0,17},{1,16},{2,19},{3,18},{4,21},{5,20},{6,23},{7,22},{8,25},{9,... | collective-permute-start | bytes 344072 | tf_op jit(solution)/shard_map/ppermute | solution.py:412
  190.3 9.6 %collective-permute-start.20 = (bf16[448,128]{1,0:T(8,128)(2,1)S(1)}, bf16[448,128]{1,0:T(8,128)(2,1)S(1)}, u32[]{:S(2)}, u32[]{:S(2)}) collective-permute-start(bf16[448,128]{1,0:T(8,128)(2,1)S(1)} %constant_dynamic-update-slice_fusion.refs_0_), channel_id=1, source_target_pairs={{0,16},{1,17},{2,18},{3,19},{4,20},{5,21},{6,22},{7,23},{8,24},{9,... | collective-permute-start | bytes 344072 | tf_op jit(solution)/shard_map/ppermute | solution.py:412
  193.8 6.0 %collective-permute-start.19 = (bf16[448,128]{1,0:T(8,128)(2,1)S(1)}, bf16[448,128]{1,0:T(8,128)(2,1)S(1)}, u32[]{:S(2)}, u32[]{:S(2)}) collective-permute-start(bf16[448,128]{1,0:T(8,128)(2,1)S(1)} %constant_dynamic-update-slice_fusion.refs_0_), channel_id=1, source_target_pairs={{0,1},{1,0},{2,3},{3,2},{4,5},{5,4},{6,7},{7,6},{8,9},{9,8},{10,11... | collective-permute-start | bytes 344072 | tf_op jit(solution)/shard_map/ppermute | solution.py:412
  (36 other events, 217.6 us)
